TPU v7x, 32 devices: a whole 2x2x4 slice. The times are simulated.
32 devices in a mesh: seq: 16 (over z, y, core), head: 2 (over x).
Axes of the slice: x: 2, y: 2, z: 4, core: 2. Of those that a mesh axis runs over, the one named last changes fastest.
Arguments:
- layer_input: bfloat16 [4, 1024, 1024], P(None, 'seq'), may hold values from -6 to 6
- output_grad: bfloat16 [4, 1024, 1024], P(None, 'seq'), may hold values from -6 to 6
- random_pick: int32 [4, 16, 16, 3], P(None, 'seq', 'head'), may hold values from 0 to 65519
- doc_blocks: int32 [8], replicated, may hold values from 1 to 32, 64 in all
- last_fill: int32 [8], replicated, may hold values from 1 to 64
- shard_owner: int32 [16], replicated, may hold values from 0 to 15, each once
- qkv_weight: float32 [3, 1024, 1024], P(None, 'seq', 'head'), may hold values from -0.1875 to 0.1875
- qkv_first: float32 [3, 1024, 1024], P(None, 'seq', 'head'), may hold values from -40 to 40
- qkv_second: float32 [3, 1024, 1024], P(None, 'seq', 'head'), may hold values from 4.096 to 16.384
- proj_weight: float32 [1024, 1024], P('head', 'seq'), may hold values from -3 to 3
- proj_first: float32 [1024, 1024], P('head', 'seq'), may hold values from -6 to 6
- proj_second: float32 [1024, 1024], P('head', 'seq'), may hold values from 0.016 to 0.064
- up_weight: float32 [1024, 4096], P('seq', 'head'), may hold values from -0.1875 to 0.1875
- up_first: float32 [1024, 4096], P('seq', 'head'), may hold values from -6 to 6
- up_second: float32 [1024, 4096], P('seq', 'head'), may hold values from 0.256 to 1.024
- down_weight: float32 [4096, 1024], P('head', 'seq'), may hold values from -0.09375 to 0.09375
- down_first: float32 [4096, 1024], P('head', 'seq'), may hold values from -20 to 20
- down_second: float32 [4096, 1024], P('head', 'seq'), may hold values from 1.024 to 4.096
- vec_params: float32 [9, 1024], replicated, may hold values from -1 to 1.83, as said below
- vec_first: float32 [9, 1024], replicated, may hold values from -40 to 40
- vec_second: float32 [9, 1024], replicated, may hold values from 4.096 to 16.384
Outputs:
- layer_output: bfloat16 [4, 1024, 1024], P(None, 'seq')
- input_grad: float32 [4, 1024, 1024], P(None, 'seq')
- qkv_new: float32 [3, 1024, 1024], P(None, 'seq', 'head')
- qkv_first_new: float32 [3, 1024, 1024], P(None, 'seq', 'head')
- qkv_second_new: float32 [3, 1024, 1024], P(None, 'seq', 'head')
- qkv_copy: bfloat16 [3, 1024, 1024], P(None, 'seq', 'head')
- proj_new: float32 [1024, 1024], P('head', 'seq')
- proj_first_new: float32 [1024, 1024], P('head', 'seq')
- proj_second_new: float32 [1024, 1024], P('head', 'seq')
- proj_copy: bfloat16 [1024, 1024], P('head', 'seq')
- up_new: float32 [1024, 4096], P('seq', 'head')
- up_first_new: float32 [1024, 4096], P('seq', 'head')
- up_second_new: float32 [1024, 4096], P('seq', 'head')
- up_copy: bfloat16 [1024, 4096], P('seq', 'head')
- down_new: float32 [4096, 1024], P('head', 'seq')
- down_first_new: float32 [4096, 1024], P('head', 'seq')
- down_second_new: float32 [4096, 1024], P('head', 'seq')
- down_copy: bfloat16 [4096, 1024], P('head', 'seq')
- vec_new: float32 [9, 1024], replicated
- vec_first_new: float32 [9, 1024], replicated
- vec_second_new: float32 [9, 1024], replicated
Inputs may be any that keep to these rules, and one draw needn't show every extreme that they name: `doc_blocks`: blocks taken by each of 8 documents packed in order; they sum to 64, and one document has exactly 32. `last_fill`: tokens of a document's last block that belong to it. `shard_owner`: A permutation: every index of seq owns exactly one block of weight rows. `vec_params`: rows 0 and 2 are the two norms' gains, rows 1 and 3 their shifts, row 4 the bias of the second feed-forward projection, rows 5 to 8 the bias of the first, 1024 values to a row; gains are positive.
All inputs are finite; a program needn't handle non-finite values.
Results may differ from a plain program's by a relative error of at most 0.015.
Values may be sent and summed in bfloat16 or wider, within the bound.
No kernel may reach another device: no remote copies, remote signals or barrier semaphores. Data moves between devices by JAX's collectives and lax.ppermute only.
A program may use at most 256 MiB of HBM per device.

v0:
```python
import jax
import jax.numpy as jnp
from jax import lax
from jax.sharding import PartitionSpec as P

D = 1024
DH = 64
FF = 4096
BLOCK = 64
STEP = 10


eps_norm = 1e-05
masked_score = -1e30
beta_one = 0.9
beta_two = 0.999
eps_adam = 1e-08
decay_rate = 0.01
rate_qkv = 0.1
rate_proj = 1.0
rate_up = 0.1
rate_down = 0.05
rate_vector = 2.0


def with_halo(block, sides, width):
    for axis, dim in sides:
        count = lax.axis_size(axis)
        forward = [(i, i + 1) for i in range(count - 1)]
        forward.append((count - 1, 0))
        backward = [(target, source) for source, target in forward]
        low = lax.ppermute(
            lax.slice_in_dim(block, block.shape[dim] - width, None, axis=dim), axis, forward
        )
        high = lax.ppermute(lax.slice_in_dim(block, 0, width, axis=dim), axis, backward)
        block = jnp.concatenate([low, block, high], axis=dim)
    return block


def shifted(value, axis, steps):
    count = lax.axis_size(axis)
    pairs = [(source, (source + steps) % count) for source in range(count)]
    return lax.ppermute(value, axis, pairs)


def lookup(index_table, index_rows):
    matches = index_rows[..., None] == jnp.arange(index_table.shape[0], dtype=jnp.int32)
    return jnp.sum(jnp.where(matches, index_table, 0), axis=-1)


def owning_doc(doc_end, block_ids):
    return jnp.sum((block_ids[..., None] >= doc_end).astype(jnp.int32), axis=-1)


def doc_tables(doc_blocks, last_fill):
    doc_end = jnp.cumsum(doc_blocks)
    doc_start = doc_end - doc_blocks
    doc_length = (doc_blocks - 1) * BLOCK + last_fill
    return (doc_end, doc_start, doc_length)


def key_lists(query_ids, pick_table, doc_blocks, last_fill, block_total):
    doc_end, doc_start, doc_length = doc_tables(doc_blocks, last_fill)
    query_doc = owning_doc(doc_end, query_ids)
    doc_first = lookup(doc_start, query_doc)
    doc_count = lookup(doc_blocks, query_doc)
    query_length = lookup(doc_length, query_doc)
    head_count = pick_table.shape[1]
    fixed_ids = jnp.stack(
        [
            (query_ids - 1) % block_total,
            query_ids,
            (query_ids + 1) % block_total,
            doc_first,
            (doc_first + 1) % block_total,
        ],
        axis=-1,
    )
    random_ids = doc_first[:, None, None] + pick_table % doc_count[:, None, None]
    key_ids = jnp.concatenate(
        [jnp.broadcast_to(fixed_ids[:, None, :], (query_ids.shape[0], head_count, 5)), random_ids],
        axis=-1,
    )
    key_pos = (key_ids - doc_first[:, None, None])[..., None] * BLOCK + jnp.arange(
        BLOCK, dtype=jnp.int32
    )
    same_doc = owning_doc(doc_end, key_ids) == query_doc[:, None, None]
    key_live = same_doc[..., None] & (key_pos < query_length[:, None, None, None])
    return (key_ids, key_live)


def norm_rows(token_rows, gain_row, bias_row):
    row_mean = jnp.mean(token_rows, axis=-1, keepdims=True)
    centred = token_rows - row_mean
    row_var = jnp.mean(centred * centred, axis=-1, keepdims=True)
    inv_scale = lax.rsqrt(row_var + eps_norm)
    unit_rows = centred * inv_scale
    return (unit_rows * gain_row + bias_row, unit_rows, inv_scale)


def norm_back(grad_in, unit_rows, inv_scale, gain_row):
    scaled = grad_in * gain_row
    first_mean = jnp.mean(scaled, axis=-1, keepdims=True)
    second_mean = jnp.mean(scaled * unit_rows, axis=-1, keepdims=True)
    return inv_scale * (scaled - first_mean - unit_rows * second_mean)


def gelu_tanh(values):
    return jax.nn.gelu(values, approximate=True)


def reorder(weight, dim_pos, index_table, lane_count):
    moved_axis = jnp.moveaxis(weight, dim_pos, 0)
    shaped = moved_axis.reshape(
        (lane_count, moved_axis.shape[0] // lane_count) + moved_axis.shape[1:]
    )
    picked = jnp.take(shaped, index_table, axis=0)
    return jnp.moveaxis(picked.reshape(moved_axis.shape), 0, dim_pos)


def adam_step(param_old, gradient, first_old, second_old, step_rate):
    first_new = beta_one * first_old + (1.0 - beta_one) * gradient
    second_new = beta_two * second_old + (1.0 - beta_two) * gradient * gradient
    first_hat = first_new / (1.0 - beta_one**STEP)
    second_hat = second_new / (1.0 - beta_two**STEP)
    updated = param_old - step_rate * (
        first_hat / (jnp.sqrt(second_hat) + eps_adam) + decay_rate * param_old
    )
    return (updated, first_new, second_new)


def head_total(partial_rows):
    return lax.psum(partial_rows.astype(jnp.bfloat16), "head").astype(jnp.float32)


def body(
    layer_input,
    output_grad,
    random_pick,
    doc_blocks,
    last_fill,
    shard_owner,
    qkv_weight,
    qkv_first,
    qkv_second,
    proj_weight,
    proj_first,
    proj_second,
    up_weight,
    up_first,
    up_second,
    down_weight,
    down_first,
    down_second,
    vec_params,
    vec_first,
    vec_second,
):
    lane_count = lax.axis_size("seq")
    lane_index = lax.axis_index("seq")
    head_count_axis = lax.axis_size("head")
    head_index = lax.axis_index("head")
    blocks_here = layer_input.shape[0]
    head_here = random_pick.shape[2]
    feat_width = head_here * DH
    units_here = up_weight.shape[1]
    row_count = blocks_here * BLOCK
    block_total = blocks_here * lane_count
    score_scale = DH ** (-0.5)
    token_rows = layer_input.reshape(row_count, D).astype(jnp.float32)
    grad_rows = output_grad.reshape(row_count, D).astype(jnp.float32)
    query_ids = jnp.arange(blocks_here, dtype=jnp.int32) * lane_count + lane_index
    key_ids, key_live = key_lists(query_ids, random_pick[:, 0], doc_blocks, last_fill, block_total)
    far_owner = key_ids[:, :, 3:] % lane_count
    far_slot = key_ids[:, :, 3:] // lane_count
    head_pick = jnp.arange(head_here, dtype=jnp.int32)[None, :, None]
    inverse = (
        jnp.zeros((lane_count,), jnp.int32)
        .at[shard_owner]
        .set(jnp.arange(lane_count, dtype=jnp.int32))
    )
    lowered = (
        qkv_weight.astype(jnp.bfloat16),
        proj_weight.astype(jnp.bfloat16),
        up_weight.astype(jnp.bfloat16),
        down_weight.astype(jnp.bfloat16),
    )
    gathered = (
        lax.all_gather(lowered[0], "seq", axis=1, tiled=True),
        lax.all_gather(lowered[1], "seq", axis=1, tiled=True),
        lax.all_gather(lowered[2], "seq", axis=0, tiled=True),
        lax.all_gather(lowered[3], "seq", axis=1, tiled=True),
    )
    qkv_full = reorder(gathered[0], 1, shard_owner, lane_count)
    proj_full = reorder(gathered[1], 1, shard_owner, lane_count)
    up_full = reorder(gathered[2], 0, shard_owner, lane_count)
    down_full = reorder(gathered[3], 1, shard_owner, lane_count)
    up_bias = lax.dynamic_slice_in_dim(
        vec_params[5:].reshape(FF), head_index * units_here, units_here
    )

    def gather_keys(kv_local):
        extended = with_halo(kv_local[None], (("seq", 0),), 1)
        prev_blocks = jnp.where(lane_index == 0, jnp.roll(extended[0], 1, axis=0), extended[0])
        next_blocks = jnp.where(
            lane_index == lane_count - 1, jnp.roll(extended[2], -1, axis=0), extended[2]
        )
        window = jnp.stack([prev_blocks, kv_local, next_blocks], axis=1)
        window = window.reshape(blocks_here, 3, BLOCK, head_here, 2 * DH).transpose(0, 3, 1, 2, 4)
        empty_blocks = jnp.zeros((blocks_here, head_here, 5, BLOCK, 2 * DH), jnp.bfloat16)
        pieces = lax.all_gather(kv_local[None], "seq", axis=0, tiled=True)
        piece_count = pieces.shape[0]
        flat_rows = pieces.reshape(piece_count * blocks_here, BLOCK, head_here, 2 * DH)
        inside = (far_owner >= 0) & (far_owner < piece_count)
        source = jnp.clip(far_owner, 0, piece_count - 1) * blocks_here + far_slot
        picked = flat_rows[source, :, head_pick, :]
        far_blocks = jnp.where(inside[..., None, None], picked, empty_blocks)
        return jnp.concatenate([window, far_blocks], axis=2)

    def score_rows(queries, kv_all):
        scores = (
            jnp.einsum(
                "bthd,bhckd->bhtck", queries, kv_all[..., :DH], preferred_element_type=jnp.float32
            )
            * score_scale
        )
        return jnp.where(key_live[:, :, None], scores, masked_score)

    def forward_pass(rows_in, qkv_in, proj_in, up_in, down_in):
        normed_one, unit_one, scale_one = norm_rows(rows_in, vec_params[0], vec_params[1])
        low_one = normed_one.astype(jnp.bfloat16)
        qkv_rows = jnp.einsum(
            "td,cde->cte", low_one, qkv_in, preferred_element_type=jnp.float32
        ).astype(jnp.bfloat16)
        queries = qkv_rows[0].reshape(blocks_here, BLOCK, head_here, DH)
        kv_local = jnp.stack(
            [
                qkv_rows[1].reshape(blocks_here, BLOCK, head_here, DH),
                qkv_rows[2].reshape(blocks_here, BLOCK, head_here, DH),
            ],
            axis=3,
        )
        kv_local = kv_local.reshape(blocks_here, BLOCK, head_here * 2 * DH)
        kv_all = gather_keys(kv_local)
        masked = score_rows(queries, kv_all)
        row_max = jnp.max(masked, axis=(3, 4), keepdims=True)
        exp_scores = jnp.exp(masked - row_max)
        exp_total = jnp.sum(exp_scores, axis=(3, 4), keepdims=True)
        attn_probs = (exp_scores / exp_total).astype(jnp.bfloat16)
        log_total = row_max + jnp.log(exp_total)
        context = jnp.einsum(
            "bhtck,bhckd->bthd", attn_probs, kv_all[..., DH:], preferred_element_type=jnp.float32
        ).astype(jnp.bfloat16)
        context = context.reshape(row_count, feat_width)
        attn_sum = lax.psum(
            jnp.dot(context, proj_in, preferred_element_type=jnp.float32).astype(jnp.bfloat16),
            "head",
        ).astype(jnp.float32)
        mid_rows = rows_in + attn_sum
        normed_two, unit_two, scale_two = norm_rows(mid_rows, vec_params[2], vec_params[3])
        low_two = normed_two.astype(jnp.bfloat16)
        hidden = jnp.dot(low_two, up_in, preferred_element_type=jnp.float32) + up_bias
        active = gelu_tanh(hidden).astype(jnp.bfloat16)
        ffn_sum = lax.psum(
            jnp.dot(active, down_in, preferred_element_type=jnp.float32).astype(jnp.bfloat16),
            "head",
        ).astype(jnp.float32)
        result = mid_rows + ffn_sum + vec_params[4]
        kept_state = (
            low_one,
            unit_one,
            scale_one,
            queries,
            kv_all,
            log_total,
            context,
            unit_two,
            scale_two,
            low_two,
            hidden,
            active,
        )
        return (result, kept_state)

    result_first, unused_state = forward_pass(token_rows, qkv_full, proj_full, up_full, down_full)
    barrier_out = lax.optimization_barrier(
        (token_rows, qkv_full, proj_full, up_full, down_full, result_first)
    )
    result = barrier_out[5]
    result_again, kept_state = forward_pass(
        barrier_out[0], barrier_out[1], barrier_out[2], barrier_out[3], barrier_out[4]
    )
    (
        low_one,
        unit_one,
        scale_one,
        queries,
        kv_all,
        log_total,
        context,
        unit_two,
        scale_two,
        low_two,
        hidden,
        active,
    ) = kept_state
    grad_low = grad_rows.astype(jnp.bfloat16)
    down_grad = jnp.dot(active.T, grad_low, preferred_element_type=jnp.float32)
    act_grad = jnp.dot(grad_low, down_full.T, preferred_element_type=jnp.float32)
    hidden_grad = jax.vjp(gelu_tanh, hidden)[1](act_grad)[0]
    up_bias_grad = jnp.sum(hidden_grad, axis=0)
    hidden_low = hidden_grad.astype(jnp.bfloat16)
    up_grad = jnp.dot(low_two.T, hidden_low, preferred_element_type=jnp.float32)
    two_grad = head_total(jnp.dot(hidden_low, up_full.T, preferred_element_type=jnp.float32))
    mid_grad = grad_rows + norm_back(two_grad, unit_two, scale_two, vec_params[2])
    attn_low = mid_grad.astype(jnp.bfloat16)
    proj_grad = jnp.dot(context.T, attn_low, preferred_element_type=jnp.float32)
    ctx_grad = jnp.dot(attn_low, proj_full.T, preferred_element_type=jnp.float32).astype(
        jnp.bfloat16
    )
    ctx_grad = ctx_grad.reshape(blocks_here, BLOCK, head_here, DH)
    masked = score_rows(queries, kv_all)
    attn_probs = jnp.exp(masked - log_total)
    probs_low = attn_probs.astype(jnp.bfloat16)
    val_grad = jnp.einsum(
        "bhtck,bthd->bhckd", probs_low, ctx_grad, preferred_element_type=jnp.float32
    )
    prob_grad = jnp.einsum(
        "bthd,bhckd->bhtck", ctx_grad, kv_all[..., DH:], preferred_element_type=jnp.float32
    )
    row_dot = jnp.sum(attn_probs * prob_grad, axis=(3, 4), keepdims=True)
    score_low = (attn_probs * (prob_grad - row_dot)).astype(jnp.bfloat16)
    query_grad = (
        jnp.einsum(
            "bhtck,bhckd->bthd", score_low, kv_all[..., :DH], preferred_element_type=jnp.float32
        )
        * score_scale
    )
    key_grad = (
        jnp.einsum("bhtck,bthd->bhckd", score_low, queries, preferred_element_type=jnp.float32)
        * score_scale
    )
    kv_grad = jnp.concatenate([key_grad, val_grad], axis=-1)
    window_grad = (
        kv_grad[:, :, :3]
        .transpose(0, 2, 3, 1, 4)
        .reshape(blocks_here, 3, BLOCK, head_here * 2 * DH)
    )
    send_back = jnp.where(
        lane_index == 0, jnp.roll(window_grad[:, 0], -1, axis=0), window_grad[:, 0]
    )
    from_next = shifted(send_back.astype(jnp.bfloat16), "seq", -1).astype(send_back.dtype)
    send_ahead = jnp.where(
        lane_index == lane_count - 1, jnp.roll(window_grad[:, 2], 1, axis=0), window_grad[:, 2]
    )
    from_prev = shifted(send_ahead.astype(jnp.bfloat16), "seq", 1).astype(send_ahead.dtype)
    flat_grad = kv_grad[:, :, 3:].reshape(blocks_here * head_here * 5, BLOCK, 2 * DH)
    piece_count = lax.axis_size("seq") * 1
    inside = (far_owner >= 0) & (far_owner < piece_count)
    target = (far_owner * blocks_here + far_slot) * head_here + head_pick
    target = jnp.where(inside, target, piece_count * blocks_here * head_here).reshape(-1)
    summed = jax.ops.segment_sum(
        flat_grad, target, num_segments=piece_count * blocks_here * head_here
    )
    summed = summed.reshape(piece_count, blocks_here, head_here, BLOCK, 2 * DH).transpose(
        0, 1, 3, 2, 4
    )
    far_back = lax.psum_scatter(
        summed.reshape(piece_count, blocks_here, BLOCK, head_here * 2 * DH),
        "seq",
        scatter_dimension=0,
        tiled=True,
    )
    kv_local_grad = window_grad[:, 1] + from_next + from_prev + far_back[0]
    kv_split = kv_local_grad.reshape(blocks_here, BLOCK, head_here, 2, DH)
    qkv_grad_low = jnp.stack(
        [
            query_grad.reshape(row_count, feat_width),
            kv_split[:, :, :, 0].reshape(row_count, feat_width),
            kv_split[:, :, :, 1].reshape(row_count, feat_width),
        ]
    ).astype(jnp.bfloat16)
    qkv_grad = jnp.einsum("td,cte->cde", low_one, qkv_grad_low, preferred_element_type=jnp.float32)
    one_grad = head_total(
        jnp.einsum("cte,cde->td", qkv_grad_low, qkv_full, preferred_element_type=jnp.float32)
    )
    input_grad = mid_grad + norm_back(one_grad, unit_one, scale_one, vec_params[0])
    shared_rows = jnp.stack(
        [
            jnp.sum(one_grad * unit_one, axis=0),
            jnp.sum(one_grad, axis=0),
            jnp.sum(two_grad * unit_two, axis=0),
            jnp.sum(two_grad, axis=0),
            jnp.sum(grad_rows, axis=0),
        ]
    )
    column_group = jnp.arange(D, dtype=jnp.int32) // (D // head_count_axis)
    shared_rows = jnp.where(
        (column_group == head_index)[None, :], shared_rows, jnp.zeros_like(shared_rows)
    )
    bias_rows = lax.dynamic_update_slice_in_dim(
        jnp.zeros((FF,), jnp.float32), up_bias_grad, head_index * units_here, 0
    ).reshape(FF // D, D)
    vec_grad = lax.psum(jnp.concatenate([shared_rows, bias_rows], axis=0), ("seq", "head"))
    owned_grads = (
        lax.psum_scatter(
            reorder(qkv_grad, 1, inverse, lane_count), "seq", scatter_dimension=1, tiled=True
        ),
        lax.psum_scatter(
            reorder(proj_grad, 1, inverse, lane_count), "seq", scatter_dimension=1, tiled=True
        ),
        lax.psum_scatter(
            reorder(up_grad, 0, inverse, lane_count), "seq", scatter_dimension=0, tiled=True
        ),
        lax.psum_scatter(
            reorder(down_grad, 1, inverse, lane_count), "seq", scatter_dimension=1, tiled=True
        ),
    )
    input_grad, owned_grads, vec_grad = (input_grad, owned_grads, vec_grad)
    qkv_new, qkv_first_new, qkv_second_new = adam_step(
        qkv_weight, owned_grads[0], qkv_first, qkv_second, rate_qkv
    )
    proj_new, proj_first_new, proj_second_new = adam_step(
        proj_weight, owned_grads[1], proj_first, proj_second, rate_proj
    )
    up_new, up_first_new, up_second_new = adam_step(
        up_weight, owned_grads[2], up_first, up_second, rate_up
    )
    down_new, down_first_new, down_second_new = adam_step(
        down_weight, owned_grads[3], down_first, down_second, rate_down
    )
    vec_new, vec_first_new, vec_second_new = adam_step(
        vec_params, vec_grad, vec_first, vec_second, rate_vector
    )
    layer_output = result.astype(jnp.bfloat16).reshape(blocks_here, BLOCK, D)
    return (
        layer_output,
        input_grad.reshape(blocks_here, BLOCK, D),
        qkv_new,
        qkv_first_new,
        qkv_second_new,
        qkv_new.astype(jnp.bfloat16),
        proj_new,
        proj_first_new,
        proj_second_new,
        proj_new.astype(jnp.bfloat16),
        up_new,
        up_first_new,
        up_second_new,
        up_new.astype(jnp.bfloat16),
        down_new,
        down_first_new,
        down_second_new,
        down_new.astype(jnp.bfloat16),
        vec_new,
        vec_first_new,
        vec_second_new,
    )


def solution(mesh):
    placed = (
        P(None, "seq", None),
        P(None, "seq", None),
        P(None, "seq", "head", None),
        P(),
        P(),
        P(),
        P(None, "seq", "head"),
        P(None, "seq", "head"),
        P(None, "seq", "head"),
        P("head", "seq"),
        P("head", "seq"),
        P("head", "seq"),
        P("seq", "head"),
        P("seq", "head"),
        P("seq", "head"),
        P("head", "seq"),
        P("head", "seq"),
        P("head", "seq"),
        P(),
        P(),
        P(),
    )
    return jax.shard_map(
        body,
        mesh=mesh,
        in_specs=placed,
        out_specs=(
            P(None, "seq", None),
            P(None, "seq", None),
            P(None, "seq", "head"),
            P(None, "seq", "head"),
            P(None, "seq", "head"),
            P(None, "seq", "head"),
            P("head", "seq"),
            P("head", "seq"),
            P("head", "seq"),
            P("head", "seq"),
            P("seq", "head"),
            P("seq", "head"),
            P("seq", "head"),
            P("seq", "head"),
            P("head", "seq"),
            P("head", "seq"),
            P("head", "seq"),
            P("head", "seq"),
            P(),
            P(),
            P(),
        ),
        check_vma=False,
    )
```

profile of v0, /device:TPU:0, one launch (start us, length us, event | category | flops | bytes accessed | tf_op | source)
XLA Modules:
  0.0 1279.7 jit_solution(16222964425661885140)
XLA Ops:
  19.0 39.8 %all-gather.7.cloned.1.call-done = bf16[3,1024,512]{2,1,0:T(8,128)(2,1)} async-done(((bf16[3,64,512]{2,1,0:T(8,128)(2,1)}), bf16[3,1024,512]{2,1,0:T(8,128)(2,1)}) %all-gather.7.cloned.1.call-update) | async-done | bytes 3145744 | tf_op jit(solution)/shard_map/all_gather | solution.py:189
  68.7 3.9 pad_maximum_fusion.14
  78.9 22.9 %all-gather.9.cloned.1.call-done = bf16[512,1024]{0,1:T(8,128)(2,1)} async-done(((bf16[512,64]{0,1:T(8,128)(2,1)}), bf16[512,1024]{0,1:T(8,128)(2,1)}) %all-gather.9.cloned.1.call-update) | async-done | bytes 1048592 | tf_op jit(solution)/shard_map/all_gather | solution.py:190
  114.6 38.8 %all-gather.11.cloned.1.call-done = bf16[1024,2048]{1,0:T(8,128)(2,1)} async-done(((bf16[64,2048]{1,0:T(8,128)(2,1)}), bf16[1024,2048]{1,0:T(8,128)(2,1)}) %all-gather.11.cloned.1.call-update) | async-done | bytes 4194320 | tf_op jit(solution)/shard_map/all_gather | solution.py:191
  153.4 5.0 gather_fusion.6
  158.3 46.7 %all-gather.15.cloned.1.call-done = bf16[2048,1024]{0,1:T(8,128)(2,1)} async-done(((bf16[2048,64]{0,1:T(8,128)(2,1)}), bf16[2048,1024]{0,1:T(8,128)(2,1)}) %all-gather.15.cloned.1.call-update) | async-done | bytes 4194320 | tf_op jit(solution)/shard_map/all_gather | solution.py:192
  205.0 5.0 gather_fusion.7
  210.0 71.0 %all-gather.13.cloned.1.call-done = bf16[16,4,64,1024]{3,2,1,0:T(8,128)(2,1)} async-done(((bf16[1,4,64,1024]{3,2,1,0:T(8,128)(2,1)}), bf16[16,4,64,1024]{3,2,1,0:T(8,128)(2,1)}) %all-gather.13.cloned.1.call-update) | async-done | bytes 8388624 | tf_op jit(solution)/shard_map/all_gather | solution.py:211
  281.1 8.8 copy.307
  289.8 9.3 copy.228
  299.2 7.0 gather_fusion.2
  308.3 7.1 fusion
  315.5 3.3 fusion.2
  318.8 10.4 fusion.59
  332.4 7.5 broadcast_select_fusion.2
  339.9 19.2 %all-reduce.6.cloned.1.call-done = bf16[256,1024]{1,0:T(8,128)(2,1)} async-done(((bf16[256,1024]{1,0:T(8,128)(2,1)}), bf16[256,1024]{1,0:T(8,128)(2,1)}) %all-reduce.6.cloned.1.call-update) | async-done | bytes 524304 | tf_op jit(solution)/shard_map/psum | solution.py:255
  361.8 7.2 convolution_convert_fusion.5
  370.4 27.4 %all-reduce.8.cloned.1.call-done = bf16[256,1024]{1,0:T(8,128)(2,1)} async-done(((bf16[256,1024]{1,0:T(8,128)(2,1)}), bf16[256,1024]{1,0:T(8,128)(2,1)}) %all-reduce.8.cloned.1.call-update) | async-done | bytes 524304 | tf_op jit(solution)/shard_map/psum | solution.py:264
  400.3 3.0 fusion.51
  407.0 3.9 pad_maximum_fusion.15
  412.5 3.7 collective-permute-start.3
  417.9 8.5 collective-permute-done.3
  426.6 4.9 collective-permute-done.2
  436.4 52.2 %all-gather.17.cloned.1.call-done = bf16[16,4,64,1024]{3,2,1,0:T(8,128)(2,1)} async-done(((bf16[1,4,64,1024]{3,2,1,0:T(8,128)(2,1)}), bf16[16,4,64,1024]{3,2,1,0:T(8,128)(2,1)}) %all-gather.17.cloned.1.call-update) | async-done | bytes 8388624 | tf_op jit(solution)/shard_map/all_gather | solution.py:211
  488.6 8.8 copy.313
  497.4 9.3 copy.243
  506.7 7.0 gather_fusion.3
  515.7 7.4 fusion.20
  523.2 3.3 fusion.1
  526.5 9.7 fusion.58
  538.3 26.9 %all-reduce.10.cloned.1.call-done = bf16[256,1024]{1,0:T(8,128)(2,1)} async-done(((bf16[256,1024]{1,0:T(8,128)(2,1)}), bf16[256,1024]{1,0:T(8,128)(2,1)}) %all-reduce.10.cloned.1.call-update) | async-done | bytes 524304 | tf_op jit(solution)/shard_map/psum | solution.py:255
  566.7 3.7 convolution_add_fusion
  570.5 3.0 fusion.168
  577.0 28.4 %all-reduce.12.cloned.1.call-done = bf16[256,1024]{1,0:T(8,128)(2,1)} async-done(((bf16[256,1024]{1,0:T(8,128)(2,1)}), bf16[256,1024]{1,0:T(8,128)(2,1)}) %all-reduce.12.cloned.1.call-update) | async-done | bytes 524304 | tf_op jit(solution)/shard_map/psum | solution.py:133
  612.8 7.0 fusion.4
  619.9 8.7 multiply_reduce_fusion
  628.7 3.8 multiply_convert_fusion
  634.5 4.3 pad_maximum_fusion
  639.3 7.9 broadcast_in_dim.224
  647.2 25.1 %scatter_fusion = f32[512,64,128]{2,1,0:T(8,128)} fusion(f32[512,64,128]{2,1,0:T(8,128)} %broadcast_in_dim.224, s32[160]{0:T(256)S(1)} %reshape.793, f32[160,64,128]{2,1,0:T(8,128)} %bitcast.336), kind=kCustom, calls=%fused_computation.10 | custom fusion | flops 1310720 | bytes 15729280 | tf_op jit(solution)/shard_map/scatter-add | solution.py:362
  672.3 11.8 copy.338
  691.4 4.1 gather_fusion.5
  695.6 3.5 bitcast_select_fusion.2
  699.3 7.5 fusion.91
  706.8 9.1 gather_fusion.8
  715.9 6.5 fusion.72
  722.4 7.7 gather_fusion.9
  730.1 11.1 broadcast_select_fusion
  741.9 3.9 copy_bitcast_fusion.1
  748.8 3.3 collective-permute-start.4
  755.3 15.2 %collective-permute-done.4 = bf16[4,64,1024]{2,1,0:T(8,128)(2,1)} collective-permute-done((bf16[4,64,1024]{2,1,0:T(8,128)(2,1)}, bf16[4,64,1024]{2,1,0:T(8,128)(2,1)}, u32[]{:S(2)}, u32[]{:S(2)}) %collective-permute-start.4) | collective-permute-done | bytes 524320 | tf_op jit(solution)/shard_map/ppermute | solution.py:43
  770.5 4.8 collective-permute-done.5
  775.3 92.9 %reduce-scatter.6.cloned.1.call-done = f32[1,4,64,1024]{3,2,1,0:T(8,128)} async-done(((f32[16,4,64,1024]{3,2,1,0:T(8,128)}), f32[1,4,64,1024]{3,2,1,0:T(8,128)}) %reduce-scatter.6.cloned.1.call-update) | async-done | bytes 1048592 | tf_op jit(solution)/shard_map/reduce_scatter | solution.py:368
  874.0 6.9 slice_reduce_fusion
  885.2 5.0 fusion.151
  890.1 6.4 gather_fusion.4
  896.5 7.1 copy.261
  905.8 6.0 bitcast_select_fusion
  917.0 15.5 %reduce-scatter.10.cloned.1.call-done = f32[512,64]{0,1:T(8,128)} async-done(((f32[512,1024]{0,1:T(8,128)}), f32[512,64]{0,1:T(8,128)}) %reduce-scatter.10.cloned.1.call-update) | async-done | bytes 131088 | tf_op jit(solution)/shard_map/reduce_scatter | solution.py:409
  934.2 106.5 %reduce-scatter.14.cloned.1.call-done = f32[2048,64]{0,1:T(8,128)} async-done(((f32[2048,1024]{0,1:T(8,128)}), f32[2048,64]{0,1:T(8,128)}) %reduce-scatter.14.cloned.1.call-update) | async-done | bytes 524304 | tf_op jit(solution)/shard_map/reduce_scatter | solution.py:415
  1043.5 106.0 %reduce-scatter.12.cloned.1.call-done = f32[64,2048]{1,0:T(8,128)} async-done(((f32[1024,2048]{1,0:T(8,128)}), f32[64,2048]{1,0:T(8,128)}) %reduce-scatter.12.cloned.1.call-update) | async-done | bytes 524304 | tf_op jit(solution)/shard_map/reduce_scatter | solution.py:412
  1152.4 28.3 %all-reduce.14.cloned.1.call-done = bf16[256,1024]{1,0:T(8,128)(2,1)} async-done(((bf16[256,1024]{1,0:T(8,128)(2,1)}), bf16[256,1024]{1,0:T(8,128)(2,1)}) %all-reduce.14.cloned.1.call-update) | async-done | bytes 524304 | tf_op jit(solution)/shard_map/psum | solution.py:133
  1184.5 39.8 %psum.47 = f32[9,1024]{1,0:T(8,128)S(1)} all-reduce(f32[9,1024]{1,0:T(8,128)S(1)} %pad_maximum_fusion.16), channel_id=1, replica_groups=mesh['seq'=16,'head'=2] {'seq','head'}, use_global_device_ids=true, to_apply=%region_41.44 | all-reduce | flops 9216 | bytes 73728 | tf_op jit(solution)/shard_map/psum | solution.py:404
  1228.3 42.1 %reduce-scatter.8.cloned.1.call-done = f32[3,64,512]{2,1,0:T(8,128)} async-done(((f32[3,1024,512]{2,1,0:T(8,128)}), f32[3,64,512]{2,1,0:T(8,128)}) %reduce-scatter.8.cloned.1.call-update) | async-done | bytes 393232 | tf_op jit(solution)/shard_map/reduce_scatter | solution.py:406
  (327 shorter events, 131.9 us)
Async XLA Ops:
  7.2 11.2 copy-start.59
  7.2 11.7 copy-start.39
  7.2 51.5 %all-gather.7.cloned.1.call-start = ((), (), s32[]{:S(2)}) async-start(), calls=%async_computation.5 | async-start | bytes 3342336 | tf_op jit(solution)/shard_map/all_gather | solution.py:189
  9.0 92.9 %all-gather.9.cloned.1.call-start = ((), (), s32[]{:S(2)}) async-start(), calls=%async_computation.6 | async-start | bytes 1114112 | tf_op jit(solution)/shard_map/all_gather | solution.py:190
  10.6 142.8 %all-gather.11.cloned.1.call-start = ((), (), s32[]{:S(2)}) async-start(), calls=%async_computation.7 | async-start | bytes 4456448 | tf_op jit(solution)/shard_map/all_gather | solution.py:191
  12.5 192.6 %all-gather.15.cloned.1.call-start = ((), (), s32[]{:S(2)}) async-start(), calls=%async_computation.10 | async-start | bytes 4456448 | tf_op jit(solution)/shard_map/all_gather | solution.py:192
  14.3 266.8 %all-gather.13.cloned.1.call-start = ((), (), s32[]{:S(2)}) async-start(), calls=%async_computation.8 | async-start | bytes 8912896 | tf_op jit(solution)/shard_map/all_gather | solution.py:211
  15.7 45.9 %copy-start.50 = (pred[1024]{0:T(1024)(128)(4,1)}, pred[1024]{0:T(1024)(128)(4,1)S(1)}, u32[]{:S(2)}) copy-start(pred[1024]{0:T(1024)(128)(4,1)S(1)} %broadcast_in_dim.206) | copy-start | bytes 3076
  19.0 381.4 %copy-start.42 = (f32[1,1024]{1,0:T(1,128)}, f32[1,1024]{1,0:T(1,128)S(1)}, u32[]{:S(2)}) copy-start(f32[1,1024]{1,0:T(1,128)S(1)} %get-tuple-element.87) | copy-start | bytes 12292
  19.0 381.4 %copy-start.46 = (f32[1,1024]{1,0:T(1,128)}, f32[1,1024]{1,0:T(1,128)S(1)}, u32[]{:S(2)}) copy-start(f32[1,1024]{1,0:T(1,128)S(1)} %get-tuple-element.86) | copy-start | bytes 12292
  66.4 7.8 copy-start.56
  66.4 8.2 copy-start.57
  66.5 8.6 copy-start.52
  68.7 34.9 %copy-start.54 = (pred[16]{0:T(512)(128)(4,1)S(1)}, pred[16]{0:T(512)(128)(4,1)}, u32[]{:S(2)}) copy-start(pred[16]{0:T(512)(128)(4,1)} %copy-done.53) | copy-start | bytes 52
  74.2 285.0 %all-reduce.6.cloned.1.call-start = ((), (), s32[]{:S(2)}) async-start(), calls=%async_computation.9 | async-start | bytes 1048576 | tf_op jit(solution)/shard_map/psum | solution.py:255
  76.3 30.1 %collective-permute-start.1 = (bf16[1,4,64,1024]{3,2,1,0:T(8,128)(2,1)}, bf16[1,4,64,1024]{3,2,1,0:T(8,128)(2,1)}, u32[]{:S(2)}, u32[]{:S(2)}) collective-permute-start(bf16[1,4,64,1024]{3,2,1,0:T(8,128)(2,1)} %broadcast_in_dim_reshape.11), channel_id=1, source_target_pairs={{2,0},{4,2},{6,4},{8,6},{10,8},{12,10},{14,12},{16,14},{18,16},{20... | collective-permute-start | bytes 1572872 | tf_op jit(solution)/shard_map/ppermute | solution.py:35
  78.4 30.4 %collective-permute-start = (bf16[1,4,64,1024]{3,2,1,0:T(8,128)(2,1)}, bf16[1,4,64,1024]{3,2,1,0:T(8,128)(2,1)}, u32[]{:S(2)}, u32[]{:S(2)}) collective-permute-start(bf16[1,4,64,1024]{3,2,1,0:T(8,128)(2,1)} %broadcast_in_dim_reshape.11), channel_id=1, source_target_pairs={{0,2},{2,4},{4,6},{6,8},{8,10},{10,12},{12,14},{14,16},{16,18},{18... | collective-permute-start | bytes 1572872 | tf_op jit(solution)/shard_map/ppermute | solution.py:32
  299.2 9.1 copy-start.36
  318.8 12.1 copy-start.15
  332.2 65.6 %all-reduce.8.cloned.1.call-start = ((), (), s32[]{:S(2)}) async-start(), calls=%async_computation.11 | async-start | bytes 1048576 | tf_op jit(solution)/shard_map/psum | solution.py:264
  361.8 7.4 copy-start.51
  369.0 28.8 %copy-start.9 = (bf16[256,1024]{1,0:T(8,128)(2,1)S(1)}, bf16[256,1024]{1,0:T(8,128)(2,1)}, u32[]{:S(2)}) copy-start(bf16[256,1024]{1,0:T(8,128)(2,1)} %all-reduce.6.cloned.1.call-done) | copy-start | bytes 1572868
  369.0 119.5 %all-gather.17.cloned.1.call-start = ((), (), s32[]{:S(2)}) async-start(), calls=%async_computation.12 | async-start | bytes 8912896 | tf_op jit(solution)/shard_map/all_gather | solution.py:211
  412.4 152.8 %all-reduce.10.cloned.1.call-start = ((), (), s32[]{:S(2)}) async-start(), calls=%async_computation.13 | async-start | bytes 1048576 | tf_op jit(solution)/shard_map/psum | solution.py:255
  412.5 13.9 %collective-permute-start.3 = (bf16[1,4,64,1024]{3,2,1,0:T(8,128)(2,1)}, bf16[1,4,64,1024]{3,2,1,0:T(8,128)(2,1)S(1)}, u32[]{:S(2)}, u32[]{:S(2)}) collective-permute-start(bf16[1,4,64,1024]{3,2,1,0:T(8,128)(2,1)} %broadcast_in_dim_reshape.12), channel_id=1, source_target_pairs={{2,0},{4,2},{6,4},{8,6},{10,8},{12,10},{14,12},{16,14},{18,16},{20... | collective-permute-start | bytes 1572872 | tf_op jit(solution)/shard_map/ppermute | solution.py:35
  416.2 15.3 %collective-permute-start.2 = (bf16[1,4,64,1024]{3,2,1,0:T(8,128)(2,1)}, bf16[1,4,64,1024]{3,2,1,0:T(8,128)(2,1)}, u32[]{:S(2)}, u32[]{:S(2)}) collective-permute-start(bf16[1,4,64,1024]{3,2,1,0:T(8,128)(2,1)} %broadcast_in_dim_reshape.12), channel_id=1, source_target_pairs={{0,2},{2,4},{4,6},{6,8},{8,10},{10,12},{12,14},{14,16},{16,18},{18... | collective-permute-start | bytes 1572872 | tf_op jit(solution)/shard_map/ppermute | solution.py:32
  417.7 98.0 %copy-start.25 = (bf16[4,64,8,64,1]{3,1,4,2,0:T(8,128)(2,1)}, bf16[4,64,8,64,1]{3,1,4,2,0:T(8,128)(2,1)S(1)}, u32[]{:S(2)}) copy-start(bf16[4,64,8,64,1]{3,1,4,2,0:T(8,128)(2,1)S(1)} %copy.269) | copy-start | bytes 786436
  506.7 9.1 copy-start.28
  515.7 10.7 copy-start.19
  526.5 10.4 copy-start.7
  536.6 33.9 %copy-start.8 = (bf16[4,64,8,64]{3,2,1,0:T(8,128)(2,1)}, bf16[4,64,8,64]{3,2,1,0:T(8,128)(2,1)S(1)}, u32[]{:S(2)}) copy-start(bf16[4,64,8,64]{3,2,1,0:T(8,128)(2,1)S(1)} %copy.247) | copy-start | bytes 786436
  538.2 67.2 %all-reduce.12.cloned.1.call-start = ((), (), s32[]{:S(2)}) async-start(), calls=%async_computation.14 | async-start | bytes 1048576 | tf_op jit(solution)/shard_map/psum | solution.py:133
  576.6 291.6 %reduce-scatter.6.cloned.1.call-start = ((), (), s32[]{:S(2)}) async-start(), calls=%async_computation.15 | async-start | bytes 17825792 | tf_op jit(solution)/shard_map/reduce_scatter | solution.py:368
  612.8 7.1 copy-start.20
  612.8 7.1 copy-start.27
  612.8 7.1 copy-start.30
  612.8 15.9 %slice-start = ((s8[8388608]{0:T(1024)(128)(4,1)}), s8[4194304]{0:T(1024)(128)(4,1)S(1)}, s32[]{:S(2)}) async-start(s8[8388608]{0:T(1024)(128)(4,1)} %bitcast.325), calls=%async_computation.21 | async-start | bytes 8388608
  619.9 13.9 %copy-start = (f32[4,8,8,64,64]{4,3,2,1,0:T(8,128)}, f32[4,8,8,64,64]{4,3,2,1,0:T(8,128)S(1)}, u32[]{:S(2)}) copy-start(f32[4,8,8,64,64]{4,3,2,1,0:T(8,128)S(1)} %fusion.4) | copy-start | bytes 12582916
  619.9 8.8 slice-start.1
  684.2 248.3 %reduce-scatter.10.cloned.1.call-start = ((), (), s32[]{:S(2)}) async-start(), calls=%async_computation.18 | async-start | bytes 2228224 | tf_op jit(solution)/shard_map/reduce_scatter | solution.py:409
  699.1 341.6 %reduce-scatter.14.cloned.1.call-start = ((), (), s32[]{:S(2)}) async-start(), calls=%async_computation.20 | async-start | bytes 8912896 | tf_op jit(solution)/shard_map/reduce_scatter | solution.py:415
  706.8 9.1 copy-start.11
  741.3 408.3 %reduce-scatter.12.cloned.1.call-start = ((), (), s32[]{:S(2)}) async-start(), calls=%async_computation.19 | async-start | bytes 8912896 | tf_op jit(solution)/shard_map/reduce_scatter | solution.py:412
  741.8 438.9 %all-reduce.14.cloned.1.call-start = ((), (), s32[]{:S(2)}) async-start(), calls=%async_computation.16 | async-start | bytes 1048576 | tf_op jit(solution)/shard_map/psum | solution.py:133
  741.9 10.4 copy-start.21
  741.9 10.4 copy-start.31
  745.9 6.5 copy-start.5
  748.8 21.7 %collective-permute-start.4 = (bf16[4,64,1024]{2,1,0:T(8,128)(2,1)}, bf16[4,64,1024]{2,1,0:T(8,128)(2,1)}, u32[]{:S(2)}, u32[]{:S(2)}) collective-permute-start(bf16[4,64,1024]{2,1,0:T(8,128)(2,1)} %get-tuple-element.71), channel_id=1, source_target_pairs={{0,30},{2,0},{4,2},{6,4},{8,6},{10,8},{12,10},{14,12},{16,14},{18,... | collective-permute-start | bytes 1572872 | tf_op jit(solution)/shard_map/ppermute | solution.py:43
  752.1 23.3 %collective-permute-start.5 = (bf16[4,64,1024]{2,1,0:T(8,128)(2,1)}, bf16[4,64,1024]{2,1,0:T(8,128)(2,1)}, u32[]{:S(2)}, u32[]{:S(2)}) collective-permute-start(bf16[4,64,1024]{2,1,0:T(8,128)(2,1)} %get-tuple-element.72), channel_id=1, source_target_pairs={{0,2},{2,4},{4,6},{6,8},{8,10},{10,12},{12,14},{14,16},{16,18},{18... | collective-permute-start | bytes 1572872 | tf_op jit(solution)/shard_map/ppermute | solution.py:43
  871.2 14.0 %copy-start.43 = (f32[1,1024]{1,0:T(1,128)S(1)}, f32[1,1024]{1,0:T(1,128)}, u32[]{:S(2)}) copy-start(f32[1,1024]{1,0:T(1,128)} %copy-done.42) | copy-start | bytes 12292
  871.2 14.0 %copy-start.45 = (f32[256]{0:T(256)S(1)}, f32[256]{0:T(256)}, u32[]{:S(2)}) copy-start(f32[256]{0:T(256)} %copy-done.44) | copy-start | bytes 3076
  871.2 14.0 %copy-start.47 = (f32[1,1024]{1,0:T(1,128)S(1)}, f32[1,1024]{1,0:T(1,128)}, u32[]{:S(2)}) copy-start(f32[1,1024]{1,0:T(1,128)} %copy-done.46) | copy-start | bytes 12292
  871.2 14.0 %copy-start.49 = (f32[256]{0:T(256)S(1)}, f32[256]{0:T(256)}, u32[]{:S(2)}) copy-start(f32[256]{0:T(256)} %copy-done.48) | copy-start | bytes 3076
  896.5 7.1 copy-start.18
  896.5 7.1 copy-start.22
  905.5 364.9 %reduce-scatter.8.cloned.1.call-start = ((), (), s32[]{:S(2)}) async-start(), calls=%async_computation.17 | async-start | bytes 6684672 | tf_op jit(solution)/shard_map/reduce_scatter | solution.py:406
  911.9 20.6 %copy-start.35 = (f32[512,64]{0,1:T(8,128)S(1)}, f32[512,64]{0,1:T(8,128)}, u32[]{:S(2)}) copy-start(f32[512,64]{0,1:T(8,128)} %param.34) | copy-start | bytes 393220
  911.9 20.6 %copy-start.40 = (f32[512,64]{0,1:T(8,128)S(1)}, f32[512,64]{0,1:T(8,128)}, u32[]{:S(2)}) copy-start(f32[512,64]{0,1:T(8,128)} %param.35) | copy-start | bytes 393220
  911.9 20.6 %copy-start.41 = (f32[512,64]{0,1:T(8,128)S(1)}, f32[512,64]{0,1:T(8,128)}, u32[]{:S(2)}) copy-start(f32[512,64]{0,1:T(8,128)} %param.36) | copy-start | bytes 393220
  911.9 128.8 %copy-start.23 = (f32[2048,64]{0,1:T(8,128)S(1)}, f32[2048,64]{0,1:T(8,128)}, u32[]{:S(2)}) copy-start(f32[2048,64]{0,1:T(8,128)} %param.40) | copy-start | bytes 1572868
  913.6 235.9 %copy-start.24 = (f32[64,2048]{1,0:T(8,128)S(1)}, f32[64,2048]{1,0:T(8,128)}, u32[]{:S(2)}) copy-start(f32[64,2048]{1,0:T(8,128)} %param.37) | copy-start | bytes 1572868
  1043.5 226.9 %copy-start.33 = (f32[3,64,512]{2,1,0:T(8,128)S(1)}, f32[3,64,512]{2,1,0:T(8,128)}, u32[]{:S(2)}) copy-start(f32[3,64,512]{2,1,0:T(8,128)} %param.31) | copy-start | bytes 1179652
  1043.5 226.9 %copy-start.37 = (f32[3,64,512]{2,1,0:T(8,128)S(1)}, f32[3,64,512]{2,1,0:T(8,128)}, u32[]{:S(2)}) copy-start(f32[3,64,512]{2,1,0:T(8,128)} %param.32) | copy-start | bytes 1179652
  1152.4 118.0 %copy-start.38 = (f32[3,64,512]{2,1,0:T(8,128)S(1)}, f32[3,64,512]{2,1,0:T(8,128)}, u32[]{:S(2)}) copy-start(f32[3,64,512]{2,1,0:T(8,128)} %param.33) | copy-start | bytes 1179652
  (20 other events, 52.9 us)
Sparse Core Ops, SparseCore 0:
  10.8 47.9 all-gather.6
  61.5 40.3 all-gather.8
  104.6 48.7 all-gather.10
  156.0 49.0 all-gather.14
  207.6 73.3 all-gather.12
  332.3 26.8 all-reduce.5
  369.1 28.5 all-reduce.7
  412.5 75.9 all-gather.16
  538.3 26.8 all-reduce.9
  576.7 28.5 all-reduce.11
  684.3 183.8 reduce-scatter.5
  871.8 60.5 reduce-scatter.9
  937.1 103.5 reduce-scatter.13
  1045.1 104.3 reduce-scatter.11
  1152.3 28.3 all-reduce.13
  1184.5 85.8 reduce-scatter.7
where the time goes:
time: 1290 us; the launch traced here: 1280 us
  waiting for transfers between devices  799 us (62%)
  local copies, waits for them, and re-layouts  177 us (14%)
  other arithmetic  135 us (10%)
  matrix products  101 us (8%)
  blocking collectives  39.8 us (3%)
  between operations  15.8 us (1%)
    all_gather x2, waiting for transfers between devices, gather_keys(): pieces = lax.all_gather(kv_local[None], 'seq', axis=0, tiled=True)  123 us
    reduce_scatter x1, waiting for transfers between devices, body(): lax.psum_scatter(reorder(down_grad, 1, inverse, lane_count), 'seq', scatt...  106 us
    reduce_scatter x1, waiting for transfers between devices, body(): lax.psum_scatter(reorder(up_grad, 0, inverse, lane_count), 'seq', scatter...  106 us
    reduce_scatter x1, waiting for transfers between devices, body(): lax.psum_scatter(summed.reshape(piece_count, blocks_here, BLOCK, head_her...  92.9 us
    psum x2, waiting for transfers between devices, head_total(): lax.psum(partial_rows.astype(jnp.bfloat16), 'head').astype(jnp.float32)  56.7 us
    gather x10, local copies, waits for them, and re-layouts, reorder(): picked = jnp.take(shaped, index_table, axis=0)  49 us
    all_gather x1, waiting for transfers between devices, body(): lax.all_gather(lowered[3], 'seq', axis=1, tiled=True)  46.7 us
    psum x2, waiting for transfers between devices, forward_pass(): lax.psum(jnp.dot(context, proj_in, preferred_element_type=jnp.float32).as...  46.2 us
  transfers between devices with their start and end apart: 22, of which 20 were waited for; matrix products, arithmetic and copies ran while one was open for 15% of the time, Pallas kernels for 0%

commit v1 on v0

v1 whole, which is shorter than its diff:
```python
import functools

import jax
import jax.numpy as jnp
from jax import lax
from jax.experimental import pallas as pl
from jax.experimental.pallas import tpu as pltpu
from jax.sharding import PartitionSpec as P

D = 1024
DH = 64
FF = 4096
BLOCK = 64
STEP = 10
LISTED = 8

eps_norm = 1e-05
masked_score = -1e30
beta_one = 0.9
beta_two = 0.999
eps_adam = 1e-08
decay_rate = 0.01
rate_qkv = 0.1
rate_proj = 1.0
rate_up = 0.1
rate_down = 0.05
rate_vector = 2.0

bf16 = jnp.bfloat16
f32 = jnp.float32


def lookup(index_table, index_rows):
    matches = index_rows[..., None] == jnp.arange(index_table.shape[0], dtype=jnp.int32)
    return jnp.sum(jnp.where(matches, index_table, 0), axis=-1)


def owning_doc(doc_end, block_ids):
    return jnp.sum((block_ids[..., None] >= doc_end).astype(jnp.int32), axis=-1)


def dot(lhs, rhs, lhs_dim, rhs_dim):
    return lax.dot_general(
        lhs, rhs, (((lhs_dim,), (rhs_dim,)), ((), ())), preferred_element_type=f32
    )


def norm_rows(token_rows, gain_row, bias_row):
    row_mean = jnp.mean(token_rows, axis=-1, keepdims=True)
    centred = token_rows - row_mean
    row_var = jnp.mean(centred * centred, axis=-1, keepdims=True)
    inv_scale = lax.rsqrt(row_var + eps_norm)
    unit_rows = centred * inv_scale
    return (unit_rows * gain_row + bias_row, unit_rows, inv_scale)


def norm_back(grad_in, unit_rows, inv_scale, gain_row):
    scaled = grad_in * gain_row
    first_mean = jnp.mean(scaled, axis=-1, keepdims=True)
    second_mean = jnp.mean(scaled * unit_rows, axis=-1, keepdims=True)
    return inv_scale * (scaled - first_mean - unit_rows * second_mean)


def gelu_tanh(values):
    return jax.nn.gelu(values, approximate=True)


def adam_step(param_old, gradient, first_old, second_old, step_rate):
    first_new = beta_one * first_old + (1.0 - beta_one) * gradient
    second_new = beta_two * second_old + (1.0 - beta_two) * gradient * gradient
    first_hat = first_new / (1.0 - beta_one**STEP)
    second_hat = second_new / (1.0 - beta_two**STEP)
    updated = param_old - step_rate * (
        first_hat / (jnp.sqrt(second_hat) + eps_adam) + decay_rate * param_old
    )
    return (updated, first_new, second_new)


def xor_permute(value, axis, mask):
    count = lax.axis_size(axis)
    return lax.ppermute(value, axis, [(i, i ^ mask) for i in range(count)])


def head_sum(partial_low):
    count = lax.axis_size("head")
    if count & (count - 1):
        return lax.psum(partial_low.astype(f32), "head")
    total = partial_low
    step = 1
    while step < count:
        other = xor_permute(total.astype(bf16), "head", step)
        total = total.astype(f32) + other.astype(f32)
        step *= 2
    return total.astype(f32)


def total_sum(value):
    for axis in ("seq", "head"):
        count = lax.axis_size(axis)
        if count & (count - 1):
            value = lax.psum(value, axis)
            continue
        step = 1
        while step < count:
            value = value + xor_permute(value, axis, step)
            step *= 2
    return value


def attend_kernel(off_ref, q_ref, kv_ref, bias_ref, ctx_ref, prob_ref):
    lanes, rows = q_ref.shape[0], q_ref.shape[1]
    left = lax.broadcasted_iota(jnp.int32, (rows, 2 * DH), 1) < DH
    scale = DH**-0.5

    def step(i, carry):
        q_pair = q_ref[i].astype(f32) * scale
        outs = []
        for half in range(2):
            q_one = q_pair if half == 0 else pltpu.roll(q_pair, DH, 1)
            q_one = jnp.where(left, q_one, 0.0).astype(bf16)
            listed = jnp.concatenate(
                [
                    kv_ref[pl.ds(pl.multiple_of(off_ref[2 * i + half, j], BLOCK), BLOCK), :]
                    for j in range(LISTED)
                ],
                axis=0,
            )
            scores = dot(q_one, listed, 1, 1) + bias_ref[i, half : half + 1, :]
            row_max = jnp.max(scores, axis=1, keepdims=True)
            grown = jnp.exp(scores - row_max)
            total = jnp.sum(grown, axis=1, keepdims=True)
            probs = (grown * (1.0 / total)).astype(bf16)
            prob_ref[i, half] = probs
            outs.append(dot(probs, listed, 1, 0))
        ctx_ref[i] = jnp.where(left, pltpu.roll(outs[0], DH, 1), outs[1]).astype(bf16)
        return carry

    lax.fori_loop(0, lanes, step, 0)


def attend_back_kernel(off_ref, q_ref, kv_ref, prob_ref, dctx_ref, dq_ref, dkv_ref):
    lanes, rows = q_ref.shape[0], q_ref.shape[1]
    left = lax.broadcasted_iota(jnp.int32, (rows, 2 * DH), 1) < DH
    scale = DH**-0.5
    dkv_ref[...] = jnp.zeros_like(dkv_ref)

    def step(i, carry):
        q_pair = q_ref[i].astype(f32) * scale
        d_pair = dctx_ref[i].astype(f32)
        outs = []
        for half in range(2):
            q_one = q_pair if half == 0 else pltpu.roll(q_pair, DH, 1)
            q_one = jnp.where(left, q_one, 0.0).astype(bf16)
            d_one = pltpu.roll(d_pair, DH, 1) if half == 0 else d_pair
            d_one = jnp.where(left, 0.0, d_one).astype(bf16)
            offs = [
                pl.multiple_of(off_ref[2 * i + half, j], BLOCK) for j in range(LISTED)
            ]
            listed = jnp.concatenate([kv_ref[pl.ds(o, BLOCK), :] for o in offs], axis=0)
            probs_low = prob_ref[i, half]
            probs = probs_low.astype(f32)
            prob_grad = dot(d_one, listed, 1, 1)
            weighted = probs * prob_grad
            row_dot = jnp.sum(weighted, axis=1, keepdims=True)
            score_low = (weighted - probs * row_dot).astype(bf16)
            outs.append(dot(score_low, listed, 1, 0) * scale)
            both = jnp.concatenate([score_low, probs_low], axis=0)
            mates = jnp.concatenate([q_one, d_one], axis=0)
            kv_grad = dot(both, mates, 0, 0)
            for j in range(LISTED):
                at = pl.ds(offs[j], BLOCK)
                dkv_ref[at, :] += kv_grad[j * BLOCK : (j + 1) * BLOCK]
        dq_ref[i] = jnp.where(left, outs[0], pltpu.roll(outs[1], DH, 1)).astype(bf16)
        return carry

    lax.fori_loop(0, lanes, step, 0)


VMEM_LIMIT = 48 * 1024 * 1024


def in_vmem():
    return pl.BlockSpec(memory_space=pltpu.VMEM)


def in_smem():
    return pl.BlockSpec(memory_space=pltpu.SMEM)


def attend(offsets, q_pairs, kv_rows, bias):
    lanes, rows, width = q_pairs.shape
    return pl.pallas_call(
        attend_kernel,
        out_shape=(
            jax.ShapeDtypeStruct((lanes, rows, width), bf16),
            jax.ShapeDtypeStruct((lanes, 2, rows, LISTED * BLOCK), bf16),
        ),
        in_specs=[in_smem(), in_vmem(), in_vmem(), in_vmem()],
        out_specs=(in_vmem(), in_vmem()),
        compiler_params=pltpu.CompilerParams(vmem_limit_bytes=VMEM_LIMIT),
    )(offsets, q_pairs, kv_rows, bias)


def attend_back(offsets, q_pairs, kv_rows, probs, dctx_pairs):
    lanes, rows, width = q_pairs.shape
    return pl.pallas_call(
        attend_back_kernel,
        out_shape=(
            jax.ShapeDtypeStruct((lanes, rows, width), bf16),
            jax.ShapeDtypeStruct(kv_rows.shape, f32),
        ),
        in_specs=[in_smem(), in_vmem(), in_vmem(), in_vmem(), in_vmem()],
        out_specs=(in_vmem(), in_vmem()),
        compiler_params=pltpu.CompilerParams(vmem_limit_bytes=VMEM_LIMIT),
    )(offsets, q_pairs, kv_rows, probs, dctx_pairs)


def body(
    layer_input,
    output_grad,
    random_pick,
    doc_blocks,
    last_fill,
    shard_owner,
    qkv_weight,
    qkv_first,
    qkv_second,
    proj_weight,
    proj_first,
    proj_second,
    up_weight,
    up_first,
    up_second,
    down_weight,
    down_first,
    down_second,
    vec_params,
    vec_first,
    vec_second,
):
    lanes = lax.axis_size("seq")
    lane_index = lax.axis_index("seq")
    head_groups = lax.axis_size("head")
    head_index = lax.axis_index("head")
    slots = layer_input.shape[0]
    heads = random_pick.shape[2]
    feat = heads * DH
    units = up_weight.shape[1]
    rows = slots * BLOCK
    block_total = slots * lanes
    share = lanes // heads
    part_rows = rows // share
    pair_rows = part_rows // 2
    my_part = lane_index % share
    width = D // lanes

    picks = random_pick[:, 0].transpose(1, 0, 2).reshape(heads, slots * 3)
    picks = jnp.broadcast_to(picks[:, None], (heads, share, slots * 3)).reshape(lanes, slots * 3)
    picks = lax.all_to_all(picks, "seq", 0, 0, tiled=True).reshape(lanes, slots, 3)

    doc_end = jnp.cumsum(doc_blocks)
    doc_start = doc_end - doc_blocks
    doc_length = (doc_blocks - 1) * BLOCK + last_fill
    half_slot = (my_part * part_rows + jnp.arange(2, dtype=jnp.int32) * pair_rows) // BLOCK
    query_ids = half_slot[None, :] * lanes + jnp.arange(lanes, dtype=jnp.int32)[:, None]
    pick_half = jnp.sum(
        jnp.where(
            (half_slot[:, None] == jnp.arange(slots, dtype=jnp.int32)[None, :])[None, :, :, None],
            picks[:, None],
            0,
        ),
        axis=2,
    )
    query_doc = owning_doc(doc_end, query_ids)
    doc_first = lookup(doc_start, query_doc)
    doc_count = lookup(doc_blocks, query_doc)
    query_length = lookup(doc_length, query_doc)
    key_ids = jnp.concatenate(
        [
            jnp.stack(
                [
                    (query_ids - 1) % block_total,
                    query_ids,
                    (query_ids + 1) % block_total,
                    doc_first,
                    (doc_first + 1) % block_total,
                ],
                axis=-1,
            ),
            doc_first[..., None] + pick_half % doc_count[..., None],
        ],
        axis=-1,
    )
    same_doc = owning_doc(doc_end, key_ids) == query_doc[..., None]
    live_count = jnp.where(
        same_doc, query_length[..., None] - (key_ids - doc_first[..., None]) * BLOCK, 0
    )
    token = jnp.arange(BLOCK, dtype=jnp.int32)
    bias = jnp.where(token < live_count[..., None], 0.0, masked_score).astype(f32)
    bias = bias.reshape(lanes, 2, LISTED * BLOCK)
    key_lane = key_ids % lanes
    key_slot = key_ids // lanes
    if part_rows >= BLOCK:
        part_slots = part_rows // BLOCK
        offsets = ((key_slot // part_slots) * lanes + key_lane) * part_rows + (
            key_slot % part_slots
        ) * BLOCK
    else:
        offsets = (key_lane * slots + key_slot) * BLOCK
    offsets = offsets.reshape(lanes * 2, LISTED)

    qkv_mine = qkv_weight.astype(bf16).transpose(1, 0, 2).reshape(width, 3 * feat)
    rest_mine = jnp.concatenate(
        [proj_weight.astype(bf16).T, up_weight.astype(bf16), down_weight.astype(bf16).T], axis=1
    )
    qkv_full = lax.all_gather(qkv_mine, "seq", axis=0, tiled=True)
    rest_full = lax.all_gather(rest_mine, "seq", axis=0, tiled=True)
    proj_full = rest_full[:, :feat]
    up_full = rest_full[:, feat : feat + units]
    down_full = rest_full[:, feat + units :]

    column = jnp.arange(D, dtype=jnp.int32)
    stored_at = lookup(shard_owner, column // width) * width + column % width
    place = (stored_at[:, None] == column[None, :]).astype(bf16)
    token_rows = dot(layer_input.reshape(rows, D), place, 1, 0)
    grad_low = dot(output_grad.reshape(rows, D), place, 1, 0).astype(bf16)
    grad_rows = grad_low.astype(f32)
    vec_rows = lax.dot_general(
        vec_params[:5],
        place.astype(f32),
        (((1,), (0,)), ((), ())),
        precision=lax.Precision.HIGHEST,
    )
    up_bias = lax.dynamic_slice_in_dim(vec_params[5:].reshape(FF), head_index * units, units)

    normed_one, unit_one, scale_one = norm_rows(token_rows, vec_rows[0], vec_rows[1])
    low_one = normed_one.astype(bf16)
    qkv_rows = dot(low_one, qkv_full, 1, 0).astype(bf16)
    by_head = qkv_rows.reshape(rows, 3, heads, DH)
    kv_send = by_head[:, 1:].transpose(2, 0, 1, 3).reshape(lanes, part_rows, 2 * DH)
    q_send = (
        by_head[:, 0]
        .reshape(share, 2, pair_rows, heads, DH)
        .transpose(3, 0, 2, 1, 4)
        .reshape(lanes, pair_rows, 2 * DH)
    )
    received = lax.all_to_all(
        jnp.concatenate([kv_send, q_send], axis=1), "seq", 0, 0, tiled=True
    )
    q_pairs = received[:, part_rows:]
    kv_parts = received[:, :part_rows][None]
    step = 1
    while step < share:
        other = xor_permute(kv_parts, "seq", step)
        high = (my_part & step) != 0
        kv_parts = jnp.where(
            high,
            jnp.concatenate([other, kv_parts], axis=0),
            jnp.concatenate([kv_parts, other], axis=0),
        )
        step *= 2
    if part_rows >= BLOCK:
        kv_rows = kv_parts.reshape(block_total * BLOCK, 2 * DH)
    else:
        kv_rows = kv_parts.transpose(1, 0, 2, 3).reshape(block_total * BLOCK, 2 * DH)
    ctx_pairs, probs = attend(offsets, q_pairs, kv_rows, bias)

    def pairs_to_rows(pairs):
        return (
            pairs.reshape(heads, share, pair_rows, 2, DH)
            .transpose(1, 3, 2, 0, 4)
            .reshape(rows, feat)
        )

    def rows_to_pairs(low_rows):
        return (
            low_rows.reshape(share, 2, pair_rows, heads, DH)
            .transpose(3, 0, 2, 1, 4)
            .reshape(lanes, pair_rows, 2 * DH)
        )

    context = pairs_to_rows(lax.all_to_all(ctx_pairs, "seq", 0, 0, tiled=True))
    attn_sum = head_sum(dot(context, proj_full, 1, 1).astype(bf16))
    mid_rows = token_rows + attn_sum
    normed_two, unit_two, scale_two = norm_rows(mid_rows, vec_rows[2], vec_rows[3])
    low_two = normed_two.astype(bf16)
    hidden = dot(low_two, up_full, 1, 0) + up_bias
    active = gelu_tanh(hidden).astype(bf16)
    act_grad = dot(grad_low, down_full, 1, 0)
    hidden_grad = jax.vjp(gelu_tanh, hidden)[1](act_grad)[0]
    hidden_low = hidden_grad.astype(bf16)
    two_grad = head_sum(dot(hidden_low, up_full, 1, 1).astype(bf16))
    ffn_sum = head_sum(dot(active, down_full, 1, 1).astype(bf16))
    result = (mid_rows + ffn_sum + vec_rows[4]).astype(bf16)
    up_bias_grad = jnp.sum(hidden_grad, axis=0)
    ffn_grads = jnp.concatenate(
        [dot(low_two, hidden_low, 0, 0).astype(bf16), dot(grad_low, active, 0, 0).astype(bf16)],
        axis=1,
    )
    ffn_owned = lax.psum_scatter(ffn_grads, "seq", scatter_dimension=0, tiled=True).astype(f32)

    mid_grad = grad_rows + norm_back(two_grad, unit_two, scale_two, vec_rows[2])
    attn_low = mid_grad.astype(bf16)
    ctx_grad = dot(attn_low, proj_full, 1, 0).astype(bf16)
    dctx_pairs = lax.all_to_all(rows_to_pairs(ctx_grad), "seq", 0, 0, tiled=True)
    dq_pairs, dkv_rows = attend_back(offsets, q_pairs, kv_rows, probs, dctx_pairs)
    if part_rows >= BLOCK:
        dkv_parts = dkv_rows.reshape(share, lanes, part_rows, 2 * DH)
    else:
        dkv_parts = dkv_rows.reshape(lanes, share, part_rows, 2 * DH).transpose(1, 0, 2, 3)
    step = share // 2
    while step >= 1:
        high = (my_part & step) != 0
        first, second = dkv_parts[:step], dkv_parts[step:]
        away = jnp.where(high, first, second).astype(bf16)
        stay = jnp.where(high, second, first)
        dkv_parts = stay + xor_permute(away, "seq", step).astype(f32)
        step //= 2
    returned = lax.all_to_all(
        jnp.concatenate([dkv_parts[0].astype(bf16), dq_pairs], axis=1),
        "seq",
        0,
        0,
        tiled=True,
    )
    dkv_back = (
        returned[:, :part_rows]
        .reshape(heads, rows, 2, DH)
        .transpose(1, 2, 0, 3)
        .reshape(rows, 2 * feat)
    )
    dqkv = jnp.concatenate([pairs_to_rows(returned[:, part_rows:]), dkv_back], axis=1)
    one_grad = head_sum(dot(dqkv, qkv_full, 1, 1).astype(bf16))
    attn_grads = jnp.concatenate(
        [dot(low_one, dqkv, 0, 0).astype(bf16), dot(attn_low, context, 0, 0).astype(bf16)],
        axis=1,
    )
    attn_owned = lax.psum_scatter(attn_grads, "seq", scatter_dimension=0, tiled=True).astype(f32)
    input_grad = mid_grad + norm_back(one_grad, unit_one, scale_one, vec_rows[0])

    shared_rows = jnp.stack(
        [
            jnp.sum(one_grad * unit_one, axis=0),
            jnp.sum(one_grad, axis=0),
            jnp.sum(two_grad * unit_two, axis=0),
            jnp.sum(two_grad, axis=0),
            jnp.sum(grad_rows, axis=0),
        ]
    )
    column_group = column // (D // head_groups)
    shared_rows = jnp.where((column_group == head_index)[None, :], shared_rows, 0.0)
    bias_rows = lax.dynamic_update_slice_in_dim(
        jnp.zeros((FF,), f32), up_bias_grad, head_index * units, 0
    ).reshape(FF // D, D)
    vec_grad = total_sum(jnp.concatenate([shared_rows, bias_rows], axis=0))

    back = (((1,), (1,)), ((), ()))
    layer_output = lax.dot_general(result, place, back, preferred_element_type=f32).astype(bf16)
    exact = functools.partial(lax.dot_general, precision=lax.Precision.HIGHEST)
    input_grad = exact(input_grad, place.astype(f32), back)
    vec_grad = jnp.concatenate([exact(vec_grad[:5], place.astype(f32), back), vec_grad[5:]], axis=0)

    qkv_grad = attn_owned[:, : 3 * feat].reshape(width, 3, feat).transpose(1, 0, 2)
    proj_grad = attn_owned[:, 3 * feat :].T
    up_grad = ffn_owned[:, :units]
    down_grad = ffn_owned[:, units:].T
    qkv_new, qkv_first_new, qkv_second_new = adam_step(
        qkv_weight, qkv_grad, qkv_first, qkv_second, rate_qkv
    )
    proj_new, proj_first_new, proj_second_new = adam_step(
        proj_weight, proj_grad, proj_first, proj_second, rate_proj
    )
    up_new, up_first_new, up_second_new = adam_step(up_weight, up_grad, up_first, up_second, rate_up)
    down_new, down_first_new, down_second_new = adam_step(
        down_weight, down_grad, down_first, down_second, rate_down
    )
    vec_new, vec_first_new, vec_second_new = adam_step(
        vec_params, vec_grad, vec_first, vec_second, rate_vector
    )
    return (
        layer_output.reshape(slots, BLOCK, D),
        input_grad.reshape(slots, BLOCK, D),
        qkv_new,
        qkv_first_new,
        qkv_second_new,
        qkv_new.astype(bf16),
        proj_new,
        proj_first_new,
        proj_second_new,
        proj_new.astype(bf16),
        up_new,
        up_first_new,
        up_second_new,
        up_new.astype(bf16),
        down_new,
        down_first_new,
        down_second_new,
        down_new.astype(bf16),
        vec_new,
        vec_first_new,
        vec_second_new,
    )


def solution(mesh):
    rows_by_seq = P(None, "seq", None)
    cols = P("head", "seq")
    ups = P("seq", "head")
    qkvs = P(None, "seq", "head")
    placed = (
        (rows_by_seq, rows_by_seq, P(None, "seq", "head", None), P(), P(), P())
        + (qkvs,) * 3
        + (cols,) * 3
        + (ups,) * 3
        + (cols,) * 3
        + (P(),) * 3
    )
    return jax.shard_map(
        body,
        mesh=mesh,
        in_specs=placed,
        out_specs=(rows_by_seq, rows_by_seq)
        + (qkvs,) * 4
        + (cols,) * 4
        + (ups,) * 4
        + (cols,) * 4
        + (P(),) * 3,
        check_vma=False,
    )
```

time: 1290 us -> 469 us (0.36)
  waiting for transfers between devices: 799 us -> 256 us
  local copies, waits for them, and re-layouts: 177 us -> 20.9 us
  other arithmetic: 135 us -> 33.5 us
  matrix products: 101 us -> 42.6 us
  Pallas kernels: 0 us -> 29 us
  starting transfers between devices: 11.4 us -> 27.2 us
    reduce_scatter x5 -> x2, waiting for transfers between devices: 363 us -> 109 us  [the longest x1 104 us: body(): lax.psum_scatter(ffn_grads, 'seq', scatter_dimension=0, tiled=True)]
    all_gather x6 -> x2, waiting for transfers between devices: 271 us -> 48.1 us  [the longest x1 31.8 us: body(): qkv_full = lax.all_gather(qkv_mine, 'seq', axis=0, tiled=True)]
    psum x5 -> x0, waiting for transfers between devices: 130 us -> none  [the longest x2 56.7 us: head_total(): lax.psum(partial_rows.astype(jnp.bfloat16), 'head').astype(jnp.float32)]
    gather x12 -> x0, local copies, waits for them, and re-layouts: 63 us -> none  [the longest x10 49 us: reorder(): picked = jnp.take(shaped, index_table, axis=0)]
    dot_general x22 -> x18, matrix products: 101 us -> 42.6 us  [the longest x14 30.8 us: dot(): lax.dot_general(lhs, rhs, (((lhs_dim,), (rhs_dim,)), ((), ())), preferred...]
    all_to_all x0 -> x3, waiting for transfers between devices: none -> 47.5 us  [the longest x1 30.6 us: body(): lax.all_to_all(jnp.concatenate([kv_send, q_send], axis=1), 'seq', 0, 0, t...]
    psum x1 -> x0, blocking collectives: 39.8 us -> none  [body(): lax.psum(jnp.concatenate([shared_rows, bias_rows], axis=0), ('seq', 'head'))]
    all_to_all x0 -> x2, blocking collectives: none -> 37.2 us  [the longest x1 23.6 us: body(): context = pairs_to_rows(lax.all_to_all(ctx_pairs, 'seq', 0, 0, tiled=True))]
  transfers between devices with their start and end apart: 22 -> 18, of which waited for: 20 -> 15; matrix products, arithmetic and copies ran while one was open for 15% -> 14% of each run, Pallas kernels for 0% -> 3%
where the time goes in v1:
time: 469 us; the launch traced here: 462 us
  waiting for transfers between devices  256 us (55%)
  matrix products  42.6 us (9%)
  blocking collectives  37.2 us (8%)
  other arithmetic  33.5 us (7%)
  Pallas kernels  29 us (6%)
  starting transfers between devices  27.2 us (6%)
  local copies, waits for them, and re-layouts  20.9 us (4%)
  between operations  15.3 us (3%)
    reduce_scatter x1, waiting for transfers between devices, body(): lax.psum_scatter(ffn_grads, 'seq', scatter_dimension=0, tiled=True)  104 us
    ppermute x11, waiting for transfers between devices, xor_permute(): return lax.ppermute(value, axis, [(i, i ^ mask) for i in range(count)])  52.2 us
    all_gather x1, waiting for transfers between devices, body(): qkv_full = lax.all_gather(qkv_mine, 'seq', axis=0, tiled=True)  31.8 us
    dot_general x14, matrix products, dot(): lax.dot_general(lhs, rhs, (((lhs_dim,), (rhs_dim,)), ((), ())), preferred...  30.8 us
    all_to_all x1, waiting for transfers between devices, body(): lax.all_to_all(jnp.concatenate([kv_send, q_send], axis=1), 'seq', 0, 0, t...  30.6 us
    all_to_all x1, blocking collectives, body(): context = pairs_to_rows(lax.all_to_all(ctx_pairs, 'seq', 0, 0, tiled=True))  23.6 us
    all_to_all x1, waiting for transfers between devices, body(): lax.all_to_all(jnp.concatenate([dkv_parts[0].astype(bf16), dq_pairs], axi...  17 us
    all_gather x1, waiting for transfers between devices, body(): rest_full = lax.all_gather(rest_mine, 'seq', axis=0, tiled=True)  16.3 us
  transfers between devices with their start and end apart: 18, of which 15 were waited for; matrix products, arithmetic and copies ran while one was open for 14% of the time, Pallas kernels for 3%

profile of v1, /device:TPU:0, one launch (start us, length us, event | category | flops | bytes accessed | tf_op | source)
XLA Modules:
  0.0 462.2 jit_solution(7149659004359469204)
XLA Ops:
  7.3 1.1 convert_bitcast_fusion.2
  9.2 1.1 convert_element_type.154
  12.9 7.4 %all-to-all-start = ((s32[16,1,12]{2,1,0:T(1,128)}), s32[16,1,12]{2,1,0:T(1,128)S(1)}, u32[]{:S(2)}, u32[]{:S(2)}) async-start(s32[16,1,12]{2,1,0:T(1,128)} %bitcast.8), calls=%async_computation | async-start | bytes 16384 | tf_op jit(solution)/shard_map/all_to_all | solution.py:259
  22.1 1.0 fusion.127
  25.5 1.5 fusion.44
  27.0 31.8 %all-gather.3.cloned.1.call-done = bf16[1024,1536]{1,0:T(8,128)(2,1)} async-done(((bf16[64,1536]{1,0:T(8,128)(2,1)}), bf16[1024,1536]{1,0:T(8,128)(2,1)}) %all-gather.3.cloned.1.call-update) | async-done | bytes 3145744 | tf_op jit(solution)/shard_map/all_gather | solution.py:316
  58.8 3.0 convolution_convert_fusion.3
  62.4 2.0 copy.321
  67.0 3.6 all-to-all-start.1
  71.4 30.6 %all-to-all-done.1 = bf16[16,192,128]{2,1,0:T(8,128)(2,1)S(1)} async-done(((bf16[16,192,128]{2,1,0:T(8,128)(2,1)}), bf16[16,192,128]{2,1,0:T(8,128)(2,1)S(1)}, u32[]{:S(2)}, u32[]{:S(2)}) %all-to-all-start.1) | async-done | bytes 786464 | tf_op jit(solution)/shard_map/all_to_all | solution.py:347
  102.8 1.3 collective-permute-done
  104.2 1.4 maximum_select_fusion
  105.5 13.9 %shard_map.364 = (bf16[16,64,128]{2,1,0:T(8,128)(2,1)S(1)}, bf16[16,2,64,512]{3,2,1,0:T(8,128)(2,1)S(1)}) custom-call(s32[32,8]{1,0:T(8,128)S(1)} %fusion.85.off_ref, bf16[16,64,128]{2,1,0:T(8,128)(2,1)S(1)} %slice.104.q_ref, bf16[4096,128]{1,0:T(8,128)(2,1)S(1)} %bitcast.157, f32[16,2,512]{2,1,0:T(2,128)S(1)} %compare_select_fusion.bias_ref), custom_call_target="tpu_custom_call" | custom-call | tf_op jit(solution)/shard_map/pallas_call | solution.py:192
  119.4 1.3 copy-done.2
  120.7 23.6 %all_to_all.29 = bf16[16,64,128]{2,1,0:T(8,128)(2,1)S(1)} all-to-all(bf16[16,64,128]{2,1,0:T(8,128)(2,1)S(1)} %get-tuple-element.25), channel_id=1, replica_groups=mesh['seq'=16,'head'=2] {'seq'}, dimensions={0} | all-to-all | bytes 524288 | tf_op jit(solution)/shard_map/all_to_all | solution.py:382
  145.2 16.3 %all-gather.5.cloned.1.call-done = bf16[1024,4608]{1,0:T(8,128)(2,1)} async-done(((bf16[64,4608]{1,0:T(8,128)(2,1)}), bf16[1024,4608]{1,0:T(8,128)(2,1)}) %all-gather.5.cloned.1.call-update) | async-done | bytes 9437200 | tf_op jit(solution)/shard_map/all_gather | solution.py:317
  161.6 1.7 convolution_convert_fusion.5
  163.3 1.5 collective-permute-start.1
  164.8 1.1 convert_reduce_fusion
  165.9 11.6 %collective-permute-done.1 = bf16[256,1024]{0,1:T(8,128)(2,1)} collective-permute-done((bf16[256,1024]{0,1:T(8,128)(2,1)S(1)}, bf16[256,1024]{0,1:T(8,128)(2,1)}, u32[]{:S(2)}, u32[]{:S(2)}) %collective-permute-start.1) | collective-permute-done | bytes 524320 | tf_op jit(solution)/shard_map/ppermute | solution.py:81
  177.5 1.3 fusion.125
  179.0 1.4 fusion.17
  180.4 2.6 fusion.128
  183.1 1.3 fusion.38
  184.4 1.5 collective-permute-start.3
  185.9 11.8 %collective-permute-done.3 = bf16[256,1024]{0,1:T(8,128)(2,1)S(1)} collective-permute-done((bf16[256,1024]{0,1:T(8,128)(2,1)S(1)}, bf16[256,1024]{0,1:T(8,128)(2,1)S(1)}, u32[]{:S(2)}, u32[]{:S(2)}) %collective-permute-start.3) | collective-permute-done | bytes 524320 | tf_op jit(solution)/shard_map/ppermute | solution.py:81
  198.9 1.0 copy-done.7
  201.4 13.6 %all_to_all.30.dctx_ref = bf16[16,64,128]{2,1,0:T(8,128)(2,1)S(1)} all-to-all(bf16[16,64,128]{2,1,0:T(8,128)(2,1)S(1)} %reshape.744), channel_id=1, replica_groups=mesh['seq'=16,'head'=2] {'seq'}, dimensions={0} | all-to-all | bytes 524288 | tf_op jit(solution)/shard_map/all_to_all | solution.py:405
  215.0 1.6 copy-done.3
  216.6 15.1 %shard_map.365 = (bf16[16,64,128]{2,1,0:T(8,128)(2,1)S(1)}, f32[4096,128]{1,0:T(8,128)S(1)}) custom-call(s32[32,8]{1,0:T(8,128)S(1)} %fusion.85.off_ref, bf16[16,64,128]{2,1,0:T(8,128)(2,1)S(1)} %slice.104.q_ref, bf16[4096,128]{1,0:T(8,128)(2,1)S(1)} %bitcast.158, bf16[16,2,64,512]{3,2,1,0:T(8,128)(2,1)S(1)} %copy-done.3, ...), custom_call_target="tpu_custom_call" | custom-call | tf_op jit(solution)/shard_map/pallas_call | solution.py:206
  232.0 1.8 collective-permute-done.4
  234.9 3.6 all-to-all-start.4
  238.9 1.4 convolution_convert_fusion.4
  240.3 17.0 %all-to-all-done.4 = bf16[16,192,128]{2,1,0:T(8,128)(2,1)S(1)} async-done(((bf16[16,192,128]{2,1,0:T(8,128)(2,1)}), bf16[16,192,128]{2,1,0:T(8,128)(2,1)S(1)}, u32[]{:S(2)}, u32[]{:S(2)}) %all-to-all-start.4) | async-done | bytes 786464 | tf_op jit(solution)/shard_map/all_to_all | solution.py:419
  258.7 1.2 reshape.745
  259.9 1.1 copy.364
  261.1 1.4 reshape.746
  262.6 1.0 convolution_convert_fusion
  263.8 2.6 pad_maximum_fusion.1
  266.6 4.7 %convolution_convert_fusion.2 = bf16[1024,2048]{1,0:T(8,128)(2,1)} fusion(bf16[256,2048]{1,0:T(8,128)(2,1)} %copy-done.15, f32[256,1024]{0,1:T(8,128)S(1)} %get-tuple-element.165, f32[1024]{0:T(1024)S(1)} %bitcast.177, f32[1024]{0:T(1024)S(1)} %bitcast.175, f32[256]{0:T(256)S(1)} %add_rsqrt_fusion, f32[256]{0:T(256)S(1)} %broadcast_multiply_fusion.4), kind=kOutput, calls=%fused_computation.10 | convolution fusion | flops 1077149696 | bytes 6301696 | tf_op jit(solution)/shard_map/dot_general | solution.py:43
  271.3 3.5 convolution_convert_fusion.1
  274.8 8.3 %pad_maximum_fusion = bf16[1024,4096]{1,0:T(8,128)(2,1)} fusion(bf16[1024,2048]{1,0:T(8,128)(2,1)} %convolution_convert_fusion.1, bf16[1024,2048]{1,0:T(8,128)(2,1)} %convolution_convert_fusion.2), kind=kLoop, calls=%fused_computation | loop fusion | flops 16777216 | bytes 16777216 | tf_op jit(solution)/shard_map/concatenate | solution.py:396
  283.2 3.2 convolution_convert_fusion.6
  286.3 1.5 collective-permute-start.5
  287.8 4.4 fusion.41
  293.5 7.7 %collective-permute-done.5 = bf16[256,1024]{0,1:T(8,128)(2,1)S(1)} collective-permute-done((bf16[256,1024]{0,1:T(8,128)(2,1)S(1)}, bf16[256,1024]{0,1:T(8,128)(2,1)S(1)}, u32[]{:S(2)}, u32[]{:S(2)}) %collective-permute-start.5) | collective-permute-done | bytes 524320 | tf_op jit(solution)/shard_map/ppermute | solution.py:81
  302.0 1.2 collective-permute-done.6
  303.2 1.2 collective-permute-start.7
  304.5 7.3 %collective-permute-done.2 = bf16[256,1024]{0,1:T(8,128)(2,1)} collective-permute-done((bf16[256,1024]{0,1:T(8,128)(2,1)}, bf16[256,1024]{0,1:T(8,128)(2,1)}, u32[]{:S(2)}, u32[]{:S(2)}) %collective-permute-start.2) | collective-permute-done | bytes 524320 | tf_op jit(solution)/shard_map/ppermute | solution.py:81
  311.8 3.3 fusion.37
  315.1 2.8 collective-permute-start.8
  317.9 4.8 %collective-permute-done.8 = f32[9,1024]{1,0:T(8,128)S(1)} collective-permute-done((f32[9,1024]{1,0:T(8,128)S(1)}, f32[9,1024]{1,0:T(8,128)S(1)}, u32[]{:S(2)}, u32[]{:S(2)}) %collective-permute-start.8) | collective-permute-done | bytes 36896 | tf_op jit(solution)/shard_map/ppermute | solution.py:81
  322.7 1.4 collective-permute-start.9
  324.1 4.5 collective-permute-done.9
  328.7 1.4 collective-permute-start.10
  330.1 5.1 %fusion = f32[256,1024]{1,0:T(8,128)} fusion(s32[1024]{0:T(1024)S(1)} %fusion.102, f32[256,1024]{0,1:T(8,128)S(1)} %copy-done.9, bf16[256,1024]{0,1:T(8,128)(2,1)S(1)} %collective-permute-done.5, bf16[256,1024]{0,1:T(8,128)(2,1)S(1)} %convolution_convert_fusion.6, f32[1024,256]{1,0:T(8,128)S(1)} %copy-done.6, f32[256]{0:T(256)S(1)} %broadcast_multiply_fusion, ...), kind=kOutput, calls=%fused_computation.3 | convolution fusion | flops 3225157632 | bytes 4206592 | tf_op jit(solution)/shard_map/dot_general | solution.py:460
  335.3 2.0 fusion.1
  338.0 4.6 reduce-scatter.3.cloned.1.call-done
  343.6 1.0 convert_element_type.185
  345.5 1.3 fusion.122
  346.7 104.0 %reduce-scatter.5.cloned.1.call-done = bf16[64,4096]{1,0:T(8,128)(2,1)} async-done(((bf16[1024,4096]{1,0:T(8,128)(2,1)}), bf16[64,4096]{1,0:T(8,128)(2,1)}) %reduce-scatter.5.cloned.1.call-update) | async-done | bytes 524304 | tf_op jit(solution)/shard_map/reduce_scatter | solution.py:400
  450.7 1.1 convert_element_type.190
  451.9 1.5 fusion.118
  453.7 1.5 fusion.116
  (219 shorter events, 24.5 us)
Async XLA Ops:
  7.2 157.6 %copy-start = (bf16[4,64,1024]{2,1,0:T(8,128)(2,1)S(1)}, bf16[4,64,1024]{2,1,0:T(8,128)(2,1)}, u32[]{:S(2)}) copy-start(bf16[4,64,1024]{2,1,0:T(8,128)(2,1)} %param.22) | copy-start | bytes 1572868
  7.2 4.0 copy-start.12
  7.2 51.6 %all-gather.3.cloned.1.call-start = ((), (), s32[]{:S(2)}) async-start(), calls=%async_computation.7 | async-start | bytes 3342336 | tf_op jit(solution)/shard_map/all_gather | solution.py:316
  8.4 3.8 copy-start.33
  8.4 11.9 %copy-start.35 = (s32[8]{0:T(128)S(1)}, s32[8]{0:T(128)}, u32[]{:S(2)}) copy-start(s32[8]{0:T(128)} %param.24) | copy-start | bytes 100
  8.4 12.3 %copy-start.37 = (s32[8]{0:T(128)S(1)}, s32[8]{0:T(128)}, u32[]{:S(2)}) copy-start(s32[8]{0:T(128)} %param.25) | copy-start | bytes 100
  8.4 13.6 %copy-start.38 = (s32[16]{0:T(128)S(1)}, s32[16]{0:T(128)}, u32[]{:S(2)}) copy-start(s32[16]{0:T(128)} %param.26) | copy-start | bytes 196
  9.1 13.0 %copy-start.42 = (bf16[4,64,1024]{2,1,0:T(8,128)(2,1)S(1)}, bf16[4,64,1024]{2,1,0:T(8,128)(2,1)}, u32[]{:S(2)}) copy-start(bf16[4,64,1024]{2,1,0:T(8,128)(2,1)} %param.21) | copy-start | bytes 1572868
  9.1 152.4 %all-gather.5.cloned.1.call-start = ((), (), s32[]{:S(2)}) async-start(), calls=%async_computation.8 | async-start | bytes 10027008 | tf_op jit(solution)/shard_map/all_gather | solution.py:317
  12.9 54.1 %all-to-all-start = ((s32[16,1,12]{2,1,0:T(1,128)}), s32[16,1,12]{2,1,0:T(1,128)S(1)}, u32[]{:S(2)}, u32[]{:S(2)}) async-start(s32[16,1,12]{2,1,0:T(1,128)} %bitcast.8), calls=%async_computation | async-start | bytes 16384 | tf_op jit(solution)/shard_map/all_to_all | solution.py:259
  22.1 3.4 copy-start.30
  23.1 38.7 %copy-start.4 = (f32[1024,256]{1,0:T(8,128)}, f32[1024,256]{1,0:T(8,128)S(1)}, u32[]{:S(2)}) copy-start(f32[1024,256]{1,0:T(8,128)S(1)} %get-tuple-element.179) | copy-start | bytes 3145732
  66.0 36.1 %copy-start.36 = (s32[32]{0:T(128)S(1)}, s32[32]{0:T(128)}, u32[]{:S(2)}) copy-start(s32[32]{0:T(128)} %add.497) | copy-start | bytes 388
  66.0 36.1 %copy-start.40 = (s32[32]{0:T(128)S(1)}, s32[32]{0:T(128)}, u32[]{:S(2)}) copy-start(s32[32]{0:T(128)} %compare_select_fusion.8) | copy-start | bytes 388
  66.0 36.1 %copy-start.41 = (pred[32]{0:T(512)(128)(4,1)S(1)}, pred[32]{0:T(512)(128)(4,1)}, u32[]{:S(2)}) copy-start(pred[32]{0:T(512)(128)(4,1)} %broadcast_compare_fusion.1) | copy-start | bytes 100
  66.0 36.3 %copy-start.34 = (s32[32,1]{0,1:T(1,128)S(1)}, s32[32,1]{0,1:T(1,128)}, u32[]{:S(2)}) copy-start(s32[32,1]{0,1:T(1,128)} %get-tuple-element.184) | copy-start | bytes 388
  66.0 36.3 %copy-start.39 = (s32[32,1]{0,1:T(1,128)S(1)}, s32[32,1]{0,1:T(1,128)}, u32[]{:S(2)}) copy-start(s32[32,1]{0,1:T(1,128)} %and_select_fusion.5) | copy-start | bytes 388
  67.0 35.0 %all-to-all-start.1 = ((bf16[16,192,128]{2,1,0:T(8,128)(2,1)}), bf16[16,192,128]{2,1,0:T(8,128)(2,1)S(1)}, u32[]{:S(2)}, u32[]{:S(2)}) async-start(bf16[16,192,128]{2,1,0:T(8,128)(2,1)} %pad_maximum_fusion.2), calls=%async_computation.1 | async-start | bytes 1572864 | tf_op jit(solution)/shard_map/all_to_all | solution.py:347
  102.0 2.1 collective-permute-start
  119.4 1.3 copy-start.2
  145.2 20.7 %copy-start.16 = (bf16[256,512]{1,0:T(8,128)(2,1)}, bf16[256,512]{1,0:T(8,128)(2,1)S(1)}, u32[]{:S(2)}) copy-start(bf16[256,512]{1,0:T(8,128)(2,1)S(1)} %reshape.739) | copy-start | bytes 786436
  163.3 14.3 %collective-permute-start.1 = (bf16[256,1024]{0,1:T(8,128)(2,1)S(1)}, bf16[256,1024]{0,1:T(8,128)(2,1)}, u32[]{:S(2)}, u32[]{:S(2)}) collective-permute-start(bf16[256,1024]{0,1:T(8,128)(2,1)S(1)} %convolution_convert_fusion.5), channel_id=1, source_target_pairs={{0,1},{1,0},{2,3},{3,2},{4,5},{5,4},{6,7},{7,6},{8,9},{9,8},{10,11... | collective-permute-start | bytes 1572872 | tf_op jit(solution)/shard_map/ppermute | solution.py:81
  164.8 12.7 %copy-start.5 = (f32[1024,256]{1,0:T(8,128)S(1)}, f32[1024,256]{1,0:T(8,128)}, u32[]{:S(2)}) copy-start(f32[1024,256]{1,0:T(8,128)} %copy-done.4) | copy-start | bytes 3145732
  164.8 14.1 %copy-start.29 = (bf16[1024,4608]{1,0:T(8,128)(2,1)S(1)}, bf16[1024,4608]{1,0:T(8,128)(2,1)}, u32[]{:S(2)}) copy-start(bf16[1024,4608]{1,0:T(8,128)(2,1)} %all-gather.5.cloned.1.call-done) | copy-start | bytes 28311556
  165.9 32.5 %copy-start.22 = (bf16[1024,256]{1,0:T(8,128)(2,1)}, bf16[1024,256]{1,0:T(8,128)(2,1)S(1)}, u32[]{:S(2)}) copy-start(bf16[1024,256]{1,0:T(8,128)(2,1)S(1)} %get-tuple-element.183) | copy-start | bytes 1572868
  180.4 2.6 copy-start.43
  183.1 1.3 copy-start.15
  184.4 13.3 %collective-permute-start.3 = (bf16[256,1024]{0,1:T(8,128)(2,1)S(1)}, bf16[256,1024]{0,1:T(8,128)(2,1)S(1)}, u32[]{:S(2)}, u32[]{:S(2)}) collective-permute-start(bf16[256,1024]{0,1:T(8,128)(2,1)S(1)} %fusion.38), channel_id=1, source_target_pairs={{0,1},{1,0},{2,3},{3,2},{4,5},{5,4},{6,7},{7,6},{8,9},{9,8},{10,11... | collective-permute-start | bytes 1572872 | tf_op jit(solution)/shard_map/ppermute | solution.py:81
  198.9 1.0 copy-start.7
  215.0 1.6 copy-start.3
  231.8 2.0 collective-permute-start.4
  234.0 4.9 %copy-start.8 = (f32[256,1024]{0,1:T(8,128)S(1)}, f32[256,1024]{0,1:T(8,128)}, u32[]{:S(2)}) copy-start(f32[256,1024]{0,1:T(8,128)} %copy-done.7) | copy-start | bytes 3145732
  234.0 4.9 %copy-start.17 = (bf16[256,512]{1,0:T(8,128)(2,1)S(1)}, bf16[256,512]{1,0:T(8,128)(2,1)}, u32[]{:S(2)}) copy-start(bf16[256,512]{1,0:T(8,128)(2,1)} %copy-done.16) | copy-start | bytes 786436
  234.9 22.3 %all-to-all-start.4 = ((bf16[16,192,128]{2,1,0:T(8,128)(2,1)}), bf16[16,192,128]{2,1,0:T(8,128)(2,1)S(1)}, u32[]{:S(2)}, u32[]{:S(2)}) async-start(bf16[16,192,128]{2,1,0:T(8,128)(2,1)} %pad_maximum_fusion.3), calls=%async_computation.4 | async-start | bytes 1572864 | tf_op jit(solution)/shard_map/all_to_all | solution.py:419
  238.6 104.0 %reduce-scatter.3.cloned.1.call-start = ((), (), s32[]{:S(2)}) async-start(), calls=%async_computation.9 | async-start | bytes 4456448 | tf_op jit(solution)/shard_map/reduce_scatter | solution.py:438
  258.0 4.6 copy-start.6
  262.6 1.2 copy-start.10
  266.5 4.8 %copy-start.23 = (bf16[1024,256]{1,0:T(8,128)(2,1)S(1)}, bf16[1024,256]{1,0:T(8,128)(2,1)}, u32[]{:S(2)}) copy-start(bf16[1024,256]{1,0:T(8,128)(2,1)} %copy-done.22) | copy-start | bytes 1572868
  266.5 184.2 %reduce-scatter.5.cloned.1.call-start = ((), (), s32[]{:S(2)}) async-start(), calls=%async_computation.10 | async-start | bytes 8912896 | tf_op jit(solution)/shard_map/reduce_scatter | solution.py:400
  266.6 4.7 %copy-start.44 = (f32[256,2048]{1,0:T(8,128)S(1)}, f32[256,2048]{1,0:T(8,128)}, u32[]{:S(2)}) copy-start(f32[256,2048]{1,0:T(8,128)} %copy-done.43) | copy-start | bytes 6291460
  283.2 4.6 %copy-start.45 = (f32[256,2048]{1,0:T(8,128)S(1)}, f32[256,2048]{1,0:T(8,128)}, u32[]{:S(2)}) copy-start(f32[256,2048]{1,0:T(8,128)} %copy-done.43) | copy-start | bytes 6291460
  286.3 14.8 %collective-permute-start.5 = (bf16[256,1024]{0,1:T(8,128)(2,1)S(1)}, bf16[256,1024]{0,1:T(8,128)(2,1)S(1)}, u32[]{:S(2)}, u32[]{:S(2)}) collective-permute-start(bf16[256,1024]{0,1:T(8,128)(2,1)S(1)} %convolution_convert_fusion.6), channel_id=1, source_target_pairs={{0,1},{1,0},{2,3},{3,2},{4,5},{5,4},{6,7},{7,6},{8,9},{9,8},{10,11... | collective-permute-start | bytes 1572872 | tf_op jit(solution)/shard_map/ppermute | solution.py:81
  292.2 19.6 %collective-permute-start.2 = (bf16[256,1024]{0,1:T(8,128)(2,1)}, bf16[256,1024]{0,1:T(8,128)(2,1)}, u32[]{:S(2)}, u32[]{:S(2)}) collective-permute-start(bf16[256,1024]{0,1:T(8,128)(2,1)} %fusion.41), channel_id=1, source_target_pairs={{0,1},{1,0},{2,3},{3,2},{4,5},{5,4},{6,7},{7,6},{8,9},{9,8},{10,11... | collective-permute-start | bytes 1572872 | tf_op jit(solution)/shard_map/ppermute | solution.py:81
  301.9 1.3 collective-permute-start.6
  303.2 11.8 %collective-permute-start.7 = (f32[9,1024]{1,0:T(8,128)S(1)}, f32[9,1024]{1,0:T(8,128)S(1)}, u32[]{:S(2)}, u32[]{:S(2)}) collective-permute-start(f32[9,1024]{1,0:T(8,128)S(1)} %fusion.114), channel_id=1, source_target_pairs={{0,4},{2,6},{4,0},{6,2},{8,12},{10,14},{12,8},{14,10},{16,20},{18,... | collective-permute-start | bytes 110600 | tf_op jit(solution)/shard_map/ppermute | solution.py:81
  311.8 18.3 %copy-start.9 = (f32[256,1024]{0,1:T(8,128)S(1)}, f32[256,1024]{0,1:T(8,128)}, u32[]{:S(2)}) copy-start(f32[256,1024]{0,1:T(8,128)} %copy-done.7) | copy-start | bytes 3145732
  315.1 7.6 %collective-permute-start.8 = (f32[9,1024]{1,0:T(8,128)S(1)}, f32[9,1024]{1,0:T(8,128)S(1)}, u32[]{:S(2)}, u32[]{:S(2)}) collective-permute-start(f32[9,1024]{1,0:T(8,128)S(1)} %add.563), channel_id=1, source_target_pairs={{0,8},{2,10},{4,12},{6,14},{8,0},{10,2},{12,4},{14,6},{16,24},{18,... | collective-permute-start | bytes 110600 | tf_op jit(solution)/shard_map/ppermute | solution.py:81
  322.7 5.9 %collective-permute-start.9 = (f32[9,1024]{1,0:T(8,128)S(1)}, f32[9,1024]{1,0:T(8,128)S(1)}, u32[]{:S(2)}, u32[]{:S(2)}) collective-permute-start(f32[9,1024]{1,0:T(8,128)S(1)} %add.564), channel_id=1, source_target_pairs={{0,16},{2,18},{4,20},{6,22},{8,24},{10,26},{12,28},{14,30},{16,0},... | collective-permute-start | bytes 110600 | tf_op jit(solution)/shard_map/ppermute | solution.py:81
  328.7 8.6 %copy-start.31 = (f32[9,1024]{1,0:T(8,128)S(1)}, f32[9,1024]{1,0:T(8,128)}, u32[]{:S(2)}) copy-start(f32[9,1024]{1,0:T(8,128)} %param.40) | copy-start | bytes 110596
  328.7 8.6 %copy-start.32 = (f32[9,1024]{1,0:T(8,128)S(1)}, f32[9,1024]{1,0:T(8,128)}, u32[]{:S(2)}) copy-start(f32[9,1024]{1,0:T(8,128)} %param.41) | copy-start | bytes 110596
  328.7 6.5 %collective-permute-start.10 = (f32[9,1024]{1,0:T(8,128)S(1)}, f32[9,1024]{1,0:T(8,128)S(1)}, u32[]{:S(2)}, u32[]{:S(2)}) collective-permute-start(f32[9,1024]{1,0:T(8,128)S(1)} %add.565), channel_id=1, source_target_pairs={{0,1},{1,0},{2,3},{3,2},{4,5},{5,4},{6,7},{7,6},{8,9},{9,8},{10,11... | collective-permute-start | bytes 110600 | tf_op jit(solution)/shard_map/ppermute | solution.py:81
  335.2 9.4 %copy-start.24 = (f32[512,64]{0,1:T(8,128)S(1)}, f32[512,64]{0,1:T(8,128)}, u32[]{:S(2)}) copy-start(f32[512,64]{0,1:T(8,128)} %param.30) | copy-start | bytes 393220
  335.2 9.4 %copy-start.27 = (f32[512,64]{0,1:T(8,128)S(1)}, f32[512,64]{0,1:T(8,128)}, u32[]{:S(2)}) copy-start(f32[512,64]{0,1:T(8,128)} %param.31) | copy-start | bytes 393220
  335.2 9.4 %copy-start.28 = (f32[512,64]{0,1:T(8,128)S(1)}, f32[512,64]{0,1:T(8,128)}, u32[]{:S(2)}) copy-start(f32[512,64]{0,1:T(8,128)} %param.32) | copy-start | bytes 393220
  335.2 10.2 %copy-start.14 = (f32[3,64,512]{2,1,0:T(8,128)S(1)}, f32[3,64,512]{2,1,0:T(8,128)}, u32[]{:S(2)}) copy-start(f32[3,64,512]{2,1,0:T(8,128)} %param.27) | copy-start | bytes 1179652
  335.2 10.2 %copy-start.25 = (f32[3,64,512]{2,1,0:T(8,128)S(1)}, f32[3,64,512]{2,1,0:T(8,128)}, u32[]{:S(2)}) copy-start(f32[3,64,512]{2,1,0:T(8,128)} %param.28) | copy-start | bytes 1179652
  335.2 10.2 %copy-start.26 = (f32[3,64,512]{2,1,0:T(8,128)S(1)}, f32[3,64,512]{2,1,0:T(8,128)}, u32[]{:S(2)}) copy-start(f32[3,64,512]{2,1,0:T(8,128)} %param.29) | copy-start | bytes 1179652
  345.4 106.4 %copy-start.11 = (f32[64,2048]{1,0:T(8,128)S(1)}, f32[64,2048]{1,0:T(8,128)}, u32[]{:S(2)}) copy-start(f32[64,2048]{1,0:T(8,128)} %param.33) | copy-start | bytes 1572868
  345.4 106.4 %copy-start.18 = (f32[64,2048]{1,0:T(8,128)S(1)}, f32[64,2048]{1,0:T(8,128)}, u32[]{:S(2)}) copy-start(f32[64,2048]{1,0:T(8,128)} %param.34) | copy-start | bytes 1572868
  345.4 106.4 %copy-start.19 = (f32[64,2048]{1,0:T(8,128)S(1)}, f32[64,2048]{1,0:T(8,128)}, u32[]{:S(2)}) copy-start(f32[64,2048]{1,0:T(8,128)} %param.35) | copy-start | bytes 1572868
  451.8 1.6 copy-start.13
  451.8 1.5 copy-start.20
  451.9 1.9 copy-start.21
  451.9 3.4 copy-start.1
Sparse Core Ops, SparseCore 0:
  10.9 47.8 all-gather.2
  61.1 100.4 all-gather.4
  266.6 75.9 reduce-scatter.2
  347.1 103.5 reduce-scatter.4

commit v2 on v1

--- a/solution.py
+++ b/solution.py
@@ -94,17 +94,46 @@
     return total.astype(f32)
 
 
-def total_sum(value):
-    for axis in ("seq", "head"):
-        count = lax.axis_size(axis)
-        if count & (count - 1):
-            value = lax.psum(value, axis)
-            continue
-        step = 1
-        while step < count:
-            value = value + xor_permute(value, axis, step)
-            step *= 2
+def seq_sum(value):
+    step = 1
+    while step < lax.axis_size("seq"):
+        value = value + xor_permute(value, "seq", step)
+        step *= 2
     return value
+
+
+def lane_cuts(lanes):
+    chips = lanes // 2
+    ys = 1 << ((chips.bit_length() - 1) // 2)
+    return 2, ys, chips // ys
+
+
+def relative_lanes(lanes):
+    cores, ys, zs = lane_cuts(lanes)
+    return [(kz * ys + ky) * cores + kc for kc in range(cores) for ky in range(ys) for kz in range(zs)]
+
+
+def relative_gather(mine):
+    cores, ys, zs = lane_cuts(lax.axis_size("seq"))
+    column = [mine] + [xor_permute(mine, "seq", kz * ys * cores) for kz in range(1, zs)]
+    pieces = list(column)
+    for ky in range(1, ys):
+        pieces += [xor_permute(piece, "seq", ky * cores) for piece in column]
+    near = jnp.concatenate(pieces, axis=0)
+    return near, xor_permute(near, "seq", 1)
+
+
+def relative_scatter(near, far):
+    cores, ys, zs = lane_cuts(lax.axis_size("seq"))
+    total = near + xor_permute(far, "seq", 1).astype(f32)
+    for shift, count in ((cores, ys), (ys * cores, zs)):
+        size = total.shape[0] // count
+        kept = total[:size]
+        sent = total[size:].astype(bf16)
+        for k in range(1, count):
+            kept = kept + xor_permute(sent[(k - 1) * size : k * size], "seq", k * shift).astype(f32)
+        total = kept
+    return total
 
 
 def attend_kernel(off_ref, q_ref, kv_ref, bias_ref, ctx_ref, prob_ref):
@@ -310,32 +339,47 @@
     offsets = offsets.reshape(lanes * 2, LISTED)
 
     qkv_mine = qkv_weight.astype(bf16).transpose(1, 0, 2).reshape(width, 3 * feat)
+    qkv_near, qkv_far = relative_gather(qkv_mine)
     rest_mine = jnp.concatenate(
         [proj_weight.astype(bf16).T, up_weight.astype(bf16), down_weight.astype(bf16).T], axis=1
     )
-    qkv_full = lax.all_gather(qkv_mine, "seq", axis=0, tiled=True)
+    rest_mine, picks = lax.optimization_barrier((rest_mine, picks))
     rest_full = lax.all_gather(rest_mine, "seq", axis=0, tiled=True)
     proj_full = rest_full[:, :feat]
     up_full = rest_full[:, feat : feat + units]
     down_full = rest_full[:, feat + units :]
 
     column = jnp.arange(D, dtype=jnp.int32)
-    stored_at = lookup(shard_owner, column // width) * width + column % width
-    place = (stored_at[:, None] == column[None, :]).astype(bf16)
-    token_rows = dot(layer_input.reshape(rows, D), place, 1, 0)
+    owner = lookup(shard_owner, column // width)
+    masks = jnp.array(relative_lanes(lanes), jnp.int32)
+    position = jnp.sum(
+        jnp.where(
+            masks[None, :] == (owner ^ lane_index)[:, None], jnp.arange(lanes, dtype=jnp.int32), 0
+        ),
+        axis=1,
+    )
+    place = (owner * width + column % width)[:, None] == column[None, :]
+    place_near = (position * width + column % width)[:, None] == column[None, :]
+    place, place_near = place.astype(bf16), place_near.astype(bf16)
+    rows_in = layer_input.reshape(rows, D)
+    token_rows = dot(rows_in, place, 1, 0)
     grad_low = dot(output_grad.reshape(rows, D), place, 1, 0).astype(bf16)
     grad_rows = grad_low.astype(f32)
-    vec_rows = lax.dot_general(
-        vec_params[:5],
-        place.astype(f32),
-        (((1,), (0,)), ((), ())),
-        precision=lax.Precision.HIGHEST,
-    )
+    exact = functools.partial(
+        lax.dot_general, precision=lax.Precision.HIGHEST, preferred_element_type=f32
+    )
+    ahead = (((1,), (0,)), ((), ()))
+    back = (((1,), (1,)), ((), ()))
+    vec_rows = exact(vec_params[:5], place.astype(f32), ahead)
+    vec_near = exact(vec_params[:2], place_near.astype(f32), ahead)
     up_bias = lax.dynamic_slice_in_dim(vec_params[5:].reshape(FF), head_index * units, units)
 
-    normed_one, unit_one, scale_one = norm_rows(token_rows, vec_rows[0], vec_rows[1])
+    normed_one, unit_one, scale_one = norm_rows(
+        dot(rows_in, place_near, 1, 0), vec_near[0], vec_near[1]
+    )
     low_one = normed_one.astype(bf16)
-    qkv_rows = dot(low_one, qkv_full, 1, 0).astype(bf16)
+    half = D // 2
+    qkv_rows = (dot(low_one[:, :half], qkv_near, 1, 0) + dot(low_one[:, half:], qkv_far, 1, 0)).astype(bf16)
     by_head = qkv_rows.reshape(rows, 3, heads, DH)
     kv_send = by_head[:, 1:].transpose(2, 0, 1, 3).reshape(lanes, part_rows, 2 * DH)
     q_send = (
@@ -397,11 +441,16 @@
         [dot(low_two, hidden_low, 0, 0).astype(bf16), dot(grad_low, active, 0, 0).astype(bf16)],
         axis=1,
     )
-    ffn_owned = lax.psum_scatter(ffn_grads, "seq", scatter_dimension=0, tiled=True).astype(f32)
 
     mid_grad = grad_rows + norm_back(two_grad, unit_two, scale_two, vec_rows[2])
     attn_low = mid_grad.astype(bf16)
     ctx_grad = dot(attn_low, proj_full, 1, 0).astype(bf16)
+    ffn_grads, ctx_grad = lax.optimization_barrier((ffn_grads, ctx_grad))
+    ffn_owned = lax.psum_scatter(ffn_grads, "seq", scatter_dimension=0, tiled=True).astype(f32)
+    attn_near = dot(attn_low, dot(place, place_near, 0, 0).astype(bf16), 1, 0).astype(bf16)
+    proj_owned = relative_scatter(
+        dot(attn_near[:, :half], context, 0, 0), dot(attn_near[:, half:], context, 0, 0).astype(bf16)
+    )
     dctx_pairs = lax.all_to_all(rows_to_pairs(ctx_grad), "seq", 0, 0, tiled=True)
     dq_pairs, dkv_rows = attend_back(offsets, q_pairs, kv_rows, probs, dctx_pairs)
     if part_rows >= BLOCK:
@@ -430,38 +479,40 @@
         .reshape(rows, 2 * feat)
     )
     dqkv = jnp.concatenate([pairs_to_rows(returned[:, part_rows:]), dkv_back], axis=1)
-    one_grad = head_sum(dot(dqkv, qkv_full, 1, 1).astype(bf16))
-    attn_grads = jnp.concatenate(
-        [dot(low_one, dqkv, 0, 0).astype(bf16), dot(attn_low, context, 0, 0).astype(bf16)],
-        axis=1,
-    )
-    attn_owned = lax.psum_scatter(attn_grads, "seq", scatter_dimension=0, tiled=True).astype(f32)
-    input_grad = mid_grad + norm_back(one_grad, unit_one, scale_one, vec_rows[0])
-
-    shared_rows = jnp.stack(
-        [
-            jnp.sum(one_grad * unit_one, axis=0),
-            jnp.sum(one_grad, axis=0),
-            jnp.sum(two_grad * unit_two, axis=0),
-            jnp.sum(two_grad, axis=0),
-            jnp.sum(grad_rows, axis=0),
-        ]
-    )
-    column_group = column // (D // head_groups)
-    shared_rows = jnp.where((column_group == head_index)[None, :], shared_rows, 0.0)
-    bias_rows = lax.dynamic_update_slice_in_dim(
-        jnp.zeros((FF,), f32), up_bias_grad, head_index * units, 0
-    ).reshape(FF // D, D)
-    vec_grad = total_sum(jnp.concatenate([shared_rows, bias_rows], axis=0))
-
-    back = (((1,), (1,)), ((), ()))
+    one_part = jnp.concatenate([dot(dqkv, qkv_near, 1, 1), dot(dqkv, qkv_far, 1, 1)], axis=1)
+    one_grad = head_sum(one_part.astype(bf16))
+    qkv_owned = []
+    for cols in (dqkv[:, : 3 * feat // 2], dqkv[:, 3 * feat // 2 :]):
+        far = dot(low_one[:, half:], cols, 0, 0).astype(bf16)
+        qkv_owned.append(relative_scatter(dot(low_one[:, :half], cols, 0, 0), far))
+    qkv_owned = jnp.concatenate(qkv_owned, axis=1)
+
     layer_output = lax.dot_general(result, place, back, preferred_element_type=f32).astype(bf16)
-    exact = functools.partial(lax.dot_general, precision=lax.Precision.HIGHEST)
-    input_grad = exact(input_grad, place.astype(f32), back)
-    vec_grad = jnp.concatenate([exact(vec_grad[:5], place.astype(f32), back), vec_grad[5:]], axis=0)
-
-    qkv_grad = attn_owned[:, : 3 * feat].reshape(width, 3, feat).transpose(1, 0, 2)
-    proj_grad = attn_owned[:, 3 * feat :].T
+    input_grad = exact(mid_grad, place.astype(f32), back) + exact(
+        norm_back(one_grad, unit_one, scale_one, vec_near[0]), place_near.astype(f32), back
+    )
+    early_rows = jnp.stack(
+        [jnp.sum(two_grad * unit_two, axis=0), jnp.sum(two_grad, axis=0), jnp.sum(grad_rows, axis=0)]
+    )
+    early_rows = exact(early_rows, place.astype(f32), back)
+    early_rows = seq_sum(jnp.concatenate([early_rows, up_bias_grad.reshape(units // D, D)], axis=0))
+    late_rows = jnp.stack([jnp.sum(one_grad * unit_one, axis=0), jnp.sum(one_grad, axis=0)])
+    late_rows = seq_sum(exact(late_rows, place_near.astype(f32), back))
+    bias_rows = early_rows[3:]
+    step = 1
+    while step < head_groups:
+        other = xor_permute(bias_rows, "head", step)
+        high = (head_index & step) != 0
+        bias_rows = jnp.where(
+            high,
+            jnp.concatenate([other, bias_rows], axis=0),
+            jnp.concatenate([bias_rows, other], axis=0),
+        )
+        step *= 2
+    vec_grad = jnp.concatenate([late_rows, early_rows[:3], bias_rows], axis=0)
+
+    qkv_grad = qkv_owned.reshape(width, 3, feat).transpose(1, 0, 2)
+    proj_grad = proj_owned.T
     up_grad = ffn_owned[:, :units]
     down_grad = ffn_owned[:, units:].T
     qkv_new, qkv_first_new, qkv_second_new = adam_step(

time: 469 us -> 394 us (0.84)
  waiting for transfers between devices: 256 us -> 142 us
  starting transfers between devices: 27.2 us -> 74.7 us
  blocking collectives: 37.2 us -> 0 us
  matrix products: 42.6 us -> 63.4 us
  local copies, waits for them, and re-layouts: 20.9 us -> 26.2 us
    reduce_scatter x1, waiting for transfers between devices: 104 us -> 0.01 us  [body(): lax.psum_scatter(ffn_grads, 'seq', scatter_dimension=0, tiled=True)]
    ppermute x11 -> x38, waiting for transfers between devices: 52.2 us -> 101 us  [xor_permute(): return lax.ppermute(value, axis, [(i, i ^ mask) for i in range(count)])]
    all_to_all x2 -> x0, blocking collectives: 37.2 us -> none  [the longest x1 23.6 us: body(): context = pairs_to_rows(lax.all_to_all(ctx_pairs, 'seq', 0, 0, tiled=True))]
    ppermute x11 -> x38, starting transfers between devices: 12.2 us -> 48 us  [xor_permute(): return lax.ppermute(value, axis, [(i, i ^ mask) for i in range(count)])]
    all_gather x1 -> x0, waiting for transfers between devices: 31.8 us -> none  [body(): qkv_full = lax.all_gather(qkv_mine, 'seq', axis=0, tiled=True)]
    all_to_all x1, waiting for transfers between devices: 17 us -> 0.01 us  [body(): lax.all_to_all(jnp.concatenate([dkv_parts[0].astype(bf16), dq_pairs], axi...]
    all_gather x1, waiting for transfers between devices: 16.3 us -> 0.02 us  [body(): rest_full = lax.all_gather(rest_mine, 'seq', axis=0, tiled=True)]
    all_to_all x0 -> x2, starting transfers between devices: none -> 13.7 us  [the longest x1 9.88 us: body(): context = pairs_to_rows(lax.all_to_all(ctx_pairs, 'seq', 0, 0, tiled=True))]
  transfers between devices with their start and end apart: 18 -> 45, of which waited for: 15 -> 21; matrix products, arithmetic and copies ran while one was open for 14% -> 23% of each run, Pallas kernels for 3% -> 8%
where the time goes in v2:
time: 394 us; the launch traced here: 386 us
  waiting for transfers between devices  142 us (36%)
  starting transfers between devices  74.7 us (19%)
  matrix products  63.4 us (16%)
  other arithmetic  33.7 us (9%)
  Pallas kernels  29.7 us (8%)
  local copies, waits for them, and re-layouts  26.2 us (7%)
  between operations  15.8 us (4%)
    ppermute x38, waiting for transfers between devices, xor_permute(): return lax.ppermute(value, axis, [(i, i ^ mask) for i in range(count)])  101 us
    ppermute x38, starting transfers between devices, xor_permute(): return lax.ppermute(value, axis, [(i, i ^ mask) for i in range(count)])  48 us
    dot_general x22, matrix products, dot(): lax.dot_general(lhs, rhs, (((lhs_dim,), (rhs_dim,)), ((), ())), preferred...  43.5 us
    all_to_all x1, waiting for transfers between devices, body(): lax.all_to_all(jnp.concatenate([kv_send, q_send], axis=1), 'seq', 0, 0, t...  29.5 us
    pallas_call x1, Pallas kernels, attend_back(): pl.pallas_call(attend_back_kernel, out_shape=(jax.ShapeDtypeStruct((lanes...  15.1 us
    pallas_call x1, Pallas kernels, attend(): pl.pallas_call(attend_kernel, out_shape=(jax.ShapeDtypeStruct((lanes, row...  14.6 us
    all_to_all x1, starting transfers between devices, body(): context = pairs_to_rows(lax.all_to_all(ctx_pairs, 'seq', 0, 0, tiled=True))  9.88 us
    unnamed x104, local copies, waits for them, and re-layouts  9.66 us
  transfers between devices with their start and end apart: 45, of which 21 were waited for; matrix products, arithmetic and copies ran while one was open for 23% of the time, Pallas kernels for 8%

profile of v2, /device:TPU:0, one launch (start us, length us, event | category | flops | bytes accessed | tf_op | source)
XLA Modules:
  0.0 385.8 jit_solution(10628542848622722422)
XLA Ops:
  11.5 3.0 collective-permute-start.3
  14.5 3.6 collective-permute-start.2
  19.6 5.0 %all-to-all-start = ((s32[16,1,12]{2,1,0:T(1,128)}), s32[16,1,12]{2,1,0:T(1,128)S(1)}, u32[]{:S(2)}, u32[]{:S(2)}) async-start(s32[16,1,12]{2,1,0:T(1,128)} %bitcast.8), calls=%async_computation | async-start | bytes 16384 | tf_op jit(solution)/shard_map/all_to_all | solution.py:288
  28.2 1.9 collective-permute-start.6
  30.1 22.1 %collective-permute-done.1 = bf16[64,1536]{1,0:T(8,128)(2,1)S(1)} collective-permute-done((bf16[64,1536]{1,0:T(8,128)(2,1)S(1)}, bf16[64,1536]{1,0:T(8,128)(2,1)S(1)}, u32[]{:S(2)}, u32[]{:S(2)}) %collective-permute-start.1) | collective-permute-done | bytes 196640 | tf_op jit(solution)/shard_map/ppermute | solution.py:81
  52.4 1.9 collective-permute-start.4
  57.0 3.0 collective-permute-done.4
  66.3 2.0 fusion.116
  68.3 2.0 fusion.25
  70.9 2.0 copy.322
  75.5 3.7 all-to-all-start.1
  80.0 29.5 %all-to-all-done.1 = bf16[16,192,128]{2,1,0:T(8,128)(2,1)S(1)} async-done(((bf16[16,192,128]{2,1,0:T(8,128)(2,1)}), bf16[16,192,128]{2,1,0:T(8,128)(2,1)S(1)}, u32[]{:S(2)}, u32[]{:S(2)}) %all-to-all-start.1) | async-done | bytes 786464 | tf_op jit(solution)/shard_map/all_to_all | solution.py:391
  111.9 1.7 maximum_select_fusion
  113.6 14.6 %shard_map.373 = (bf16[16,64,128]{2,1,0:T(8,128)(2,1)}, bf16[16,2,64,512]{3,2,1,0:T(8,128)(2,1)S(1)}) custom-call(s32[32,8]{1,0:T(8,128)S(1)} %fusion.137.off_ref, bf16[16,64,128]{2,1,0:T(8,128)(2,1)S(1)} %slice.220.q_ref, bf16[4096,128]{1,0:T(8,128)(2,1)S(1)} %bitcast.166, f32[16,2,512]{2,1,0:T(2,128)S(1)} %compare_select_fusion.bias_ref), custom_call_target="tpu_custom_call" | custom-call | tf_op jit(solution)/shard_map/pallas_call | solution.py:221
  129.5 9.9 %all-to-all-start.2 = ((bf16[16,64,128]{2,1,0:T(8,128)(2,1)}), bf16[16,64,128]{2,1,0:T(8,128)(2,1)S(1)}, u32[]{:S(2)}, u32[]{:S(2)}) async-start(bf16[16,64,128]{2,1,0:T(8,128)(2,1)} %get-tuple-element.27), calls=%async_computation.2 | async-start | bytes 524288 | tf_op jit(solution)/shard_map/all_to_all | solution.py:426
  139.9 2.1 fusion.67
  142.0 7.5 %all-to-all-done.2 = bf16[16,64,128]{2,1,0:T(8,128)(2,1)S(1)} async-done(((bf16[16,64,128]{2,1,0:T(8,128)(2,1)}), bf16[16,64,128]{2,1,0:T(8,128)(2,1)S(1)}, u32[]{:S(2)}, u32[]{:S(2)}) %all-to-all-start.2) | async-done | bytes 262176 | tf_op jit(solution)/shard_map/all_to_all | solution.py:426
  150.4 2.6 convolution_convert_fusion.4
  153.0 1.7 collective-permute-start.9
  156.7 10.3 %collective-permute-done.9 = bf16[256,1024]{0,1:T(8,128)(2,1)} collective-permute-done((bf16[256,1024]{0,1:T(8,128)(2,1)}, bf16[256,1024]{0,1:T(8,128)(2,1)}, u32[]{:S(2)}, u32[]{:S(2)}) %collective-permute-start.9) | collective-permute-done | bytes 524320 | tf_op jit(solution)/shard_map/ppermute | solution.py:81
  167.0 2.2 fusion.191
  170.9 3.4 convolution_convert_fusion
  174.3 2.8 fusion.198
  177.0 3.3 convolution_convert_fusion.1
  181.7 1.7 collective-permute-start.11
  183.4 7.9 %pad_maximum_fusion = bf16[1024,4096]{1,0:T(8,128)(2,1)} fusion(bf16[1024,2048]{1,0:T(8,128)(2,1)} %convolution_convert_fusion, bf16[1024,2048]{1,0:T(8,128)(2,1)} %convolution_convert_fusion.1), kind=kLoop, calls=%fused_computation | loop fusion | flops 16777216 | bytes 16777216 | tf_op jit(solution)/shard_map/concatenate | solution.py:440
  191.3 3.4 collective-permute-done.11
  194.6 1.7 multiply_reduce_fusion
  198.8 2.4 convolution_convert_fusion.8
  201.3 2.0 fusion.6
  206.6 2.0 reshape.741
  208.6 3.8 all-to-all-start.3
  212.4 5.5 %fusion.54 = bf16[256,1024]{1,0:T(8,128)(2,1)} fusion(s32[1024]{0:T(1024)S(1)} %fusion.161, s32[1024]{0:T(1024)S(1)} %get-tuple-element.193, f32[256,1024]{0,1:T(8,128)} %copy-done.6), kind=kOutput, calls=%fused_computation.60 | convolution fusion | flops 2688024576 | bytes 1581056 | tf_op jit(solution)/shard_map/dot_general | solution.py:43
  217.9 4.5 %all-to-all-done.3.dctx_ref = bf16[16,64,128]{2,1,0:T(8,128)(2,1)S(1)} async-done(((bf16[16,64,128]{2,1,0:T(8,128)(2,1)}), bf16[16,64,128]{2,1,0:T(8,128)(2,1)S(1)}, u32[]{:S(2)}, u32[]{:S(2)}) %all-to-all-start.3) | async-done | bytes 262176 | tf_op jit(solution)/shard_map/all_to_all | solution.py:454
  222.4 1.7 copy-done.3
  224.1 15.1 %shard_map.374 = (bf16[16,64,128]{2,1,0:T(8,128)(2,1)S(1)}, f32[4096,128]{1,0:T(8,128)S(1)}) custom-call(s32[32,8]{1,0:T(8,128)S(1)} %fusion.137.off_ref, bf16[16,64,128]{2,1,0:T(8,128)(2,1)S(1)} %slice.220.q_ref, bf16[4096,128]{1,0:T(8,128)(2,1)S(1)} %bitcast.167, bf16[16,2,64,512]{3,2,1,0:T(8,128)(2,1)S(1)} %copy-done.3, ...), custom_call_target="tpu_custom_call" | custom-call | tf_op jit(solution)/shard_map/pallas_call | solution.py:235
  242.4 3.8 all-to-all-start.4
  246.2 5.1 %fusion.64 = bf16[256,1024]{0,1:T(8,128)(2,1)} fusion(bf16[1024,4608]{1,0:T(8,128)(2,1)} %all-gather.2.cloned.1.call-done, f32[256,2048]{1,0:T(8,128)} %copy-done.46), kind=kOutput, calls=%fused_computation.66 | convolution fusion | flops 1078722560 | bytes 6815744 | tf_op jit(solution)/shard_map/dot_general | solution.py:43
  251.3 1.7 collective-permute-start.10
  253.8 1.9 collective-permute-start.34
  255.7 2.1 collective-permute-done.34
  257.8 1.8 collective-permute-start.35
  259.6 14.2 %collective-permute-done.35 = f32[5,1024]{1,0:T(8,128)S(1)} collective-permute-done((f32[5,1024]{1,0:T(8,128)S(1)}, f32[5,1024]{1,0:T(8,128)S(1)}, u32[]{:S(2)}, u32[]{:S(2)}) %collective-permute-start.35) | collective-permute-done | bytes 20512 | tf_op jit(solution)/shard_map/ppermute | solution.py:81
  273.9 4.7 %collective-permute-start.36 = (f32[5,1024]{1,0:T(8,128)S(1)}, f32[5,1024]{1,0:T(8,128)S(1)}, u32[]{:S(2)}, u32[]{:S(2)}) collective-permute-start(f32[5,1024]{1,0:T(8,128)S(1)} %add.648), channel_id=1, source_target_pairs={{0,16},{2,18},{4,20},{6,22},{8,24},{10,26},{12,28},{14,30},{16,0},... | collective-permute-start | bytes 61448 | tf_op jit(solution)/shard_map/ppermute | solution.py:81
  278.6 8.6 %collective-permute-done.36 = f32[5,1024]{1,0:T(8,128)S(1)} collective-permute-done((f32[5,1024]{1,0:T(8,128)S(1)}, f32[5,1024]{1,0:T(8,128)S(1)}, u32[]{:S(2)}, u32[]{:S(2)}) %collective-permute-start.36) | collective-permute-done | bytes 20512 | tf_op jit(solution)/shard_map/ppermute | solution.py:81
  287.2 1.7 collective-permute-start.37
  291.8 3.2 fusion.60
  295.0 3.6 collective-permute-done.25
  299.4 2.4 collective-permute-start.28
  304.7 2.0 convolution_convert_fusion.7
  306.8 2.0 convolution_convert_fusion.6
  311.5 1.8 fusion.183
  314.8 6.6 %collective-permute-done.13 = bf16[256,1024]{0,1:T(8,128)(2,1)S(1)} collective-permute-done((bf16[256,1024]{0,1:T(8,128)(2,1)S(1)}, bf16[256,1024]{0,1:T(8,128)(2,1)S(1)}, u32[]{:S(2)}, u32[]{:S(2)}) %collective-permute-start.13) | collective-permute-done | bytes 524320 | tf_op jit(solution)/shard_map/ppermute | solution.py:81
  322.1 2.0 fusion
  326.3 2.6 collective-permute-done.30
  330.2 4.3 %fusion.2 = f32[256,1024]{1,0:T(8,128)S(1)} fusion(s32[1024]{0:T(1024)S(1)} %fusion.161, bf16[256,1024]{0,1:T(8,128)(2,1)S(1)} %collective-permute-done.13, f32[1024,256]{1,0:T(8,128)S(1)} %copy-done.5, f32[256]{0:T(256)S(1)} %broadcast_multiply_fusion, f32[256]{0:T(256)S(1)} %broadcast_multiply_fusion.1, f32[256]{0:T(256)S(1)} %add_rsqrt_fusion.1, ...), kind=kOutput, calls=%fused_computation.4 | convolution fusion | flops 3225681920 | bytes 3158016 | tf_op jit(solution)/shard_map/dot_general | solution.py:491
  334.5 2.4 collective-permute-start.32
  336.9 4.8 %fusion.53 = f32[256,1024]{1,0:T(8,128)} fusion(f32[256,1024]{1,0:T(8,128)S(1)} %fusion.2, f32[256,1024]{0,1:T(8,128)S(1)} %copy-done.7, s32[1024]{0:T(1024)S(1)} %get-tuple-element.193), kind=kOutput, calls=%fused_computation.57 | convolution fusion | flops 3222536192 | bytes 3149824 | tf_op jit(solution)/shard_map/dot_general | solution.py:491
  343.8 1.8 collective-permute-start.15
  345.6 8.8 %collective-permute-done.20 = bf16[256,768]{1,0:T(8,128)(2,1)S(1)} collective-permute-done((bf16[256,768]{1,0:T(8,128)(2,1)S(1)}, bf16[256,768]{1,0:T(8,128)(2,1)S(1)}, u32[]{:S(2)}, u32[]{:S(2)}) %collective-permute-start.20) | collective-permute-done | bytes 393248 | tf_op jit(solution)/shard_map/ppermute | solution.py:81
  358.0 2.2 collective-permute-done.15
  363.9 5.2 %collective-permute-done.22 = bf16[64,768]{1,0:T(8,128)(2,1)S(1)} collective-permute-done((bf16[64,768]{1,0:T(8,128)(2,1)S(1)}, bf16[64,768]{1,0:T(8,128)(2,1)S(1)}, u32[]{:S(2)}, u32[]{:S(2)}) %collective-permute-start.22) | collective-permute-done | bytes 98336 | tf_op jit(solution)/shard_map/ppermute | solution.py:81
  369.1 3.4 collective-permute-done.17
  375.1 1.5 fusion.179
  (304 shorter events, 70.3 us)
Async XLA Ops:
  7.2 18.8 %copy-start = (bf16[4,64,1024]{2,1,0:T(8,128)(2,1)S(1)}, bf16[4,64,1024]{2,1,0:T(8,128)(2,1)}, u32[]{:S(2)}) copy-start(bf16[4,64,1024]{2,1,0:T(8,128)(2,1)} %param.22) | copy-start | bytes 1572868
  7.2 143.2 %all-gather.2.cloned.1.call-start = ((), (), s32[]{:S(2)}) async-start(), calls=%async_computation.6 | async-start | bytes 10027008 | tf_op jit(solution)/shard_map/all_gather | solution.py:347
  8.3 16.3 %copy-start.35 = (s32[8]{0:T(128)S(1)}, s32[8]{0:T(128)}, u32[]{:S(2)}) copy-start(s32[8]{0:T(128)} %param.25) | copy-start | bytes 100
  8.3 16.7 %copy-start.39 = (s32[8]{0:T(128)S(1)}, s32[8]{0:T(128)}, u32[]{:S(2)}) copy-start(s32[8]{0:T(128)} %param.26) | copy-start | bytes 100
  8.3 16.9 %copy-start.40 = (s32[16]{0:T(128)S(1)}, s32[16]{0:T(128)}, u32[]{:S(2)}) copy-start(s32[16]{0:T(128)} %param.27) | copy-start | bytes 196
  8.3 17.0 %copy-start.41 = (s32[16]{0:T(128)S(1)}, s32[16]{0:T(128)}, u32[]{:S(2)}) copy-start(s32[16]{0:T(128)} %constant.238.clone) | copy-start | bytes 196
  11.5 44.9 %collective-permute-start.3 = (bf16[64,1536]{1,0:T(8,128)(2,1)S(1)}, bf16[64,1536]{1,0:T(8,128)(2,1)S(1)}, u32[]{:S(2)}, u32[]{:S(2)}) collective-permute-start(bf16[64,1536]{1,0:T(8,128)(2,1)S(1)} %bitcast.183), channel_id=1, source_target_pairs={{0,4},{2,6},{4,0},{6,2},{8,12},{10,14},{12,8},{14,10},{16,20},{18,... | collective-permute-start | bytes 589832 | tf_op jit(solution)/shard_map/ppermute | solution.py:81
  14.5 13.7 %collective-permute-start.2 = (bf16[64,1536]{1,0:T(8,128)(2,1)S(1)}, bf16[64,1536]{1,0:T(8,128)(2,1)S(1)}, u32[]{:S(2)}, u32[]{:S(2)}) collective-permute-start(bf16[64,1536]{1,0:T(8,128)(2,1)S(1)} %bitcast.184), channel_id=1, source_target_pairs={{0,24},{2,26},{4,28},{6,30},{8,16},{10,18},{12,20},{14,22},{16,8},... | collective-permute-start | bytes 589832 | tf_op jit(solution)/shard_map/ppermute | solution.py:81
  18.1 34.1 %collective-permute-start.1 = (bf16[64,1536]{1,0:T(8,128)(2,1)S(1)}, bf16[64,1536]{1,0:T(8,128)(2,1)S(1)}, u32[]{:S(2)}, u32[]{:S(2)}) collective-permute-start(bf16[64,1536]{1,0:T(8,128)(2,1)S(1)} %bitcast.185), channel_id=1, source_target_pairs={{0,16},{2,18},{4,20},{6,22},{8,24},{10,26},{12,28},{14,30},{16,0},... | collective-permute-start | bytes 589832 | tf_op jit(solution)/shard_map/ppermute | solution.py:81
  18.1 34.3 %collective-permute-start = (bf16[64,1536]{1,0:T(8,128)(2,1)S(1)}, bf16[64,1536]{1,0:T(8,128)(2,1)S(1)}, u32[]{:S(2)}, u32[]{:S(2)}) collective-permute-start(bf16[64,1536]{1,0:T(8,128)(2,1)S(1)} %bitcast.186), channel_id=1, source_target_pairs={{0,8},{2,10},{4,12},{6,14},{8,0},{10,2},{12,4},{14,6},{16,24},{18,... | collective-permute-start | bytes 589832 | tf_op jit(solution)/shard_map/ppermute | solution.py:81
  19.6 55.9 %all-to-all-start = ((s32[16,1,12]{2,1,0:T(1,128)}), s32[16,1,12]{2,1,0:T(1,128)S(1)}, u32[]{:S(2)}, u32[]{:S(2)}) async-start(s32[16,1,12]{2,1,0:T(1,128)} %bitcast.8), calls=%async_computation | async-start | bytes 16384 | tf_op jit(solution)/shard_map/all_to_all | solution.py:288
  24.8 38.2 %copy-start.36 = (s32[2]{0:T(128)}, s32[2]{0:T(128)S(1)}, u32[]{:S(2)}) copy-start(s32[2]{0:T(128)S(1)} %broadcast_multiply_fusion.6) | copy-start | bytes 28
  27.0 39.0 %copy-start.4 = (f32[1024,256]{1,0:T(8,128)}, f32[1024,256]{1,0:T(8,128)S(1)}, u32[]{:S(2)}) copy-start(f32[1024,256]{1,0:T(8,128)S(1)} %get-tuple-element.200) | copy-start | bytes 3145732
  27.0 37.5 %copy-start.29 = (f32[9,1024]{1,0:T(8,128)S(1)}, f32[9,1024]{1,0:T(8,128)}, u32[]{:S(2)}) copy-start(f32[9,1024]{1,0:T(8,128)} %param.40) | copy-start | bytes 110596
  28.2 33.2 %collective-permute-start.6 = (bf16[64,1536]{1,0:T(8,128)(2,1)S(1)}, bf16[64,1536]{1,0:T(8,128)(2,1)S(1)}, u32[]{:S(2)}, u32[]{:S(2)}) collective-permute-start(bf16[64,1536]{1,0:T(8,128)(2,1)S(1)} %collective-permute-done.2), channel_id=1, source_target_pairs={{0,4},{2,6},{4,0},{6,2},{8,12},{10,14},{12,8},{14,10},{16,20},{18,... | collective-permute-start | bytes 589832 | tf_op jit(solution)/shard_map/ppermute | solution.py:81
  52.2 8.5 %collective-permute-start.5 = (bf16[64,1536]{1,0:T(8,128)(2,1)S(1)}, bf16[64,1536]{1,0:T(8,128)(2,1)S(1)}, u32[]{:S(2)}, u32[]{:S(2)}) collective-permute-start(bf16[64,1536]{1,0:T(8,128)(2,1)S(1)} %collective-permute-done.1), channel_id=1, source_target_pairs={{0,4},{2,6},{4,0},{6,2},{8,12},{10,14},{12,8},{14,10},{16,20},{18,... | collective-permute-start | bytes 589832 | tf_op jit(solution)/shard_map/ppermute | solution.py:81
  52.4 7.6 %collective-permute-start.4 = (bf16[64,1536]{1,0:T(8,128)(2,1)S(1)}, bf16[64,1536]{1,0:T(8,128)(2,1)S(1)}, u32[]{:S(2)}, u32[]{:S(2)}) collective-permute-start(bf16[64,1536]{1,0:T(8,128)(2,1)S(1)} %collective-permute-done), channel_id=1, source_target_pairs={{0,4},{2,6},{4,0},{6,2},{8,12},{10,14},{12,8},{14,10},{16,20},{18,... | collective-permute-start | bytes 589832 | tf_op jit(solution)/shard_map/ppermute | solution.py:81
  62.1 4.2 %collective-permute-start.7 = (bf16[512,1536]{1,0:T(8,128)(2,1)}, bf16[512,1536]{1,0:T(8,128)(2,1)}, u32[]{:S(2)}, u32[]{:S(2)}) collective-permute-start(bf16[512,1536]{1,0:T(8,128)(2,1)} %constant_dynamic-update-slice_fusion), channel_id=1, source_target_pairs={{0,2},{2,0},{4,6},{6,4},{8,10},{10,8},{12,14},{14,12},{16,18},{18,... | collective-permute-start | bytes 4718600 | tf_op jit(solution)/shard_map/ppermute | solution.py:81
  74.5 35.4 %copy-start.38 = (s32[32]{0:T(128)S(1)}, s32[32]{0:T(128)}, u32[]{:S(2)}) copy-start(s32[32]{0:T(128)} %add.560) | copy-start | bytes 388
  74.5 35.4 %copy-start.42 = (pred[32]{0:T(512)(128)(4,1)S(1)}, pred[32]{0:T(512)(128)(4,1)}, u32[]{:S(2)}) copy-start(pred[32]{0:T(512)(128)(4,1)} %broadcast_compare_fusion.1) | copy-start | bytes 100
  74.5 35.4 %copy-start.43 = (s32[32]{0:T(128)S(1)}, s32[32]{0:T(128)}, u32[]{:S(2)}) copy-start(s32[32]{0:T(128)} %compare_select_fusion.8) | copy-start | bytes 388
  74.5 35.6 %copy-start.34 = (s32[32,1]{0,1:T(1,128)S(1)}, s32[32,1]{0,1:T(1,128)}, u32[]{:S(2)}) copy-start(s32[32,1]{0,1:T(1,128)} %get-tuple-element.205) | copy-start | bytes 388
  75.5 34.0 %all-to-all-start.1 = ((bf16[16,192,128]{2,1,0:T(8,128)(2,1)}), bf16[16,192,128]{2,1,0:T(8,128)(2,1)S(1)}, u32[]{:S(2)}, u32[]{:S(2)}) async-start(bf16[16,192,128]{2,1,0:T(8,128)(2,1)} %pad_maximum_fusion.1), calls=%async_computation.1 | async-start | bytes 1572864 | tf_op jit(solution)/shard_map/all_to_all | solution.py:391
  109.5 2.3 collective-permute-start.8
  129.5 19.9 %all-to-all-start.2 = ((bf16[16,64,128]{2,1,0:T(8,128)(2,1)}), bf16[16,64,128]{2,1,0:T(8,128)(2,1)S(1)}, u32[]{:S(2)}, u32[]{:S(2)}) async-start(bf16[16,64,128]{2,1,0:T(8,128)(2,1)} %get-tuple-element.27), calls=%async_computation.2 | async-start | bytes 524288 | tf_op jit(solution)/shard_map/all_to_all | solution.py:426
  139.4 234.6 %reduce-scatter.2.cloned.1.call-start = ((), (), s32[]{:S(2)}) async-start(), calls=%async_computation.7 | async-start | bytes 8912896 | tf_op jit(solution)/shard_map/reduce_scatter | solution.py:449
  153.0 14.0 %collective-permute-start.9 = (bf16[256,1024]{0,1:T(8,128)(2,1)}, bf16[256,1024]{0,1:T(8,128)(2,1)}, u32[]{:S(2)}, u32[]{:S(2)}) collective-permute-start(bf16[256,1024]{0,1:T(8,128)(2,1)} %convolution_convert_fusion.4), channel_id=1, source_target_pairs={{0,1},{1,0},{2,3},{3,2},{4,5},{5,4},{6,7},{7,6},{8,9},{9,8},{10,11... | collective-permute-start | bytes 1572872 | tf_op jit(solution)/shard_map/ppermute | solution.py:81
  156.7 17.5 %copy-start.20 = (bf16[1024,256]{1,0:T(8,128)(2,1)}, bf16[1024,256]{1,0:T(8,128)(2,1)S(1)}, u32[]{:S(2)}) copy-start(bf16[1024,256]{1,0:T(8,128)(2,1)S(1)} %get-tuple-element.204) | copy-start | bytes 1572868
  181.7 13.0 %collective-permute-start.11 = (bf16[256,1024]{0,1:T(8,128)(2,1)S(1)}, bf16[256,1024]{0,1:T(8,128)(2,1)}, u32[]{:S(2)}, u32[]{:S(2)}) collective-permute-start(bf16[256,1024]{0,1:T(8,128)(2,1)S(1)} %fusion.61), channel_id=1, source_target_pairs={{0,1},{1,0},{2,3},{3,2},{4,5},{5,4},{6,7},{7,6},{8,9},{9,8},{10,11... | collective-permute-start | bytes 1572872 | tf_op jit(solution)/shard_map/ppermute | solution.py:81
  203.9 49.1 %collective-permute-start.33 = (f32[5,1024]{1,0:T(8,128)}, f32[5,1024]{1,0:T(8,128)}, u32[]{:S(2)}, u32[]{:S(2)}) collective-permute-start(f32[5,1024]{1,0:T(8,128)} %pad_maximum_fusion.13), channel_id=1, source_target_pairs={{0,2},{2,0},{4,6},{6,4},{8,10},{10,8},{12,14},{14,12},{16,18},{18,... | collective-permute-start | bytes 61448 | tf_op jit(solution)/shard_map/ppermute | solution.py:81
  208.6 13.8 %all-to-all-start.3 = ((bf16[16,64,128]{2,1,0:T(8,128)(2,1)}), bf16[16,64,128]{2,1,0:T(8,128)(2,1)S(1)}, u32[]{:S(2)}, u32[]{:S(2)}) async-start(bf16[16,64,128]{2,1,0:T(8,128)(2,1)} %reshape.741), calls=%async_computation.3 | async-start | bytes 524288 | tf_op jit(solution)/shard_map/all_to_all | solution.py:454
  224.1 15.3 %copy-start.9 = (bf16[256,512]{1,0:T(8,128)(2,1)S(1)}, bf16[256,512]{1,0:T(8,128)(2,1)}, u32[]{:S(2)}) copy-start(bf16[256,512]{1,0:T(8,128)(2,1)} %copy-done.8) | copy-start | bytes 786436
  224.1 15.3 %copy-start.23 = (bf16[256,1024]{1,0:T(8,128)(2,1)S(1)}, bf16[256,1024]{1,0:T(8,128)(2,1)}, u32[]{:S(2)}) copy-start(bf16[256,1024]{1,0:T(8,128)(2,1)} %fusion.54) | copy-start | bytes 1572868
  239.3 2.0 collective-permute-start.12
  239.7 49.2 %collective-permute-start.24 = (bf16[512,512]{1,0:T(8,128)(2,1)S(1)}, bf16[512,512]{1,0:T(8,128)(2,1)}, u32[]{:S(2)}, u32[]{:S(2)}) collective-permute-start(bf16[512,512]{1,0:T(8,128)(2,1)S(1)} %convolution_convert_fusion.5), channel_id=1, source_target_pairs={{0,2},{2,0},{4,6},{6,4},{8,10},{10,8},{12,14},{14,12},{16,18},{18,... | collective-permute-start | bytes 1572872 | tf_op jit(solution)/shard_map/ppermute | solution.py:81
  242.4 60.5 %all-to-all-start.4 = ((bf16[16,192,128]{2,1,0:T(8,128)(2,1)}), bf16[16,192,128]{2,1,0:T(8,128)(2,1)S(1)}, u32[]{:S(2)}, u32[]{:S(2)}) async-start(bf16[16,192,128]{2,1,0:T(8,128)(2,1)} %pad_maximum_fusion.2), calls=%async_computation.4 | async-start | bytes 1572864 | tf_op jit(solution)/shard_map/all_to_all | solution.py:468
  246.2 42.7 %copy-start.10 = (bf16[256,512]{1,0:T(8,128)(2,1)S(1)}, bf16[256,512]{1,0:T(8,128)(2,1)}, u32[]{:S(2)}) copy-start(bf16[256,512]{1,0:T(8,128)(2,1)} %copy-done.8) | copy-start | bytes 786436
  251.3 40.5 %collective-permute-start.10 = (bf16[256,1024]{0,1:T(8,128)(2,1)}, bf16[256,1024]{0,1:T(8,128)(2,1)}, u32[]{:S(2)}, u32[]{:S(2)}) collective-permute-start(bf16[256,1024]{0,1:T(8,128)(2,1)} %fusion.64), channel_id=1, source_target_pairs={{0,1},{1,0},{2,3},{3,2},{4,5},{5,4},{6,7},{7,6},{8,9},{9,8},{10,11... | collective-permute-start | bytes 1572872 | tf_op jit(solution)/shard_map/ppermute | solution.py:81
  253.8 4.0 %collective-permute-start.34 = (f32[5,1024]{1,0:T(8,128)S(1)}, f32[5,1024]{1,0:T(8,128)S(1)}, u32[]{:S(2)}, u32[]{:S(2)}) collective-permute-start(f32[5,1024]{1,0:T(8,128)S(1)} %fusion.177), channel_id=1, source_target_pairs={{0,4},{2,6},{4,0},{6,2},{8,12},{10,14},{12,8},{14,10},{16,20},{18,... | collective-permute-start | bytes 61448 | tf_op jit(solution)/shard_map/ppermute | solution.py:81
  257.8 16.1 %collective-permute-start.35 = (f32[5,1024]{1,0:T(8,128)S(1)}, f32[5,1024]{1,0:T(8,128)S(1)}, u32[]{:S(2)}, u32[]{:S(2)}) collective-permute-start(f32[5,1024]{1,0:T(8,128)S(1)} %add.647), channel_id=1, source_target_pairs={{0,8},{2,10},{4,12},{6,14},{8,0},{10,2},{12,4},{14,6},{16,24},{18,... | collective-permute-start | bytes 61448 | tf_op jit(solution)/shard_map/ppermute | solution.py:81
  273.9 13.3 %collective-permute-start.36 = (f32[5,1024]{1,0:T(8,128)S(1)}, f32[5,1024]{1,0:T(8,128)S(1)}, u32[]{:S(2)}, u32[]{:S(2)}) collective-permute-start(f32[5,1024]{1,0:T(8,128)S(1)} %add.648), channel_id=1, source_target_pairs={{0,16},{2,18},{4,20},{6,22},{8,24},{10,26},{12,28},{14,30},{16,0},... | collective-permute-start | bytes 61448 | tf_op jit(solution)/shard_map/ppermute | solution.py:81
  287.2 7.8 %collective-permute-start.37 = (f32[2,1024]{1,0:T(2,128)S(1)}, f32[2,1024]{1,0:T(2,128)S(1)}, u32[]{:S(2)}, u32[]{:S(2)}) collective-permute-start(f32[2,1024]{1,0:T(2,128)S(1)} %slice.254), channel_id=1, source_target_pairs={{0,1},{1,0},{2,3},{3,2},{4,5},{5,4},{6,7},{7,6},{8,9},{9,8},{10,11... | collective-permute-start | bytes 24584 | tf_op jit(solution)/shard_map/ppermute | solution.py:81
  290.4 8.2 %collective-permute-start.25 = (bf16[256,512]{1,0:T(8,128)(2,1)S(1)}, bf16[256,512]{1,0:T(8,128)(2,1)S(1)}, u32[]{:S(2)}, u32[]{:S(2)}) collective-permute-start(bf16[256,512]{1,0:T(8,128)(2,1)S(1)} %slice.348), channel_id=1, source_target_pairs={{0,4},{2,6},{4,0},{6,2},{8,12},{10,14},{12,8},{14,10},{16,20},{18,... | collective-permute-start | bytes 786440 | tf_op jit(solution)/shard_map/ppermute | solution.py:81
  299.4 10.8 %collective-permute-start.26 = (bf16[64,512]{1,0:T(8,128)(2,1)}, bf16[64,512]{1,0:T(8,128)(2,1)}, u32[]{:S(2)}, u32[]{:S(2)}) collective-permute-start(bf16[64,512]{1,0:T(8,128)(2,1)} %get-tuple-element.184), channel_id=1, source_target_pairs={{0,8},{2,10},{4,12},{6,14},{8,0},{10,2},{12,4},{14,6},{16,24},{18,... | collective-permute-start | bytes 196616 | tf_op jit(solution)/shard_map/ppermute | solution.py:81
  299.4 10.8 %collective-permute-start.28 = (bf16[64,512]{1,0:T(8,128)(2,1)}, bf16[64,512]{1,0:T(8,128)(2,1)}, u32[]{:S(2)}, u32[]{:S(2)}) collective-permute-start(bf16[64,512]{1,0:T(8,128)(2,1)} %get-tuple-element.185), channel_id=1, source_target_pairs={{0,24},{2,26},{4,28},{6,30},{8,16},{10,18},{12,20},{14,22},{16,8},... | collective-permute-start | bytes 196616 | tf_op jit(solution)/shard_map/ppermute | solution.py:81
  301.8 9.7 %collective-permute-start.27 = (bf16[64,512]{1,0:T(8,128)(2,1)}, bf16[64,512]{1,0:T(8,128)(2,1)}, u32[]{:S(2)}, u32[]{:S(2)}) collective-permute-start(bf16[64,512]{1,0:T(8,128)(2,1)} %get-tuple-element.186), channel_id=1, source_target_pairs={{0,16},{2,18},{4,20},{6,22},{8,24},{10,26},{12,28},{14,30},{16,0},... | collective-permute-start | bytes 196616 | tf_op jit(solution)/shard_map/ppermute | solution.py:81
  308.9 12.5 %collective-permute-start.13 = (bf16[256,1024]{0,1:T(8,128)(2,1)S(1)}, bf16[256,1024]{0,1:T(8,128)(2,1)S(1)}, u32[]{:S(2)}, u32[]{:S(2)}) collective-permute-start(bf16[256,1024]{0,1:T(8,128)(2,1)S(1)} %pad_maximum_fusion.5), channel_id=1, source_target_pairs={{0,1},{1,0},{2,3},{3,2},{4,5},{5,4},{6,7},{7,6},{8,9},{9,8},{10,11... | collective-permute-start | bytes 1572872 | tf_op jit(solution)/shard_map/ppermute | solution.py:81
  313.7 28.0 %collective-permute-start.19 = (bf16[512,768]{1,0:T(8,128)(2,1)S(1)}, bf16[512,768]{1,0:T(8,128)(2,1)S(1)}, u32[]{:S(2)}, u32[]{:S(2)}) collective-permute-start(bf16[512,768]{1,0:T(8,128)(2,1)S(1)} %convolution_convert_fusion.2), channel_id=1, source_target_pairs={{0,2},{2,0},{4,6},{6,4},{8,10},{10,8},{12,14},{14,12},{16,18},{18,... | collective-permute-start | bytes 2359304 | tf_op jit(solution)/shard_map/ppermute | solution.py:81
  314.2 29.1 %collective-permute-start.14 = (bf16[512,768]{1,0:T(8,128)(2,1)S(1)}, bf16[512,768]{1,0:T(8,128)(2,1)S(1)}, u32[]{:S(2)}, u32[]{:S(2)}) collective-permute-start(bf16[512,768]{1,0:T(8,128)(2,1)S(1)} %convolution_convert_fusion.3), channel_id=1, source_target_pairs={{0,2},{2,0},{4,6},{6,4},{8,10},{10,8},{12,14},{14,12},{16,18},{18,... | collective-permute-start | bytes 2359304 | tf_op jit(solution)/shard_map/ppermute | solution.py:81
  324.1 1.2 collective-permute-start.29
  325.3 3.7 collective-permute-start.30
  328.9 5.5 %collective-permute-start.31 = (f32[2,1024]{1,0:T(2,128)S(1)}, f32[2,1024]{1,0:T(2,128)S(1)}, u32[]{:S(2)}, u32[]{:S(2)}) collective-permute-start(f32[2,1024]{1,0:T(2,128)S(1)} %add.643), channel_id=1, source_target_pairs={{0,8},{2,10},{4,12},{6,14},{8,0},{10,2},{12,4},{14,6},{16,24},{18,... | collective-permute-start | bytes 24584 | tf_op jit(solution)/shard_map/ppermute | solution.py:81
  334.5 7.2 %collective-permute-start.32 = (f32[2,1024]{1,0:T(2,128)S(1)}, f32[2,1024]{1,0:T(2,128)S(1)}, u32[]{:S(2)}, u32[]{:S(2)}) collective-permute-start(f32[2,1024]{1,0:T(2,128)S(1)} %add.644), channel_id=1, source_target_pairs={{0,16},{2,18},{4,20},{6,22},{8,24},{10,26},{12,28},{14,30},{16,0},... | collective-permute-start | bytes 24584 | tf_op jit(solution)/shard_map/ppermute | solution.py:81
  342.2 12.1 %collective-permute-start.20 = (bf16[256,768]{1,0:T(8,128)(2,1)S(1)}, bf16[256,768]{1,0:T(8,128)(2,1)S(1)}, u32[]{:S(2)}, u32[]{:S(2)}) collective-permute-start(bf16[256,768]{1,0:T(8,128)(2,1)S(1)} %slice.346), channel_id=1, source_target_pairs={{0,4},{2,6},{4,0},{6,2},{8,12},{10,14},{12,8},{14,10},{16,20},{18,... | collective-permute-start | bytes 1179656 | tf_op jit(solution)/shard_map/ppermute | solution.py:81
  343.8 16.4 %collective-permute-start.15 = (bf16[256,768]{1,0:T(8,128)(2,1)S(1)}, bf16[256,768]{1,0:T(8,128)(2,1)S(1)}, u32[]{:S(2)}, u32[]{:S(2)}) collective-permute-start(bf16[256,768]{1,0:T(8,128)(2,1)S(1)} %slice.347), channel_id=1, source_target_pairs={{0,4},{2,6},{4,0},{6,2},{8,12},{10,14},{12,8},{14,10},{16,20},{18,... | collective-permute-start | bytes 1179656 | tf_op jit(solution)/shard_map/ppermute | solution.py:81
  354.5 8.0 %collective-permute-start.21 = (bf16[64,768]{1,0:T(8,128)(2,1)S(1)}, bf16[64,768]{1,0:T(8,128)(2,1)S(1)}, u32[]{:S(2)}, u32[]{:S(2)}) collective-permute-start(bf16[64,768]{1,0:T(8,128)(2,1)S(1)} %get-tuple-element.181), channel_id=1, source_target_pairs={{0,8},{2,10},{4,12},{6,14},{8,0},{10,2},{12,4},{14,6},{16,24},{18,... | collective-permute-start | bytes 294920 | tf_op jit(solution)/shard_map/ppermute | solution.py:81
  355.4 8.4 %collective-permute-start.23 = (bf16[64,768]{1,0:T(8,128)(2,1)S(1)}, bf16[64,768]{1,0:T(8,128)(2,1)S(1)}, u32[]{:S(2)}, u32[]{:S(2)}) collective-permute-start(bf16[64,768]{1,0:T(8,128)(2,1)S(1)} %get-tuple-element.182), channel_id=1, source_target_pairs={{0,24},{2,26},{4,28},{6,30},{8,16},{10,18},{12,20},{14,22},{16,8},... | collective-permute-start | bytes 294920 | tf_op jit(solution)/shard_map/ppermute | solution.py:81
  356.6 16.0 %copy-start.15 = (f32[3,64,512]{2,1,0:T(8,128)S(1)}, f32[3,64,512]{2,1,0:T(8,128)}, u32[]{:S(2)}) copy-start(f32[3,64,512]{2,1,0:T(8,128)} %param.28) | copy-start | bytes 1179652
  356.6 16.0 %copy-start.24 = (f32[3,64,512]{2,1,0:T(8,128)S(1)}, f32[3,64,512]{2,1,0:T(8,128)}, u32[]{:S(2)}) copy-start(f32[3,64,512]{2,1,0:T(8,128)} %param.29) | copy-start | bytes 1179652
  356.6 16.0 %copy-start.25 = (f32[3,64,512]{2,1,0:T(8,128)S(1)}, f32[3,64,512]{2,1,0:T(8,128)}, u32[]{:S(2)}) copy-start(f32[3,64,512]{2,1,0:T(8,128)} %param.30) | copy-start | bytes 1179652
  356.6 12.4 %collective-permute-start.22 = (bf16[64,768]{1,0:T(8,128)(2,1)S(1)}, bf16[64,768]{1,0:T(8,128)(2,1)S(1)}, u32[]{:S(2)}, u32[]{:S(2)}) collective-permute-start(bf16[64,768]{1,0:T(8,128)(2,1)S(1)} %get-tuple-element.183), channel_id=1, source_target_pairs={{0,16},{2,18},{4,20},{6,22},{8,24},{10,26},{12,28},{14,30},{16,0},... | collective-permute-start | bytes 294920 | tf_op jit(solution)/shard_map/ppermute | solution.py:81
  360.3 8.8 %collective-permute-start.16 = (bf16[64,768]{1,0:T(8,128)(2,1)S(1)}, bf16[64,768]{1,0:T(8,128)(2,1)S(1)}, u32[]{:S(2)}, u32[]{:S(2)}) collective-permute-start(bf16[64,768]{1,0:T(8,128)(2,1)S(1)} %get-tuple-element.178), channel_id=1, source_target_pairs={{0,8},{2,10},{4,12},{6,14},{8,0},{10,2},{12,4},{14,6},{16,24},{18,... | collective-permute-start | bytes 294920 | tf_op jit(solution)/shard_map/ppermute | solution.py:81
  361.3 7.8 %collective-permute-start.18 = (bf16[64,768]{1,0:T(8,128)(2,1)S(1)}, bf16[64,768]{1,0:T(8,128)(2,1)S(1)}, u32[]{:S(2)}, u32[]{:S(2)}) collective-permute-start(bf16[64,768]{1,0:T(8,128)(2,1)S(1)} %get-tuple-element.179), channel_id=1, source_target_pairs={{0,24},{2,26},{4,28},{6,30},{8,16},{10,18},{12,20},{14,22},{16,8},... | collective-permute-start | bytes 294920 | tf_op jit(solution)/shard_map/ppermute | solution.py:81
  362.4 10.1 %collective-permute-start.17 = (bf16[64,768]{1,0:T(8,128)(2,1)S(1)}, bf16[64,768]{1,0:T(8,128)(2,1)S(1)}, u32[]{:S(2)}, u32[]{:S(2)}) collective-permute-start(bf16[64,768]{1,0:T(8,128)(2,1)S(1)} %get-tuple-element.180), channel_id=1, source_target_pairs={{0,16},{2,18},{4,20},{6,22},{8,24},{10,26},{12,28},{14,30},{16,0},... | collective-permute-start | bytes 294920 | tf_op jit(solution)/shard_map/ppermute | solution.py:81
  (29 other events, 122.3 us)
Sparse Core Ops, SparseCore 0:
  11.5 107.2 all-gather.1
  201.4 124.7 reduce-scatter.1

commit v3 on v2

v3 whole, which is shorter than its diff:
```python
import functools

import jax
import jax.numpy as jnp
from jax import lax
from jax.experimental import pallas as pl
from jax.experimental.pallas import tpu as pltpu
from jax.sharding import PartitionSpec as P

D = 1024
DH = 64
FF = 4096
BLOCK = 64
STEP = 10
LISTED = 8

eps_norm = 1e-05
masked_score = -1e30
beta_one = 0.9
beta_two = 0.999
eps_adam = 1e-08
decay_rate = 0.01
rate_qkv = 0.1
rate_proj = 1.0
rate_up = 0.1
rate_down = 0.05
rate_vector = 2.0

bf16 = jnp.bfloat16
f32 = jnp.float32


def lookup(index_table, index_rows):
    matches = index_rows[..., None] == jnp.arange(index_table.shape[0], dtype=jnp.int32)
    return jnp.sum(jnp.where(matches, index_table, 0), axis=-1)


def owning_doc(doc_end, block_ids):
    return jnp.sum((block_ids[..., None] >= doc_end).astype(jnp.int32), axis=-1)


def dot(lhs, rhs, lhs_dim, rhs_dim):
    return lax.dot_general(
        lhs, rhs, (((lhs_dim,), (rhs_dim,)), ((), ())), preferred_element_type=f32
    )


def norm_rows(token_rows, gain_row, bias_row):
    row_mean = jnp.mean(token_rows, axis=-1, keepdims=True)
    centred = token_rows - row_mean
    row_var = jnp.mean(centred * centred, axis=-1, keepdims=True)
    inv_scale = lax.rsqrt(row_var + eps_norm)
    unit_rows = centred * inv_scale
    return (unit_rows * gain_row + bias_row, unit_rows, inv_scale)


def norm_back(grad_in, unit_rows, inv_scale, gain_row):
    scaled = grad_in * gain_row
    first_mean = jnp.mean(scaled, axis=-1, keepdims=True)
    second_mean = jnp.mean(scaled * unit_rows, axis=-1, keepdims=True)
    return inv_scale * (scaled - first_mean - unit_rows * second_mean)


def gelu_tanh(values):
    return jax.nn.gelu(values, approximate=True)


def adam_step(param_old, gradient, first_old, second_old, step_rate):
    first_new = beta_one * first_old + (1.0 - beta_one) * gradient
    second_new = beta_two * second_old + (1.0 - beta_two) * gradient * gradient
    first_hat = first_new / (1.0 - beta_one**STEP)
    second_hat = second_new / (1.0 - beta_two**STEP)
    updated = param_old - step_rate * (
        first_hat / (jnp.sqrt(second_hat) + eps_adam) + decay_rate * param_old
    )
    return (updated, first_new, second_new)


def xor_permute(value, axis, mask):
    count = lax.axis_size(axis)
    return lax.ppermute(value, axis, [(i, i ^ mask) for i in range(count)])


def head_other(partial_low):
    return xor_permute(partial_low, "head", 1)


def head_total(partial_low, other):
    total = partial_low.astype(f32) + other.astype(f32)
    step = 2
    while step < lax.axis_size("head"):
        total = total + xor_permute(total, "head", step)
        step *= 2
    return total


def axis_sum(value, axis):
    step = 1
    while step < lax.axis_size(axis):
        value = value + xor_permute(value, axis, step)
        step *= 2
    return value


def lane_cuts(lanes):
    chips = lanes // 2
    ys = 1 << ((chips.bit_length() - 1) // 2)
    return 2, ys, chips // ys


def relative_lanes(lanes):
    cores, ys, zs = lane_cuts(lanes)
    return [(kz * ys + ky) * cores + kc for kc in range(cores) for ky in range(ys) for kz in range(zs)]


def relative_gather(mine):
    cores, ys, zs = lane_cuts(lax.axis_size("seq"))
    column = [mine] + [xor_permute(mine, "seq", kz * ys * cores) for kz in range(1, zs)]
    pieces = list(column)
    for ky in range(1, ys):
        pieces += [xor_permute(piece, "seq", ky * cores) for piece in column]
    near = jnp.concatenate(pieces, axis=0)
    return near, xor_permute(near, "seq", 1)


GROUP = 4


def fill_rows(source_refs, kv_ref):
    start = 0
    for source_ref in source_refs:
        count = source_ref.shape[0]
        size = kv_ref.shape[0] // (count * len(source_refs))

        def copy(i, carry, start=start, size=size, source_ref=source_ref):
            at = pl.ds(pl.multiple_of(start + i * size, size), size)
            kv_ref[at, :] = source_ref[i, :size, :]
            return carry

        lax.fori_loop(0, count, copy, 0)
        start += count * size


def attend_kernel(off_ref, record_ref, *refs):
    *source_refs, bias_ref, ctx_ref, prob_ref, kv_ref = refs
    lanes, rows = ctx_ref.shape[0], ctx_ref.shape[1]
    first = record_ref.shape[1] - rows
    left = lax.broadcasted_iota(jnp.int32, (rows, 2 * DH), 1) < DH
    scale = DH**-0.5
    fill_rows(source_refs, kv_ref)

    def step(t, carry):
        units = [(t * GROUP + g, half) for g in range(GROUP) for half in range(2)]
        listed, scores = [], []
        for i, half in units:
            q_pair = record_ref[i, first:, :].astype(f32) * scale
            q_one = q_pair if half == 0 else pltpu.roll(q_pair, DH, 1)
            q_one = jnp.where(left, q_one, 0.0).astype(bf16)
            rows_here = jnp.concatenate(
                [
                    kv_ref[pl.ds(pl.multiple_of(off_ref[2 * i + half, j], BLOCK), BLOCK), :]
                    for j in range(LISTED)
                ],
                axis=0,
            )
            listed.append(rows_here)
            scores.append(dot(q_one, rows_here, 1, 1) + bias_ref[i, half : half + 1, :])
        tops = [jnp.max(score, axis=1, keepdims=True) for score in scores]
        grown = [jnp.exp(score - top) for score, top in zip(scores, tops)]
        totals = [jnp.sum(part, axis=1, keepdims=True) for part in grown]
        probs = [(part * (1.0 / total)).astype(bf16) for part, total in zip(grown, totals)]
        outs = []
        for (i, half), prob, rows_here in zip(units, probs, listed):
            prob_ref[i, half] = prob
            outs.append(dot(prob, rows_here, 1, 0))
        for g in range(GROUP):
            ctx_ref[t * GROUP + g] = jnp.where(
                left, pltpu.roll(outs[2 * g], DH, 1), outs[2 * g + 1]
            ).astype(bf16)
        return carry

    lax.fori_loop(0, lanes // GROUP, step, 0)


def attend_back_kernel(off_ref, record_ref, *refs):
    *source_refs, prob_ref, dctx_ref, dq_ref, own_ref, away_ref, kv_ref, dkv_ref = refs
    lanes, rows = dq_ref.shape[0], dq_ref.shape[1]
    first = record_ref.shape[1] - rows
    left = lax.broadcasted_iota(jnp.int32, (rows, 2 * DH), 1) < DH
    scale = DH**-0.5
    fill_rows(source_refs, kv_ref)
    dkv_ref[...] = jnp.zeros_like(dkv_ref)

    def step(t, carry):
        units = [(t * GROUP + g, half) for g in range(GROUP) for half in range(2)]
        queries, grads, offs, listed, prob_grads = [], [], [], [], []
        for i, half in units:
            q_pair = record_ref[i, first:, :].astype(f32) * scale
            d_pair = dctx_ref[i].astype(f32)
            q_one = q_pair if half == 0 else pltpu.roll(q_pair, DH, 1)
            queries.append(jnp.where(left, q_one, 0.0).astype(bf16))
            d_one = pltpu.roll(d_pair, DH, 1) if half == 0 else d_pair
            grads.append(jnp.where(left, 0.0, d_one).astype(bf16))
            offs.append(
                [pl.multiple_of(off_ref[2 * i + half, j], BLOCK) for j in range(LISTED)]
            )
            listed.append(
                jnp.concatenate([kv_ref[pl.ds(o, BLOCK), :] for o in offs[-1]], axis=0)
            )
            prob_grads.append(dot(grads[-1], listed[-1], 1, 1))
        probs_low = [prob_ref[i, half] for i, half in units]
        probs = [prob.astype(f32) for prob in probs_low]
        weighted = [prob * grad for prob, grad in zip(probs, prob_grads)]
        row_dots = [jnp.sum(part, axis=1, keepdims=True) for part in weighted]
        scores_low = [
            (part - prob * row_dot).astype(bf16)
            for part, prob, row_dot in zip(weighted, probs, row_dots)
        ]
        outs = [dot(score, rows_here, 1, 0) * scale for score, rows_here in zip(scores_low, listed)]
        for n in range(len(units)):
            both = jnp.concatenate([scores_low[n], probs_low[n]], axis=0)
            mates = jnp.concatenate([queries[n], grads[n]], axis=0)
            kv_grad = dot(both, mates, 0, 0)
            for j in range(LISTED):
                at = pl.ds(offs[n][j], BLOCK)
                dkv_ref[at, :] += kv_grad[j * BLOCK : (j + 1) * BLOCK]
        for g in range(GROUP):
            dq_ref[t * GROUP + g] = jnp.where(
                left, outs[2 * g], pltpu.roll(outs[2 * g + 1], DH, 1)
            ).astype(bf16)
        return carry

    lax.fori_loop(0, lanes // GROUP, step, 0)
    held = own_ref.shape[0]
    own_ref[...] = dkv_ref[:held, :]
    away_ref[...] = dkv_ref[held:, :].astype(bf16)


def message_kernel(own_ref, other_ref, dq_ref, mixed_ref, msg_ref):
    lanes, record = msg_ref.shape[0], msg_ref.shape[1]
    part_rows = 2 * record // 3
    pair_rows = part_rows // 2
    left = lax.broadcasted_iota(jnp.int32, (pair_rows, 2 * DH), 1) < DH

    def step(i, carry):
        row = pl.multiple_of(i * part_rows, part_rows)
        at = pl.ds(row, part_rows)
        total = own_ref[at, :]
        for k in range(other_ref.shape[0]):
            total += other_ref[k, at, :].astype(f32)
        low = total.astype(bf16)
        mixed_ref[at, : 2 * DH] = low
        msg_ref[i, :part_rows, :] = low
        dq = dq_ref[i]
        msg_ref[i, part_rows:, :] = dq
        dq = dq.astype(f32)
        second = pltpu.roll(dq, DH, 1)
        mixed_ref[pl.ds(row, pair_rows), 2 * DH :] = jnp.where(left, dq, 0.0).astype(bf16)
        mixed_ref[
            pl.ds(pl.multiple_of(row + pair_rows, pair_rows), pair_rows), 2 * DH :
        ] = jnp.where(left, second, 0.0).astype(bf16)
        return carry

    lax.fori_loop(0, lanes, step, 0)


def head_grad_kernel(head_ref, mixed_ref, *refs):
    *part_refs, out_ref = refs
    count = len(part_refs) // 2
    cut, size = part_refs[0].shape
    for k in range(count):
        row = pl.multiple_of((head_ref[0] ^ k) * size, size)
        total = dot(part_refs[k][...], mixed_ref[:cut, :], 0, 0)
        total += dot(part_refs[count + k][...], mixed_ref[cut:, :], 0, 0)
        out_ref[pl.ds(row, size), :] = total.astype(bf16)


def pack_kernel(share, low_ref, near_ref, far_ref, msg_ref, rows_ref):
    lanes, record = msg_ref.shape[0], msg_ref.shape[1]
    heads = lanes // share
    feat = heads * DH
    part_rows = 2 * record // 3
    pair_rows = part_rows // 2
    half = D // 2
    for c in range(3):
        cols = slice(c * feat, (c + 1) * feat)
        rows_ref[:, cols] = dot(low_ref[:, :half], near_ref[:, cols], 1, 0) + dot(
            low_ref[:, half:], far_ref[:, cols], 1, 0
        )
    left = lax.broadcasted_iota(jnp.int32, (part_rows, 2 * DH), 1) < DH
    for h in range(0, heads, 2):
        for r in range(share):
            at = slice(r * part_rows, (r + 1) * part_rows)
            query, keys, vals = (
                rows_ref[at, c * feat + h * DH : c * feat + (h + 2) * DH] for c in range(3)
            )
            even, odd = h * share + r, (h + 1) * share + r
            msg_ref[even, :part_rows, :] = jnp.where(left, keys, pltpu.roll(vals, DH, 1)).astype(
                bf16
            )
            msg_ref[odd, :part_rows, :] = jnp.where(left, pltpu.roll(keys, DH, 1), vals).astype(
                bf16
            )
            first, second = query[:pair_rows], query[pair_rows:]
            over = left[:pair_rows]
            msg_ref[even, part_rows:, :] = jnp.where(over, first, pltpu.roll(second, DH, 1)).astype(
                bf16
            )
            msg_ref[odd, part_rows:, :] = jnp.where(over, pltpu.roll(first, DH, 1), second).astype(
                bf16
            )


def unpack_pairs(read, heads, share, pair_rows, write):
    left = lax.broadcasted_iota(jnp.int32, (pair_rows, 2 * DH), 1) < DH
    for h in range(0, heads, 2):
        cols = slice(h * DH, (h + 2) * DH)
        for r in range(share):
            even, odd = read(h * share + r), read((h + 1) * share + r)
            base = 2 * r * pair_rows
            first = jnp.where(left, even, pltpu.roll(odd, DH, 1))
            second = jnp.where(left, pltpu.roll(even, DH, 1), odd)
            write(slice(base, base + pair_rows), cols, first)
            write(slice(base + pair_rows, base + 2 * pair_rows), cols, second)


def project_kernel(share, pairs_ref, proj_ref, ctx_ref, out_ref):
    heads, pair_rows = pairs_ref.shape[0] // share, pairs_ref.shape[1]

    def write(rows, cols, value):
        ctx_ref[rows, cols] = value.astype(bf16)

    unpack_pairs(lambda n: pairs_ref[n].astype(f32), heads, share, pair_rows, write)
    out_ref[...] = dot(ctx_ref[...], proj_ref[...], 1, 1).astype(bf16)


def dctx_kernel(share, low_ref, proj_ref, pairs_ref):
    heads, pair_rows = pairs_ref.shape[0] // share, pairs_ref.shape[1]
    left = lax.broadcasted_iota(jnp.int32, (pair_rows, 2 * DH), 1) < DH
    grad = dot(low_ref[...], proj_ref[...], 1, 0)
    for h in range(0, heads, 2):
        cols = slice(h * DH, (h + 2) * DH)
        for r in range(share):
            base = 2 * r * pair_rows
            first = grad[base : base + pair_rows, cols]
            second = grad[base + pair_rows : base + 2 * pair_rows, cols]
            pairs_ref[h * share + r] = jnp.where(left, first, pltpu.roll(second, DH, 1)).astype(
                bf16
            )
            pairs_ref[(h + 1) * share + r] = jnp.where(
                left, pltpu.roll(first, DH, 1), second
            ).astype(bf16)


def one_grad_kernel(share, msg_ref, near_ref, far_ref, unit_ref, place_ref, out_ref, late_ref, rows_ref):
    lanes, record = msg_ref.shape[0], msg_ref.shape[1]
    heads = lanes // share
    feat = heads * DH
    part_rows = 2 * record // 3
    pair_rows = part_rows // 2

    def write(rows, cols, value):
        rows_ref[rows, cols] = value.astype(bf16)

    unpack_pairs(
        lambda n: msg_ref[n, part_rows:, :].astype(f32), heads, share, pair_rows, write
    )
    left = lax.broadcasted_iota(jnp.int32, (part_rows, 2 * DH), 1) < DH
    for h in range(0, heads, 2):
        for r in range(share):
            even = msg_ref[h * share + r, :part_rows, :].astype(f32)
            odd = msg_ref[(h + 1) * share + r, :part_rows, :].astype(f32)
            at = slice(r * part_rows, (r + 1) * part_rows)
            keys = jnp.where(left, even, pltpu.roll(odd, DH, 1))
            vals = jnp.where(left, pltpu.roll(even, DH, 1), odd)
            rows_ref[at, feat + h * DH : feat + (h + 2) * DH] = keys.astype(bf16)
            rows_ref[at, 2 * feat + h * DH : 2 * feat + (h + 2) * DH] = vals.astype(bf16)
    half = D // 2
    out_ref[:, :half] = dot(rows_ref[...], near_ref[...], 1, 1).astype(bf16)
    out_ref[:, half:] = dot(rows_ref[...], far_ref[...], 1, 1).astype(bf16)
    grad = out_ref[...].astype(f32)
    gain = jnp.sum(grad * unit_ref[...], axis=0, keepdims=True)
    shift = jnp.sum(grad, axis=0, keepdims=True)
    sums = jnp.concatenate([gain, shift, jnp.zeros((14, D), f32)], axis=0).astype(bf16)
    late_ref[...] = dot(sums, place_ref[...], 1, 1).astype(bf16)


def weight_grad_kernel(lhs_a, rhs_a, lhs_b, rhs_b, out_ref, *, first):
    at = pl.program_id(0)

    @pl.when(at < first)
    def _():
        out_ref[...] = dot(lhs_a[...], rhs_a[...], 0, 0).astype(bf16)

    @pl.when(at >= first)
    def _():
        out_ref[...] = dot(lhs_b[...], rhs_b[...], 0, 0).astype(bf16)


def last_grad_kernel(lhs, rhs, whole_ref, out_ref):
    out_ref[...] = dot(lhs[...], rhs[...], 0, 0).astype(bf16)


VMEM_LIMIT = 48 * 1024 * 1024


def in_smem():
    return pl.BlockSpec(memory_space=pltpu.SMEM)


def call(kernel, outs, specs, scratch=(), out_specs=None):
    return pl.pallas_call(
        kernel,
        grid=(1,),
        out_shape=outs,
        in_specs=specs,
        out_specs=jax.tree.map(lambda o: whole(o.shape), outs) if out_specs is None else out_specs,
        scratch_shapes=list(scratch),
        compiler_params=pltpu.CompilerParams(vmem_limit_bytes=VMEM_LIMIT),
    )


def whole(shape):
    return pl.BlockSpec(tuple(shape), lambda i: (0,) * len(shape))


def array(shape, dtype=bf16):
    return jax.ShapeDtypeStruct(shape, dtype)


def ffn_weight_grads(first, second, width):
    units = first[1].shape[1]
    block = min(512, units)
    count = units // block
    specs = []
    for start, (lhs, rhs) in enumerate((first, second)):
        specs.append(whole(lhs.shape))
        specs.append(
            pl.BlockSpec(
                (rhs.shape[0], block),
                lambda i, start=start: (0, jnp.clip(i - start * count, 0, count - 1)),
            )
        )
    return pl.pallas_call(
        functools.partial(weight_grad_kernel, first=count),
        grid=(2 * count,),
        out_shape=array((D, width)),
        in_specs=specs,
        out_specs=pl.BlockSpec((D, block), lambda i: (0, i)),
        compiler_params=pltpu.CompilerParams(vmem_limit_bytes=VMEM_LIMIT),
        cost_estimate=pl.CostEstimate(
            flops=8 * D * units * first[1].shape[0], bytes_accessed=4 * D * width, transcendentals=0
        ),
    )(*first, *second)


def last_weight_grad(lhs, rhs, into):
    block = rhs.shape[1]
    return pl.pallas_call(
        last_grad_kernel,
        grid=(1,),
        out_shape=array(into.shape),
        in_specs=[whole(lhs.shape), whole(rhs.shape), pl.BlockSpec(memory_space=pl.ANY)],
        out_specs=pl.BlockSpec((D, block), lambda i: (0, into.shape[1] // block - 1)),
        input_output_aliases={2: 0},
        compiler_params=pltpu.CompilerParams(vmem_limit_bytes=VMEM_LIMIT),
    )(lhs, rhs, into)


def body(
    layer_input,
    output_grad,
    random_pick,
    doc_blocks,
    last_fill,
    shard_owner,
    qkv_weight,
    qkv_first,
    qkv_second,
    proj_weight,
    proj_first,
    proj_second,
    up_weight,
    up_first,
    up_second,
    down_weight,
    down_first,
    down_second,
    vec_params,
    vec_first,
    vec_second,
):
    lanes = lax.axis_size("seq")
    lane_index = lax.axis_index("seq")
    head_groups = lax.axis_size("head")
    head_index = lax.axis_index("head")
    slots = layer_input.shape[0]
    heads = random_pick.shape[2]
    feat = heads * DH
    units = up_weight.shape[1]
    rows = slots * BLOCK
    block_total = slots * lanes
    share = lanes // heads
    part_rows = rows // share
    pair_rows = part_rows // 2
    my_part = lane_index % share
    width = D // lanes

    picks = random_pick[:, 0].transpose(1, 0, 2).reshape(heads, slots * 3)
    picks = jnp.broadcast_to(picks[:, None], (heads, share, slots * 3)).reshape(lanes, slots * 3)
    picks = lax.all_to_all(picks, "seq", 0, 0, tiled=True).reshape(lanes, slots, 3)

    qkv_mine = qkv_weight.astype(bf16).transpose(1, 0, 2).reshape(width, 3 * feat)
    qkv_near, qkv_far = relative_gather(qkv_mine)
    rest_mine = jnp.concatenate(
        [up_weight.astype(bf16), down_weight.astype(bf16).T, proj_weight.astype(bf16).T], axis=1
    )
    rest_full = lax.all_gather(rest_mine, "seq", axis=0, tiled=True)
    up_full = rest_full[:, :units]
    down_full = rest_full[:, units : 2 * units]
    proj_block = pl.BlockSpec((D, feat), lambda i: (0, 2 * units // feat))

    column = jnp.arange(D, dtype=jnp.int32)
    owner = lookup(shard_owner, column // width)
    masks = jnp.array(relative_lanes(lanes), jnp.int32)
    position = jnp.sum(
        jnp.where(
            masks[None, :] == (owner ^ lane_index)[:, None], jnp.arange(lanes, dtype=jnp.int32), 0
        ),
        axis=1,
    )
    place = (owner * width + column % width)[:, None] == column[None, :]
    place_near = (position * width + column % width)[:, None] == column[None, :]
    place, place_near = place.astype(bf16), place_near.astype(bf16)
    rows_in = layer_input.reshape(rows, D)
    token_rows = dot(rows_in, place, 1, 0)
    grad_low = dot(output_grad.reshape(rows, D), place, 1, 0).astype(bf16)
    grad_rows = grad_low.astype(f32)
    exact = functools.partial(
        lax.dot_general, precision=lax.Precision.HIGHEST, preferred_element_type=f32
    )
    ahead = (((1,), (0,)), ((), ()))
    back = (((1,), (1,)), ((), ()))
    vec_rows = exact(vec_params[:5], place.astype(f32), ahead)
    vec_near = exact(vec_params[:2], place_near.astype(f32), ahead)
    up_bias = lax.dynamic_slice_in_dim(vec_params[5:].reshape(FF), head_index * units, units)

    normed_one, unit_one, scale_one = norm_rows(
        dot(rows_in, place_near, 1, 0), vec_near[0], vec_near[1]
    )
    low_one = normed_one.astype(bf16)
    lane_one = norm_rows(token_rows, vec_rows[0], vec_rows[1])[0].astype(bf16)
    own_cols = D // head_groups
    lane_one = lax.dynamic_slice_in_dim(lane_one, head_index * own_cols, own_cols, axis=1)
    low_one, lane_one = lax.optimization_barrier((low_one, lane_one))
    half = D // 2
    record = part_rows + pair_rows
    message = call(
        functools.partial(pack_kernel, share),
        array((lanes, record, 2 * DH)),
        [whole((rows, D)), whole((half, 3 * feat)), whole((half, 3 * feat))],
        [pltpu.VMEM((rows, 3 * feat), f32)],
    )(low_one, qkv_near, qkv_far)
    message, picks = lax.optimization_barrier((message, picks))
    received = lax.all_to_all(message, "seq", 0, 0, tiled=True)

    doc_end = jnp.cumsum(doc_blocks)
    doc_start = doc_end - doc_blocks
    doc_length = (doc_blocks - 1) * BLOCK + last_fill
    half_slot = (my_part * part_rows + jnp.arange(2, dtype=jnp.int32) * pair_rows) // BLOCK
    query_ids = half_slot[None, :] * lanes + jnp.arange(lanes, dtype=jnp.int32)[:, None]
    pick_half = jnp.sum(
        jnp.where(
            (half_slot[:, None] == jnp.arange(slots, dtype=jnp.int32)[None, :])[None, :, :, None],
            picks[:, None],
            0,
        ),
        axis=2,
    )
    query_doc = owning_doc(doc_end, query_ids)
    doc_first = lookup(doc_start, query_doc)
    doc_count = lookup(doc_blocks, query_doc)
    query_length = lookup(doc_length, query_doc)
    key_ids = jnp.concatenate(
        [
            jnp.stack(
                [
                    (query_ids - 1) % block_total,
                    query_ids,
                    (query_ids + 1) % block_total,
                    doc_first,
                    (doc_first + 1) % block_total,
                ],
                axis=-1,
            ),
            doc_first[..., None] + pick_half % doc_count[..., None],
        ],
        axis=-1,
    )
    same_doc = owning_doc(doc_end, key_ids) == query_doc[..., None]
    live_count = jnp.where(
        same_doc, query_length[..., None] - (key_ids - doc_first[..., None]) * BLOCK, 0
    )
    token = jnp.arange(BLOCK, dtype=jnp.int32)
    bias = jnp.where(token < live_count[..., None], 0.0, masked_score).astype(f32)
    bias = bias.reshape(lanes, 2, LISTED * BLOCK)
    key_lane = key_ids % lanes
    key_slot = key_ids // lanes
    if part_rows >= BLOCK:
        part_slots = part_rows // BLOCK
        offsets = (((key_slot // part_slots) ^ my_part) * lanes + key_lane) * part_rows
        offsets += (key_slot % part_slots) * BLOCK
    else:
        offsets = (key_lane * slots + key_slot) * BLOCK
    offsets = offsets.reshape(lanes * 2, LISTED)
    received, offsets, bias = lax.optimization_barrier((received, offsets, bias))

    parts = jnp.arange(share, dtype=jnp.int32)
    sources = [received] + [xor_permute(received, "seq", k) for k in range(1, share)]
    if part_rows < BLOCK:
        kv_parts = jnp.stack([part[:, :part_rows] for part in sources])
        kv_parts = kv_parts[parts ^ my_part].transpose(1, 0, 2, 3)
        sources = [kv_parts.reshape(lanes, slots * BLOCK, 2 * DH)]
    kv_shape = (block_total * BLOCK, 2 * DH)
    pairs_shape = (lanes, pair_rows, 2 * DH)
    probs_shape = (lanes, 2, pair_rows, LISTED * BLOCK)

    lane_one, sources = lax.optimization_barrier((lane_one, sources))
    all_one = lax.all_gather(lane_one.reshape(share, part_rows, own_cols), "seq", axis=0, tiled=False)
    all_one = lax.dynamic_index_in_dim(all_one, my_part, 1, keepdims=False)
    all_one = all_one.reshape(lanes * part_rows, own_cols)

    attend_specs = [in_smem(), whole(received.shape)] + [whole(part.shape) for part in sources]
    ctx_pairs, probs = call(
        attend_kernel,
        (array(pairs_shape), array(probs_shape)),
        attend_specs + [whole(bias.shape)],
        [pltpu.VMEM(kv_shape, bf16)],
    )(offsets, received, *sources, bias)
    ctx_pairs = lax.all_to_all(ctx_pairs, "seq", 0, 0, tiled=True)

    context, attn_part = call(
        functools.partial(project_kernel, share),
        (array((rows, feat)), array((rows, D))),
        [whole(pairs_shape), proj_block],
    )(ctx_pairs, rest_full)
    attn_sum = head_total(attn_part, head_other(attn_part))
    mid_rows = token_rows + attn_sum
    normed_two, unit_two, scale_two = norm_rows(mid_rows, vec_rows[2], vec_rows[3])
    low_two = normed_two.astype(bf16)
    hidden = dot(low_two, up_full, 1, 0) + up_bias
    active = gelu_tanh(hidden).astype(bf16)
    act_grad = dot(grad_low, down_full, 1, 0)
    hidden_grad = jax.vjp(gelu_tanh, hidden)[1](act_grad)[0]
    hidden_low = hidden_grad.astype(bf16)
    two_part = dot(hidden_low, up_full, 1, 1).astype(bf16)
    two_other = head_other(two_part)
    rest_grads = ffn_weight_grads(
        (low_two, hidden_low), (grad_low, active), rest_full.shape[1]
    )
    two_other, rest_grads = lax.optimization_barrier((two_other, rest_grads))
    two_grad = head_total(two_part, two_other)
    cut = all_one.shape[0] // 8
    first_part = [all_one[:cut]] + [
        xor_permute(all_one[:cut], "head", k) for k in range(1, head_groups)
    ]
    up_bias_grad = jnp.sum(hidden_grad, axis=0)

    mid_grad = grad_rows + norm_back(two_grad, unit_two, scale_two, vec_rows[2])
    attn_low = mid_grad.astype(bf16)
    dctx_pairs = call(
        functools.partial(dctx_kernel, share),
        array(pairs_shape),
        [whole((rows, D)), proj_block],
    )(attn_low, rest_full)
    rest_grads = last_weight_grad(attn_low, context, rest_grads)
    rest_owned = lax.psum_scatter(rest_grads, "seq", scatter_dimension=0, tiled=True).astype(f32)
    dctx_pairs = lax.all_to_all(dctx_pairs, "seq", 0, 0, tiled=True)
    dctx_pairs, rest_grads, first_part = lax.optimization_barrier(
        (dctx_pairs, rest_grads, first_part)
    )
    later_one, _ = lax.optimization_barrier((all_one[cut:], first_part))
    second_part = [later_one] + [
        xor_permute(later_one, "head", k) for k in range(1, head_groups)
    ]
    held_rows = lanes * part_rows
    away_rows = kv_shape[0] - held_rows
    if part_rows < BLOCK:
        back_shapes = (kv_shape[0] // 2,) * 2
    else:
        back_shapes = (held_rows, away_rows)
    dq_pairs, dkv_own, dkv_away = call(
        attend_back_kernel,
        (
            array(pairs_shape),
            array((back_shapes[0], 2 * DH), f32),
            array((back_shapes[1], 2 * DH)),
        ),
        attend_specs + [whole(probs_shape), whole(pairs_shape)],
        [pltpu.VMEM(kv_shape, bf16), pltpu.VMEM(kv_shape, f32)],
    )(offsets, received, *sources, probs, dctx_pairs)
    if part_rows < BLOCK:
        dkv_parts = jnp.concatenate([dkv_own, dkv_away.astype(f32)], axis=0)
        dkv_parts = dkv_parts.reshape(lanes, share, part_rows, 2 * DH)
        dkv_parts = dkv_parts[:, parts ^ my_part].transpose(1, 0, 2, 3)
        dkv_own = dkv_parts[0].reshape(held_rows, 2 * DH)
        dkv_away = dkv_parts[1:].astype(bf16)
    dkv_away = dkv_away.reshape(share - 1, held_rows, 2 * DH)
    others = jnp.stack([xor_permute(dkv_away[k - 1], "seq", k) for k in range(1, share)])
    others, active = lax.optimization_barrier((others, active))
    mixed, message = call(
        message_kernel,
        (array((held_rows, 4 * DH)), array((lanes, record, 2 * DH))),
        [whole((held_rows, 2 * DH)), whole(others.shape), whole(pairs_shape)],
    )(dkv_own, others, dq_pairs)
    returned = lax.all_to_all(message, "seq", 0, 0, tiled=True)
    head_grads = call(
        head_grad_kernel,
        array((D, 4 * DH)),
        [in_smem(), whole(mixed.shape)] + [whole(part.shape) for part in first_part + second_part],
    )(head_index.reshape(1).astype(jnp.int32), mixed, *first_part, *second_part)
    ffn_part = dot(active, down_full, 1, 1).astype(bf16)
    ffn_other = head_other(ffn_part)
    early_rows = jnp.stack(
        [jnp.sum(two_grad * unit_two, axis=0), jnp.sum(two_grad, axis=0), jnp.sum(grad_rows, axis=0)]
    )
    early_rows = exact(early_rows, place.astype(f32), back)
    early_rows = jnp.concatenate([early_rows, up_bias_grad.reshape(units // D, D)], axis=0)
    returned, head_grads, ffn_other, early_rows = lax.optimization_barrier(
        (returned, head_grads, ffn_other, early_rows)
    )
    result = (mid_rows + head_total(ffn_part, ffn_other) + vec_rows[4]).astype(bf16)
    head_grads = head_grads.reshape(lanes, width, 4 * DH)
    grad_q = head_grads[:, :, 2 * DH : 3 * DH]
    head_grads = jnp.concatenate(
        [
            head_grads[:, :, : 2 * DH],
            jnp.concatenate([grad_q[:, : width // 2], grad_q[:, width // 2 :]], axis=2),
        ],
        axis=1,
    )
    one_part, late_rows = call(
        functools.partial(one_grad_kernel, share),
        (array((rows, D)), array((16, D))),
        [whole(message.shape), whole((half, 3 * feat)), whole((half, 3 * feat))]
        + [whole((rows, D)), whole((D, D))],
        [pltpu.VMEM((rows, 3 * feat), bf16)],
    )(returned, qkv_near, qkv_far, unit_one, place_near)
    one_other = head_other(one_part)
    early_rows, one_part = lax.optimization_barrier((early_rows, one_part))
    early_rows = axis_sum(early_rows, "seq")
    late_rows = late_rows[:2].reshape(2 * D // (2 * DH), 2 * DH)
    late_rows = jnp.broadcast_to(late_rows[None], (lanes,) + late_rows.shape)
    head_grads = lax.all_to_all(
        jnp.concatenate([head_grads, late_rows], axis=1), "seq", 0, 0, tiled=True
    ).astype(f32)
    head_grads, one_other = lax.optimization_barrier((head_grads, one_other))
    one_grad = head_total(one_part, one_other)
    late_rows = axis_sum(jnp.sum(head_grads[:, width + width // 2 :], axis=0).reshape(2, D), "head")
    head_grads = head_grads[:, : width + width // 2]
    head_grads = jnp.sum(
        head_grads.reshape(heads, share, width + width // 2, 2 * DH), axis=1
    )
    kv_owned = head_grads[:, :width].reshape(heads, width, 2, DH).transpose(2, 1, 0, 3)
    q_owned = jnp.concatenate([head_grads[:, width:, :DH], head_grads[:, width:, DH:]], axis=1)
    qkv_grad = jnp.concatenate(
        [q_owned.transpose(1, 0, 2).reshape(1, width, feat), kv_owned.reshape(2, width, feat)], axis=0
    )

    layer_output = lax.dot_general(result, place, back, preferred_element_type=f32).astype(bf16)
    input_grad = exact(mid_grad, place.astype(f32), back) + exact(
        norm_back(one_grad, unit_one, scale_one, vec_near[0]), place_near.astype(f32), back
    )
    bias_rows = early_rows[3:]
    step = 1
    while step < head_groups:
        other = xor_permute(bias_rows, "head", step)
        high = (head_index & step) != 0
        bias_rows = jnp.where(
            high,
            jnp.concatenate([other, bias_rows], axis=0),
            jnp.concatenate([bias_rows, other], axis=0),
        )
        step *= 2
    vec_grad = jnp.concatenate([late_rows, early_rows[:3], bias_rows], axis=0)
    up_grad = rest_owned[:, :units]
    down_grad = rest_owned[:, units : 2 * units].T
    proj_grad = rest_owned[:, 2 * units :].T
    qkv_new, qkv_first_new, qkv_second_new = adam_step(
        qkv_weight, qkv_grad, qkv_first, qkv_second, rate_qkv
    )
    proj_new, proj_first_new, proj_second_new = adam_step(
        proj_weight, proj_grad, proj_first, proj_second, rate_proj
    )
    up_new, up_first_new, up_second_new = adam_step(up_weight, up_grad, up_first, up_second, rate_up)
    down_new, down_first_new, down_second_new = adam_step(
        down_weight, down_grad, down_first, down_second, rate_down
    )
    vec_new, vec_first_new, vec_second_new = adam_step(
        vec_params, vec_grad, vec_first, vec_second, rate_vector
    )
    return (
        layer_output.reshape(slots, BLOCK, D),
        input_grad.reshape(slots, BLOCK, D),
        qkv_new,
        qkv_first_new,
        qkv_second_new,
        qkv_new.astype(bf16),
        proj_new,
        proj_first_new,
        proj_second_new,
        proj_new.astype(bf16),
        up_new,
        up_first_new,
        up_second_new,
        up_new.astype(bf16),
        down_new,
        down_first_new,
        down_second_new,
        down_new.astype(bf16),
        vec_new,
        vec_first_new,
        vec_second_new,
    )


def solution(mesh):
    rows_by_seq = P(None, "seq", None)
    cols = P("head", "seq")
    ups = P("seq", "head")
    qkvs = P(None, "seq", "head")
    placed = (
        (rows_by_seq, rows_by_seq, P(None, "seq", "head", None), P(), P(), P())
        + (qkvs,) * 3
        + (cols,) * 3
        + (ups,) * 3
        + (cols,) * 3
        + (P(),) * 3
    )
    return jax.shard_map(
        body,
        mesh=mesh,
        in_specs=placed,
        out_specs=(rows_by_seq, rows_by_seq)
        + (qkvs,) * 4
        + (cols,) * 4
        + (ups,) * 4
        + (cols,) * 4
        + (P(),) * 3,
        check_vma=False,
    )
```

time: 394 us -> 350 us (0.89)
  waiting for transfers between devices: 142 us -> 89.1 us
  matrix products: 63.4 us -> 33.2 us
  blocking collectives: 0 us -> 25.5 us
  local copies, waits for them, and re-layouts: 26.2 us -> 44.1 us
  Pallas kernels: 29.7 us -> 35.5 us
  other arithmetic: 33.7 us -> 28.4 us
    ppermute x38 -> x22, waiting for transfers between devices: 101 us -> 63.5 us  [xor_permute(): return lax.ppermute(value, axis, [(i, i ^ mask) for i in range(count)])]
    all_to_all x0 -> x1, blocking collectives: none -> 25.5 us  [body(): ctx_pairs = lax.all_to_all(ctx_pairs, 'seq', 0, 0, tiled=True)]
    dot_general x22 -> x7, matrix products: 43.5 us -> 18.2 us  [dot(): lax.dot_general(lhs, rhs, (((lhs_dim,), (rhs_dim,)), ((), ())), preferred...]
    unnamed x104 -> x167, local copies, waits for them, and re-layouts: 9.66 us -> 27.1 us
    ppermute x38 -> x22, starting transfers between devices: 48 us -> 31.4 us  [xor_permute(): return lax.ppermute(value, axis, [(i, i ^ mask) for i in range(count)])]
    all_to_all x4, waiting for transfers between devices: 41.5 us -> 25.5 us  [the longest x1 25.5 us: body(): received = lax.all_to_all(message, 'seq', 0, 0, tiled=True)]
    all_to_all x4, starting transfers between devices: 21.2 us -> 35.7 us  [the longest x1 16.9 us: body(): returned = lax.all_to_all(message, 'seq', 0, 0, tiled=True)]
    concatenate x6 -> x2, other arithmetic: 10.8 us -> 1.74 us  [the longest x1 0.88 us: body(): jnp.concatenate([head_grads, late_rows], axis=1)]
  transfers between devices with their start and end apart: 45 -> 30, of which waited for: 21 -> 14; matrix products, arithmetic and copies ran while one was open for 23% -> 22% of each run, Pallas kernels for 8% -> 10%
where the time goes in v3:
time: 350 us; the launch traced here: 343 us
  waiting for transfers between devices  89.1 us (25%)
  starting transfers between devices  72.1 us (21%)
  local copies, waits for them, and re-layouts  44.1 us (13%)
  Pallas kernels  35.5 us (10%)
  matrix products  33.2 us (9%)
  other arithmetic  28.4 us (8%)
  blocking collectives  25.5 us (7%)
  between operations  15.2 us (4%)
    ppermute x22, waiting for transfers between devices, xor_permute(): return lax.ppermute(value, axis, [(i, i ^ mask) for i in range(count)])  63.5 us
    ppermute x22, starting transfers between devices, xor_permute(): return lax.ppermute(value, axis, [(i, i ^ mask) for i in range(count)])  31.4 us
    unnamed x167, local copies, waits for them, and re-layouts  27.1 us
    all_to_all x1, blocking collectives, body(): ctx_pairs = lax.all_to_all(ctx_pairs, 'seq', 0, 0, tiled=True)  25.5 us
    all_to_all x1, waiting for transfers between devices, body(): received = lax.all_to_all(message, 'seq', 0, 0, tiled=True)  25.5 us
    dot_general x7, matrix products, dot(): lax.dot_general(lhs, rhs, (((lhs_dim,), (rhs_dim,)), ((), ())), preferred...  18.2 us
    all_to_all x1, starting transfers between devices, body(): returned = lax.all_to_all(message, 'seq', 0, 0, tiled=True)  16.9 us
    pallas_call x1, Pallas kernels, body(): call(attend_back_kernel, (array(pairs_shape), array((back_shapes[0], 2 *...  7.31 us
  transfers between devices with their start and end apart: 30, of which 14 were waited for; matrix products, arithmetic and copies ran while one was open for 22% of the time, Pallas kernels for 10%

profile of v3, /device:TPU:0, one launch (start us, length us, event | category | flops | bytes accessed | tf_op | source)
XLA Modules:
  0.0 343.2 jit_solution(12660602385048966392)
XLA Ops:
  12.0 3.0 collective-permute-start
  15.1 2.6 collective-permute-start.1
  17.7 1.7 collective-permute-start.3
  20.1 5.0 %all-to-all-start = ((s32[16,1,12]{2,1,0:T(1,128)}), s32[16,1,12]{2,1,0:T(1,128)S(1)}, u32[]{:S(2)}, u32[]{:S(2)}) async-start(s32[16,1,12]{2,1,0:T(1,128)} %bitcast.14), calls=%async_computation | async-start | bytes 16384 | tf_op jit(solution)/shard_map/all_to_all | solution.py:511
  27.0 1.9 fusion.125
  28.9 1.6 copy.178
  34.6 1.5 fusion.47
  38.3 1.9 collective-permute-start.4
  40.3 1.9 collective-permute-start.6
  46.2 4.2 %collective-permute-done.5 = bf16[64,1536]{1,0:T(8,128)(2,1)S(1)} collective-permute-done((bf16[64,1536]{1,0:T(8,128)(2,1)}, bf16[64,1536]{1,0:T(8,128)(2,1)S(1)}, u32[]{:S(2)}, u32[]{:S(2)}) %collective-permute-start.5) | collective-permute-done | bytes 196640 | tf_op jit(solution)/shard_map/ppermute | solution.py:81
  50.4 3.7 %collective-permute-done.6 = bf16[64,1536]{1,0:T(8,128)(2,1)S(1)} collective-permute-done((bf16[64,1536]{1,0:T(8,128)(2,1)}, bf16[64,1536]{1,0:T(8,128)(2,1)S(1)}, u32[]{:S(2)}, u32[]{:S(2)}) %collective-permute-start.6) | collective-permute-done | bytes 196640 | tf_op jit(solution)/shard_map/ppermute | solution.py:81
  55.0 1.5 fusion.48
  57.4 1.5 add_convert_fusion.2
  60.3 2.8 shard_map.373
  64.0 5.9 %all-to-all-start.1 = ((bf16[16,192,128]{2,1,0:T(8,128)(2,1)}), bf16[16,192,128]{2,1,0:T(8,128)(2,1)S(1)}, u32[]{:S(2)}, u32[]{:S(2)}) async-start(bf16[16,192,128]{2,1,0:T(8,128)(2,1)} %copy-done.7), calls=%async_computation.1 | async-start | bytes 1572864 | tf_op jit(solution)/shard_map/all_to_all | solution.py:565
  75.8 25.5 %all-to-all-done.1.record_ref.refs_0_ = bf16[16,192,128]{2,1,0:T(8,128)(2,1)S(1)} async-done(((bf16[16,192,128]{2,1,0:T(8,128)(2,1)}), bf16[16,192,128]{2,1,0:T(8,128)(2,1)S(1)}, u32[]{:S(2)}, u32[]{:S(2)}) %all-to-all-start.1) | async-done | bytes 786464 | tf_op jit(solution)/shard_map/all_to_all | solution.py:565
  101.4 2.2 collective-permute-done.8.refs_1_
  105.7 4.6 %shard_map.374 = (bf16[16,64,128]{2,1,0:T(8,128)(2,1)S(1)}, bf16[16,2,64,512]{3,2,1,0:T(8,128)(2,1)S(1)}) custom-call(s32[32,8]{1,0:T(8,128)S(1)} %fusion.77.off_ref, bf16[16,192,128]{2,1,0:T(8,128)(2,1)S(1)} %all-to-all-done.1.record_ref.refs_0_, bf16[16,192,128]{2,1,0:T(8,128)(2,1)S(1)} %all-to-all-done.1.record_ref.refs_0_, ...), custom_call_target="tpu_custom_call" | custom-call | tf_op jit(solution)/shard_map/pallas_call | solution.py:634
  110.3 1.4 copy-done.9
  111.7 25.5 %all_to_all.34.pairs_ref = bf16[16,64,128]{2,1,0:T(8,128)(2,1)} all-to-all(bf16[16,64,128]{2,1,0:T(8,128)(2,1)S(1)} %get-tuple-element.67), channel_id=1, replica_groups=mesh['seq'=16,'head'=2] {'seq'}, dimensions={0} | all-to-all | bytes 524288 | tf_op jit(solution)/shard_map/all_to_all | solution.py:640
  138.2 2.5 shard_map.375
  141.4 1.6 collective-permute-start.9
  143.1 2.2 fusion.39
  145.3 10.4 %collective-permute-done.9 = bf16[256,1024]{1,0:T(8,128)(2,1)} collective-permute-done((bf16[256,1024]{1,0:T(8,128)(2,1)}, bf16[256,1024]{1,0:T(8,128)(2,1)}, u32[]{:S(2)}, u32[]{:S(2)}) %collective-permute-start.9) | collective-permute-done | bytes 524320 | tf_op jit(solution)/shard_map/ppermute | solution.py:81
  155.7 1.5 fusion.119
  157.7 4.6 %multiply_convert_fusion = (bf16[256,2048]{1,0:T(8,128)(2,1)S(1)}, f32[256,2048]{1,0:T(8,128)S(1)}) fusion(f32[2048]{0:T(1024)S(1)} %dynamic_slice.11, bf16[256,1024]{1,0:T(8,128)(2,1)S(1)} %add_convert_fusion.1.lhs_a, bf16[1024,4608]{1,0:T(8,128)(2,1)} %all-gather.3.cloned.1.call-done.proj_ref), kind=kOutput, calls=%fused_computation.29 | convolution fusion | flops 1078984704 | bytes 7872512 | tf_op jit(solution)/shard_map/dot_general | solution.py:43
  162.4 2.5 fusion.120
  166.2 1.6 collective-permute-start.10
  167.8 6.8 %shard_map.376.whole_ref = bf16[1024,4608]{1,0:T(8,128)(2,1)} custom-call(bf16[256,1024]{1,0:T(8,128)(2,1)S(1)} %add_convert_fusion.1.lhs_a, bf16[256,2048]{1,0:T(8,128)(2,1)S(1)} %get-tuple-element.134.rhs_a, bf16[256,1024]{1,0:T(8,128)(2,1)S(1)} %bitcast.113, bf16[256,2048]{1,0:T(8,128)(2,1)S(1)} %get-tuple-element.76.rhs_b), custom_call_target="tpu_custom_call" | custom-call | flops 4294967296 | bytes 18874368 | tf_op jit(solution)/shard_map/pallas_call | solution.py:444
  174.6 4.7 %collective-permute-done.10 = bf16[256,1024]{1,0:T(8,128)(2,1)S(1)} collective-permute-done((bf16[256,1024]{1,0:T(8,128)(2,1)S(1)}, bf16[256,1024]{1,0:T(8,128)(2,1)S(1)}, u32[]{:S(2)}, u32[]{:S(2)}) %collective-permute-start.10) | collective-permute-done | bytes 524320 | tf_op jit(solution)/shard_map/ppermute | solution.py:81
  179.9 1.5 fusion.118
  181.4 1.5 shard_map.378
  184.8 1.7 shard_map.377
  187.2 6.5 %all-to-all-start.3 = ((bf16[16,64,128]{2,1,0:T(8,128)(2,1)}), bf16[16,64,128]{2,1,0:T(8,128)(2,1)}, u32[]{:S(2)}, u32[]{:S(2)}) async-start(bf16[16,64,128]{2,1,0:T(8,128)(2,1)} %copy-done.15), calls=%async_computation.3 | async-start | bytes 524288 | tf_op jit(solution)/shard_map/all_to_all | solution.py:678
  194.8 1.5 collective-permute-start.11
  197.0 6.4 %collective-permute-done.11.refs_1_ = bf16[256,512]{1,0:T(8,128)(2,1)S(1)} collective-permute-done((bf16[256,512]{1,0:T(8,128)(2,1)S(1)}, bf16[256,512]{1,0:T(8,128)(2,1)S(1)}, u32[]{:S(2)}, u32[]{:S(2)}) %collective-permute-start.11) | collective-permute-done | bytes 262176 | tf_op jit(solution)/shard_map/ppermute | solution.py:81
  205.3 1.8 copy-done.10
  207.1 7.3 %shard_map.379 = (bf16[16,64,128]{2,1,0:T(8,128)(2,1)S(1)}, f32[2048,128]{1,0:T(8,128)S(1)}, bf16[2048,128]{1,0:T(8,128)(2,1)}) custom-call(s32[32,8]{1,0:T(8,128)S(1)} %fusion.77.off_ref, bf16[16,192,128]{2,1,0:T(8,128)(2,1)S(1)} %all-to-all-done.1.record_ref.refs_0_, bf16[16,192,128]{2,1,0:T(8,128)(2,1)S(1)} %all-to-all-done.1.record_ref.refs_0_, ...), custom_call_target="tpu_custom_call" | custom-call | tf_op jit(solution)/shard_map/pallas_call | solution.py:692
  216.1 3.0 constant_dynamic-slice_fusion
  219.2 1.4 collective-permute-start.13
  220.6 1.4 shard_map.380
  223.9 16.9 %all-to-all-start.4 = ((bf16[16,192,128]{2,1,0:T(8,128)(2,1)}), bf16[16,192,128]{2,1,0:T(8,128)(2,1)S(1)}, u32[]{:S(2)}, u32[]{:S(2)}) async-start(bf16[16,192,128]{2,1,0:T(8,128)(2,1)} %copy-done.19), calls=%async_computation.4 | async-start | bytes 1572864 | tf_op jit(solution)/shard_map/all_to_all | solution.py:716
  240.8 4.7 %fusion.41 = bf16[256,1024]{1,0:T(8,128)(2,1)} fusion(bf16[256,2048]{1,0:T(8,128)(2,1)} %copy-done.28, bf16[1024,4608]{1,0:T(8,128)(2,1)} %all-gather.3.cloned.1.call-done.proj_ref), kind=kOutput, calls=%fused_computation.43 | convolution fusion | flops 1074003968 | bytes 5767168 | tf_op jit(solution)/shard_map/dot_general | solution.py:43
  246.0 1.7 fusion.2.place_ref
  247.8 2.0 fusion.5
  249.8 12.5 %collective-permute-done.13.refs_3_ = bf16[1792,512]{1,0:T(8,128)(2,1)} collective-permute-done((bf16[1792,512]{1,0:T(8,128)(2,1)}, bf16[1792,512]{1,0:T(8,128)(2,1)}, u32[]{:S(2)}, u32[]{:S(2)}) %collective-permute-start.13) | collective-permute-done | bytes 1835040 | tf_op jit(solution)/shard_map/ppermute | solution.py:81
  265.4 3.3 shard_map.381
  269.5 3.6 %collective-permute-done.14 = bf16[256,1024]{1,0:T(8,128)(2,1)} collective-permute-done((bf16[256,1024]{1,0:T(8,128)(2,1)}, bf16[256,1024]{1,0:T(8,128)(2,1)}, u32[]{:S(2)}, u32[]{:S(2)}) %collective-permute-start.14) | collective-permute-done | bytes 524320 | tf_op jit(solution)/shard_map/ppermute | solution.py:81
  273.2 3.6 %shard_map.382 = (bf16[256,1024]{1,0:T(8,128)(2,1)S(1)}, bf16[16,1024]{1,0:T(8,128)(2,1)S(1)}) custom-call(bf16[16,192,128]{2,1,0:T(8,128)(2,1)S(1)} %all-to-all-done.4.msg_ref, bf16[512,1536]{1,0:T(8,128)(2,1)S(1)} %constant_dynamic-update-slice_fusion.near_ref, bf16[512,1536]{1,0:T(8,128)(2,1)} %collective-permute-done.7.far_ref, ...), custom_call_target="tpu_custom_call" | custom-call | tf_op jit(solution)/shard_map/pallas_call | solution.py:742
  280.6 6.3 %all-to-all-start.5 = ((bf16[16,112,128]{2,1,0:T(8,128)(2,1)}), bf16[16,112,128]{2,1,0:T(8,128)(2,1)S(1)}, u32[]{:S(2)}, u32[]{:S(2)}) async-start(bf16[16,112,128]{2,1,0:T(8,128)(2,1)} %pad_maximum_fusion.1), calls=%async_computation.5 | async-start | bytes 917504 | tf_op jit(solution)/shard_map/all_to_all | solution.py:754
  286.9 1.8 collective-permute-start.15
  289.9 1.9 collective-permute-start.18
  291.9 3.0 collective-permute-done.18
  294.9 2.1 collective-permute-start.19
  296.9 3.9 %collective-permute-done.19 = f32[5,1024]{1,0:T(8,128)S(1)} collective-permute-done((f32[5,1024]{1,0:T(8,128)S(1)}, f32[5,1024]{1,0:T(8,128)S(1)}, u32[]{:S(2)}, u32[]{:S(2)}) %collective-permute-start.19) | collective-permute-done | bytes 20512 | tf_op jit(solution)/shard_map/ppermute | solution.py:81
  300.8 4.7 %collective-permute-start.20 = (f32[5,1024]{1,0:T(8,128)S(1)}, f32[5,1024]{1,0:T(8,128)S(1)}, u32[]{:S(2)}, u32[]{:S(2)}) collective-permute-start(f32[5,1024]{1,0:T(8,128)S(1)} %add.599), channel_id=1, source_target_pairs={{0,16},{2,18},{4,20},{6,22},{8,24},{10,26},{12,28},{14,30},{16,0},... | collective-permute-start | bytes 61448 | tf_op jit(solution)/shard_map/ppermute | solution.py:81
  305.5 7.7 %collective-permute-done.20 = f32[5,1024]{1,0:T(8,128)S(1)} collective-permute-done((f32[5,1024]{1,0:T(8,128)S(1)}, f32[5,1024]{1,0:T(8,128)S(1)}, u32[]{:S(2)}, u32[]{:S(2)}) %collective-permute-start.20) | collective-permute-done | bytes 20512 | tf_op jit(solution)/shard_map/ppermute | solution.py:81
  313.3 2.2 collective-permute-start.21
  315.4 3.2 fusion.40
  320.6 1.4 fusion.56
  322.1 3.7 %fusion = f32[256,1024]{1,0:T(8,128)S(1)} fusion(s32[1024]{0:T(1024)S(1)} %copy-done.59, f32[256,1024]{1,0:T(8,128)S(1)} %get-tuple-element.132.unit_ref, bf16[256,1024]{1,0:T(8,128)(2,1)} %collective-permute-done.15, bf16[256,1024]{1,0:T(8,128)(2,1)S(1)} %copy-done.21, f32[256]{0:T(256)S(1)} %broadcast_multiply_fusion, ...), kind=kOutput, calls=%fused_computation.1 | convolution fusion | flops 3224371200 | bytes 3156992 | tf_op jit(solution)/shard_map/dot_general | solution.py:771
  325.8 3.2 fusion.38
  332.3 1.5 fusion.110
  334.2 1.5 fusion.112
  (316 shorter events, 59.4 us)
Async XLA Ops:
  7.2 18.1 %copy-start = (bf16[4,64,1024]{2,1,0:T(8,128)(2,1)S(1)}, bf16[4,64,1024]{2,1,0:T(8,128)(2,1)}, u32[]{:S(2)}) copy-start(bf16[4,64,1024]{2,1,0:T(8,128)(2,1)} %param.22) | copy-start | bytes 1572868
  7.2 4.1 %copy-start.37 = (f32[3,64,512]{2,1,0:T(8,128)S(1)}, f32[3,64,512]{2,1,0:T(8,128)}, u32[]{:S(2)}) copy-start(f32[3,64,512]{2,1,0:T(8,128)} %param.28) | copy-start | bytes 1179652
  7.2 12.2 %copy-start.60 = (s32[4,1,8,3]{2,1,3,0:T(1,128)S(1)}, s32[4,1,8,3]{2,1,3,0:T(1,128)}, u32[]{:S(2)}) copy-start(s32[4,1,8,3]{2,1,3,0:T(1,128)} %param.24) | copy-start | bytes 1156
  7.2 130.0 %all-gather.3.cloned.1.call-start = ((), (), s32[]{:S(2)}) async-start(), calls=%async_computation.7 | async-start | bytes 10027008 | tf_op jit(solution)/shard_map/all_gather | solution.py:518
  8.4 16.7 %copy-start.70 = (s32[16]{0:T(128)S(1)}, s32[16]{0:T(128)}, u32[]{:S(2)}) copy-start(s32[16]{0:T(128)} %param.27) | copy-start | bytes 196
  12.0 26.2 %collective-permute-start = (bf16[64,1536]{1,0:T(8,128)(2,1)}, bf16[64,1536]{1,0:T(8,128)(2,1)}, u32[]{:S(2)}, u32[]{:S(2)}) collective-permute-start(bf16[64,1536]{1,0:T(8,128)(2,1)} %bitcast.48), channel_id=1, source_target_pairs={{0,8},{2,10},{4,12},{6,14},{8,0},{10,2},{12,4},{14,6},{16,24},{18,... | collective-permute-start | bytes 589832 | tf_op jit(solution)/shard_map/ppermute | solution.py:81
  15.1 25.1 %collective-permute-start.1 = (bf16[64,1536]{1,0:T(8,128)(2,1)}, bf16[64,1536]{1,0:T(8,128)(2,1)}, u32[]{:S(2)}, u32[]{:S(2)}) collective-permute-start(bf16[64,1536]{1,0:T(8,128)(2,1)} %bitcast.48), channel_id=1, source_target_pairs={{0,16},{2,18},{4,20},{6,22},{8,24},{10,26},{12,28},{14,30},{16,0},... | collective-permute-start | bytes 589832 | tf_op jit(solution)/shard_map/ppermute | solution.py:81
  17.7 22.6 %collective-permute-start.2 = (bf16[64,1536]{1,0:T(8,128)(2,1)}, bf16[64,1536]{1,0:T(8,128)(2,1)}, u32[]{:S(2)}, u32[]{:S(2)}) collective-permute-start(bf16[64,1536]{1,0:T(8,128)(2,1)} %bitcast.48), channel_id=1, source_target_pairs={{0,24},{2,26},{4,28},{6,30},{8,16},{10,18},{12,20},{14,22},{16,8},... | collective-permute-start | bytes 589832 | tf_op jit(solution)/shard_map/ppermute | solution.py:81
  17.7 27.4 %collective-permute-start.3 = (bf16[64,1536]{1,0:T(8,128)(2,1)}, bf16[64,1536]{1,0:T(8,128)(2,1)}, u32[]{:S(2)}, u32[]{:S(2)}) collective-permute-start(bf16[64,1536]{1,0:T(8,128)(2,1)} %bitcast.48), channel_id=1, source_target_pairs={{0,4},{2,6},{4,0},{6,2},{8,12},{10,14},{12,8},{14,10},{16,20},{18,... | collective-permute-start | bytes 589832 | tf_op jit(solution)/shard_map/ppermute | solution.py:81
  20.1 40.1 %all-to-all-start = ((s32[16,1,12]{2,1,0:T(1,128)}), s32[16,1,12]{2,1,0:T(1,128)S(1)}, u32[]{:S(2)}, u32[]{:S(2)}) async-start(s32[16,1,12]{2,1,0:T(1,128)} %bitcast.14), calls=%async_computation | async-start | bytes 16384 | tf_op jit(solution)/shard_map/all_to_all | solution.py:511
  25.2 9.4 %copy-start.64 = (s32[1024]{0:T(1024)}, s32[1024]{0:T(1024)S(1)}, u32[]{:S(2)}) copy-start(s32[1024]{0:T(1024)S(1)} %get-tuple-element.148) | copy-start | bytes 12292
  26.6 6.3 %copy-start.31 = (f32[1024,256]{0,1:T(8,128)}, f32[1024,256]{0,1:T(8,128)S(1)}, u32[]{:S(2)}) copy-start(f32[1024,256]{0,1:T(8,128)S(1)} %copy.177) | copy-start | bytes 3145732
  27.0 28.0 %copy-start.58 = (s32[1024]{0:T(1024)}, s32[1024]{0:T(1024)S(1)}, u32[]{:S(2)}) copy-start(s32[1024]{0:T(1024)S(1)} %fusion.98) | copy-start | bytes 12292
  30.5 5.6 %copy-start.33 = (f32[1024,256]{0,1:T(8,128)}, f32[1024,256]{0,1:T(8,128)S(1)}, u32[]{:S(2)}) copy-start(f32[1024,256]{0,1:T(8,128)S(1)} %copy.178) | copy-start | bytes 3145732
  30.5 4.1 %copy-start.49 = (f32[9,1024]{1,0:T(8,128)S(1)}, f32[9,1024]{1,0:T(8,128)}, u32[]{:S(2)}) copy-start(f32[9,1024]{1,0:T(8,128)} %param.40) | copy-start | bytes 110596
  32.1 5.7 %copy-start.72 = (s32[32]{0:T(128)S(1)}, s32[32]{0:T(128)}, u32[]{:S(2)}) copy-start(s32[32]{0:T(128)} %reduce_sum.233) | copy-start | bytes 388
  34.1 23.3 %copy-start.62 = (f32[256]{0:T(256)}, f32[256]{0:T(256)S(1)}, u32[]{:S(2)}) copy-start(f32[256]{0:T(256)S(1)} %add_rsqrt_fusion.2) | copy-start | bytes 3076
  34.6 35.3 %copy-start.68 = (s32[32,1]{0,1:T(1,128)}, s32[32,1]{0,1:T(1,128)S(1)}, u32[]{:S(2)}) copy-start(s32[32,1]{0,1:T(1,128)S(1)} %get-tuple-element.128) | copy-start | bytes 388
  36.7 19.8 %copy-start.34 = (f32[256,1024]{1,0:T(8,128)S(1)}, f32[256,1024]{1,0:T(8,128)}, u32[]{:S(2)}) copy-start(f32[256,1024]{1,0:T(8,128)} %get-tuple-element.130) | copy-start | bytes 3145732
  38.3 7.9 %collective-permute-start.4 = (bf16[64,1536]{1,0:T(8,128)(2,1)}, bf16[64,1536]{1,0:T(8,128)(2,1)S(1)}, u32[]{:S(2)}, u32[]{:S(2)}) collective-permute-start(bf16[64,1536]{1,0:T(8,128)(2,1)} %collective-permute-done), channel_id=1, source_target_pairs={{0,4},{2,6},{4,0},{6,2},{8,12},{10,14},{12,8},{14,10},{16,20},{18,... | collective-permute-start | bytes 589832 | tf_op jit(solution)/shard_map/ppermute | solution.py:81
  40.2 10.2 %collective-permute-start.5 = (bf16[64,1536]{1,0:T(8,128)(2,1)}, bf16[64,1536]{1,0:T(8,128)(2,1)S(1)}, u32[]{:S(2)}, u32[]{:S(2)}) collective-permute-start(bf16[64,1536]{1,0:T(8,128)(2,1)} %collective-permute-done.1), channel_id=1, source_target_pairs={{0,4},{2,6},{4,0},{6,2},{8,12},{10,14},{12,8},{14,10},{16,20},{18,... | collective-permute-start | bytes 589832 | tf_op jit(solution)/shard_map/ppermute | solution.py:81
  40.3 13.9 %collective-permute-start.6 = (bf16[64,1536]{1,0:T(8,128)(2,1)}, bf16[64,1536]{1,0:T(8,128)(2,1)S(1)}, u32[]{:S(2)}, u32[]{:S(2)}) collective-permute-start(bf16[64,1536]{1,0:T(8,128)(2,1)} %collective-permute-done.2), channel_id=1, source_target_pairs={{0,4},{2,6},{4,0},{6,2},{8,12},{10,14},{12,8},{14,10},{16,20},{18,... | collective-permute-start | bytes 589832 | tf_op jit(solution)/shard_map/ppermute | solution.py:81
  54.2 6.1 %collective-permute-start.7 = (bf16[512,1536]{1,0:T(8,128)(2,1)S(1)}, bf16[512,1536]{1,0:T(8,128)(2,1)}, u32[]{:S(2)}, u32[]{:S(2)}) collective-permute-start(bf16[512,1536]{1,0:T(8,128)(2,1)S(1)} %constant_dynamic-update-slice_fusion.near_ref), channel_id=1, source_target_pairs={{0,2},{2,0},{4,6},{6,4},{8,10},{10,8},{12,14},{14,12},{16,18},{18,... | collective-permute-start | bytes 4718600 | tf_op jit(solution)/shard_map/ppermute | solution.py:81
  56.5 6.6 %copy-start.55 = (f32[1,1024]{1,0:T(1,128)}, f32[1,1024]{1,0:T(1,128)S(1)}, u32[]{:S(2)}) copy-start(f32[1,1024]{1,0:T(1,128)S(1)} %get-tuple-element.145) | copy-start | bytes 12292
  60.3 11.0 %copy-start.74 = (pred[16,2]{0,1:T(4,128)(4,1)S(1)}, pred[16,2]{0,1:T(4,128)(4,1)}, u32[]{:S(2)}) copy-start(pred[16,2]{0,1:T(4,128)(4,1)} %broadcast_compare_fusion) | copy-start | bytes 100
  64.0 37.4 %all-to-all-start.1 = ((bf16[16,192,128]{2,1,0:T(8,128)(2,1)}), bf16[16,192,128]{2,1,0:T(8,128)(2,1)S(1)}, u32[]{:S(2)}, u32[]{:S(2)}) async-start(bf16[16,192,128]{2,1,0:T(8,128)(2,1)} %copy-done.7), calls=%async_computation.1 | async-start | bytes 1572864 | tf_op jit(solution)/shard_map/all_to_all | solution.py:565
  69.9 123.9 %all-gather.5.cloned.1.call-start = ((), (), s32[]{:S(2)}) async-start(), calls=%async_computation.8 | async-start | bytes 4456448 | tf_op jit(solution)/shard_map/all_gather | solution.py:629
  101.3 2.3 collective-permute-start.8
  104.5 226.6 %reduce-scatter.2.cloned.1.call-start = ((), (), s32[]{:S(2)}) async-start(), calls=%async_computation.9 | async-start | bytes 10027008 | tf_op jit(solution)/shard_map/reduce_scatter | solution.py:677
  138.2 4.8 %copy-start.50 = (f32[9,1024]{1,0:T(8,128)S(1)}, f32[9,1024]{1,0:T(8,128)}, u32[]{:S(2)}) copy-start(f32[9,1024]{1,0:T(8,128)} %param.40) | copy-start | bytes 110596
  138.2 4.9 %copy-start.65 = (s32[1024]{0:T(1024)S(1)}, s32[1024]{0:T(1024)}, u32[]{:S(2)}) copy-start(s32[1024]{0:T(1024)} %copy-done.64) | copy-start | bytes 12292
  141.4 14.3 %collective-permute-start.9 = (bf16[256,1024]{1,0:T(8,128)(2,1)}, bf16[256,1024]{1,0:T(8,128)(2,1)}, u32[]{:S(2)}, u32[]{:S(2)}) collective-permute-start(bf16[256,1024]{1,0:T(8,128)(2,1)} %get-tuple-element.68), channel_id=1, source_target_pairs={{0,1},{1,0},{2,3},{3,2},{4,5},{5,4},{6,7},{7,6},{8,9},{9,8},{10,11... | collective-permute-start | bytes 1572872 | tf_op jit(solution)/shard_map/ppermute | solution.py:81
  143.0 12.7 %copy-start.32 = (f32[1024,256]{0,1:T(8,128)S(1)}, f32[1024,256]{0,1:T(8,128)}, u32[]{:S(2)}) copy-start(f32[1024,256]{0,1:T(8,128)} %copy-done.31) | copy-start | bytes 3145732
  143.0 19.3 %slice-start = ((s8[9437184]{0:T(1024)(128)(4,1)}), s8[4194304]{0:T(1024)(128)(4,1)S(1)}, s32[]{:S(2)}) async-start(s8[9437184]{0:T(1024)(128)(4,1)} %bitcast.115), calls=%async_computation.10 | async-start | bytes 8388608
  145.3 12.2 %copy-start.52 = (f32[1,1024]{1,0:T(1,128)S(1)}, f32[1,1024]{1,0:T(1,128)}, u32[]{:S(2)}) copy-start(f32[1,1024]{1,0:T(1,128)} %get-tuple-element.142) | copy-start | bytes 12292
  145.3 12.1 %copy-start.57 = (f32[1,1024]{1,0:T(1,128)S(1)}, f32[1,1024]{1,0:T(1,128)}, u32[]{:S(2)}) copy-start(f32[1,1024]{1,0:T(1,128)} %get-tuple-element.141) | copy-start | bytes 12292
  157.1 22.8 %copy-start.29 = (f32[256,1024]{1,0:T(8,128)}, f32[256,1024]{1,0:T(8,128)S(1)}, u32[]{:S(2)}) copy-start(f32[256,1024]{1,0:T(8,128)S(1)} %get-tuple-element.126) | copy-start | bytes 3145732
  157.2 5.2 %slice-start.1 = ((s8[9437184]{0:T(1024)(128)(4,1)}), s8[4194304]{0:T(1024)(128)(4,1)S(1)}, s32[]{:S(2)}) async-start(s8[9437184]{0:T(1024)(128)(4,1)} %bitcast.115), calls=%async_computation.11 | async-start | bytes 8388608
  157.7 4.7 %slice-start.2 = ((s8[9437184]{0:T(1024)(128)(4,1)}), s8[1048576]{0:T(1024)(128)(4,1)S(1)}, s32[]{:S(2)}) async-start(s8[9437184]{0:T(1024)(128)(4,1)} %bitcast.115), calls=%async_computation.12 | async-start | bytes 2097152
  162.4 5.4 %copy-start.28 = (bf16[256,2048]{1,0:T(8,128)(2,1)}, bf16[256,2048]{1,0:T(8,128)(2,1)S(1)}, u32[]{:S(2)}) copy-start(bf16[256,2048]{1,0:T(8,128)(2,1)S(1)} %get-tuple-element.76.rhs_b) | copy-start | bytes 3145732
  166.2 13.1 %collective-permute-start.10 = (bf16[256,1024]{1,0:T(8,128)(2,1)S(1)}, bf16[256,1024]{1,0:T(8,128)(2,1)S(1)}, u32[]{:S(2)}, u32[]{:S(2)}) collective-permute-start(bf16[256,1024]{1,0:T(8,128)(2,1)S(1)} %fusion.44), channel_id=1, source_target_pairs={{0,1},{1,0},{2,3},{3,2},{4,5},{5,4},{6,7},{7,6},{8,9},{9,8},{10,11... | collective-permute-start | bytes 1572872 | tf_op jit(solution)/shard_map/ppermute | solution.py:81
  187.2 16.9 %all-to-all-start.3 = ((bf16[16,64,128]{2,1,0:T(8,128)(2,1)}), bf16[16,64,128]{2,1,0:T(8,128)(2,1)}, u32[]{:S(2)}, u32[]{:S(2)}) async-start(bf16[16,64,128]{2,1,0:T(8,128)(2,1)} %copy-done.15), calls=%async_computation.3 | async-start | bytes 524288 | tf_op jit(solution)/shard_map/all_to_all | solution.py:678
  194.8 8.6 %collective-permute-start.11 = (bf16[256,512]{1,0:T(8,128)(2,1)S(1)}, bf16[256,512]{1,0:T(8,128)(2,1)S(1)}, u32[]{:S(2)}, u32[]{:S(2)}) collective-permute-start(bf16[256,512]{1,0:T(8,128)(2,1)S(1)} %bitcast.111), channel_id=1, source_target_pairs={{0,1},{1,0},{2,3},{3,2},{4,5},{5,4},{6,7},{7,6},{8,9},{9,8},{10,11... | collective-permute-start | bytes 786440 | tf_op jit(solution)/shard_map/ppermute | solution.py:81
  216.1 4.5 %copy-start.27 = (bf16[16,64,128]{2,1,0:T(8,128)(2,1)S(1)}, bf16[16,64,128]{2,1,0:T(8,128)(2,1)}, u32[]{:S(2)}) copy-start(bf16[16,64,128]{2,1,0:T(8,128)(2,1)} %copy-done.26) | copy-start | bytes 786436
  216.1 4.5 %collective-permute-start.12 = (bf16[2048,128]{1,0:T(8,128)(2,1)}, bf16[2048,128]{1,0:T(8,128)(2,1)S(1)}, u32[]{:S(2)}, u32[]{:S(2)}) collective-permute-start(bf16[2048,128]{1,0:T(8,128)(2,1)} %get-tuple-element.75), channel_id=1, source_target_pairs={{0,2},{2,0},{4,6},{6,4},{8,10},{10,8},{12,14},{14,12},{16,18},{18,... | collective-permute-start | bytes 1572872 | tf_op jit(solution)/shard_map/ppermute | solution.py:81
  216.1 4.5 %copy-start.14 = (f32[2048,128]{1,0:T(8,128)S(1)}, f32[2048,128]{1,0:T(8,128)}, u32[]{:S(2)}) copy-start(f32[2048,128]{1,0:T(8,128)} %copy-done.13) | copy-start | bytes 3145732
  219.2 43.1 %collective-permute-start.13 = (bf16[1792,512]{1,0:T(8,128)(2,1)}, bf16[1792,512]{1,0:T(8,128)(2,1)}, u32[]{:S(2)}, u32[]{:S(2)}) collective-permute-start(bf16[1792,512]{1,0:T(8,128)(2,1)} %bitcast.31.refs_2_), channel_id=1, source_target_pairs={{0,1},{1,0},{2,3},{3,2},{4,5},{5,4},{6,7},{7,6},{8,9},{9,8},{10,11... | collective-permute-start | bytes 5505032 | tf_op jit(solution)/shard_map/ppermute | solution.py:81
  223.9 49.3 %all-to-all-start.4 = ((bf16[16,192,128]{2,1,0:T(8,128)(2,1)}), bf16[16,192,128]{2,1,0:T(8,128)(2,1)S(1)}, u32[]{:S(2)}, u32[]{:S(2)}) async-start(bf16[16,192,128]{2,1,0:T(8,128)(2,1)} %copy-done.19), calls=%async_computation.4 | async-start | bytes 1572864 | tf_op jit(solution)/shard_map/all_to_all | solution.py:716
  240.8 5.2 %copy-start.59 = (s32[1024]{0:T(1024)S(1)}, s32[1024]{0:T(1024)}, u32[]{:S(2)}) copy-start(s32[1024]{0:T(1024)} %copy-done.58) | copy-start | bytes 12292
  245.5 27.7 %collective-permute-start.14 = (bf16[256,1024]{1,0:T(8,128)(2,1)}, bf16[256,1024]{1,0:T(8,128)(2,1)}, u32[]{:S(2)}, u32[]{:S(2)}) collective-permute-start(bf16[256,1024]{1,0:T(8,128)(2,1)} %fusion.41), channel_id=1, source_target_pairs={{0,1},{1,0},{2,3},{3,2},{4,5},{5,4},{6,7},{7,6},{8,9},{9,8},{10,11... | collective-permute-start | bytes 1572872 | tf_op jit(solution)/shard_map/ppermute | solution.py:81
  277.6 37.8 %copy-start.30 = (f32[256,1024]{1,0:T(8,128)S(1)}, f32[256,1024]{1,0:T(8,128)}, u32[]{:S(2)}) copy-start(f32[256,1024]{1,0:T(8,128)} %copy-done.29) | copy-start | bytes 3145732
  277.6 37.8 %copy-start.67 = (f32[1,1024]{1,0:T(1,128)S(1)}, f32[1,1024]{1,0:T(1,128)}, u32[]{:S(2)}) copy-start(f32[1,1024]{1,0:T(1,128)} %get-tuple-element.140) | copy-start | bytes 12292
  277.6 9.3 %copy-start.21 = (bf16[256,1024]{1,0:T(8,128)(2,1)S(1)}, bf16[256,1024]{1,0:T(8,128)(2,1)}, u32[]{:S(2)}) copy-start(bf16[256,1024]{1,0:T(8,128)(2,1)} %copy-done.20) | copy-start | bytes 1572868
  280.6 38.1 %all-to-all-start.5 = ((bf16[16,112,128]{2,1,0:T(8,128)(2,1)}), bf16[16,112,128]{2,1,0:T(8,128)(2,1)S(1)}, u32[]{:S(2)}, u32[]{:S(2)}) async-start(bf16[16,112,128]{2,1,0:T(8,128)(2,1)} %pad_maximum_fusion.1), calls=%async_computation.5 | async-start | bytes 917504 | tf_op jit(solution)/shard_map/all_to_all | solution.py:754
  286.9 31.9 %collective-permute-start.15 = (bf16[256,1024]{1,0:T(8,128)(2,1)S(1)}, bf16[256,1024]{1,0:T(8,128)(2,1)}, u32[]{:S(2)}, u32[]{:S(2)}) collective-permute-start(bf16[256,1024]{1,0:T(8,128)(2,1)S(1)} %copy-done.21), channel_id=1, source_target_pairs={{0,1},{1,0},{2,3},{3,2},{4,5},{5,4},{6,7},{7,6},{8,9},{9,8},{10,11... | collective-permute-start | bytes 1572872 | tf_op jit(solution)/shard_map/ppermute | solution.py:81
  288.7 1.2 collective-permute-start.17
  289.9 4.9 %collective-permute-start.18 = (f32[5,1024]{1,0:T(8,128)S(1)}, f32[5,1024]{1,0:T(8,128)S(1)}, u32[]{:S(2)}, u32[]{:S(2)}) collective-permute-start(f32[5,1024]{1,0:T(8,128)S(1)} %add.597), channel_id=1, source_target_pairs={{0,4},{2,6},{4,0},{6,2},{8,12},{10,14},{12,8},{14,10},{16,20},{18,... | collective-permute-start | bytes 61448 | tf_op jit(solution)/shard_map/ppermute | solution.py:81
  294.9 6.0 %collective-permute-start.19 = (f32[5,1024]{1,0:T(8,128)S(1)}, f32[5,1024]{1,0:T(8,128)S(1)}, u32[]{:S(2)}, u32[]{:S(2)}) collective-permute-start(f32[5,1024]{1,0:T(8,128)S(1)} %add.598), channel_id=1, source_target_pairs={{0,8},{2,10},{4,12},{6,14},{8,0},{10,2},{12,4},{14,6},{16,24},{18,... | collective-permute-start | bytes 61448 | tf_op jit(solution)/shard_map/ppermute | solution.py:81
  300.8 12.4 %collective-permute-start.20 = (f32[5,1024]{1,0:T(8,128)S(1)}, f32[5,1024]{1,0:T(8,128)S(1)}, u32[]{:S(2)}, u32[]{:S(2)}) collective-permute-start(f32[5,1024]{1,0:T(8,128)S(1)} %add.599), channel_id=1, source_target_pairs={{0,16},{2,18},{4,20},{6,22},{8,24},{10,26},{12,28},{14,30},{16,0},... | collective-permute-start | bytes 61448 | tf_op jit(solution)/shard_map/ppermute | solution.py:81
  313.2 5.4 %copy-start.51 = (f32[5,1024]{1,0:T(8,128)}, f32[5,1024]{1,0:T(8,128)S(1)}, u32[]{:S(2)}) copy-start(f32[5,1024]{1,0:T(8,128)S(1)} %add.600) | copy-start | bytes 61444
  313.3 5.4 %collective-permute-start.21 = (f32[2,1024]{1,0:T(2,128)S(1)}, f32[2,1024]{1,0:T(2,128)S(1)}, u32[]{:S(2)}, u32[]{:S(2)}) collective-permute-start(f32[2,1024]{1,0:T(2,128)S(1)} %slice.145), channel_id=1, source_target_pairs={{0,1},{1,0},{2,3},{3,2},{4,5},{5,4},{6,7},{7,6},{8,9},{9,8},{10,11... | collective-permute-start | bytes 24584 | tf_op jit(solution)/shard_map/ppermute | solution.py:81
  318.8 11.5 %collective-permute-start.16 = (f32[2,1024]{1,0:T(2,128)S(1)}, f32[2,1024]{1,0:T(2,128)S(1)}, u32[]{:S(2)}, u32[]{:S(2)}) collective-permute-start(f32[2,1024]{1,0:T(2,128)S(1)} %reshape.690), channel_id=1, source_target_pairs={{0,1},{1,0},{2,3},{3,2},{4,5},{5,4},{6,7},{7,6},{8,9},{9,8},{10,11... | collective-permute-start | bytes 24584 | tf_op jit(solution)/shard_map/ppermute | solution.py:81
  322.0 3.7 %copy-start.39 = (f32[256,1024]{1,0:T(8,128)S(1)}, f32[256,1024]{1,0:T(8,128)}, u32[]{:S(2)}) copy-start(f32[256,1024]{1,0:T(8,128)} %get-tuple-element.124) | copy-start | bytes 3145732
  332.3 4.2 %copy-start.1 = (bf16[4,64,1024]{2,1,0:T(8,128)(2,1)S(1)}, bf16[4,64,1024]{2,1,0:T(8,128)(2,1)}, u32[]{:S(2)}) copy-start(bf16[4,64,1024]{2,1,0:T(8,128)(2,1)} %param.22) | copy-start | bytes 1572868
  (45 other events, 67.9 us)
Sparse Core Ops, SparseCore 0:
  11.4 108.6 all-gather.2
  122.9 52.1 all-gather.4
  183.8 138.3 reduce-scatter.1
